TPU v7x, 32 devices: a whole 2x2x4 slice. The times are simulated.
32 devices in a mesh: pipe: 2 (over x), expert: 16 (over z, y, core).
Axes of the slice: x: 2, y: 2, z: 4, core: 2. Of those that a mesh axis runs over, the one named last changes fastest.
Arguments:
- fwd_acts: bfloat16 [2, 1024, 3584], P('pipe', 'expert'), may hold values from -6 to 6
- fwd_routes: int32 [2, 1024, 2], P('pipe', 'expert'), may hold values from 0 to 3, all different within a row; in each aligned block of 64 rows (0 to 63, 64 to 127, ..., all dimensions but the last counted through in order) at most 40 rows name the same one
- fwd_gates: float32 [2, 1024, 2], P('pipe', 'expert'), may hold values from 0.25 to 1
- back_acts: bfloat16 [2, 1024, 3584], P('pipe', 'expert'), may hold values from -6 to 6
- back_routes: int32 [2, 1024, 2], P('pipe', 'expert'), may hold values from 0 to 3, all different within a row; in each aligned block of 64 rows (0 to 63, 64 to 127, ..., all dimensions but the last counted through in order) at most 40 rows name the same one
- back_gates: float32 [2, 1024, 2], P('pipe', 'expert'), may hold values from 0.25 to 1
- back_grads: bfloat16 [2, 1024, 3584], P('pipe', 'expert'), may hold values from -0.59765625 to 0.59765625
- w_up: bfloat16 [2, 16, 3584, 256], P('pipe', 'expert'), may hold values from -0.09375 to 0.09375
- w_down: bfloat16 [2, 16, 256, 3584], P('pipe', 'expert'), may hold values from -0.1875 to 0.1875
Outputs:
- fwd_next: bfloat16 [2, 1024, 3584], P('pipe', 'expert')
- back_next: bfloat16 [2, 1024, 3584], P('pipe', 'expert')
- grad_up: float32 [2, 16, 3584, 256], P('pipe', 'expert')
- grad_down: float32 [2, 16, 256, 3584], P('pipe', 'expert')
Inputs may be any that keep to these rules, and one draw needn't show every extreme that they name: `fwd_routes`: in each aligned block of 64 rows of a section the 2 experts of a row differ, and each expert is named by at most 40 rows, by exactly 40 in some block. `back_routes`: as for fwd_routes.
All inputs are finite; a program needn't handle non-finite values.
Results may differ from a plain program's by a relative error of at most 0.005.
Values may be sent and summed in bfloat16 or wider, within the bound.
No kernel may reach another device: no remote copies, remote signals or barrier semaphores. Data moves between devices by JAX's collectives and lax.ppermute only.
A program may use at most 192 MiB of HBM per device.

v0:
```python
import jax
import jax.numpy as jnp
from jax import lax
from jax.sharding import PartitionSpec as P

GROUP = 4


HIGH = lax.Precision.HIGHEST


def passed_along(value, axis, steps):
    count = lax.axis_size(axis)
    pairs = [(source, (source + steps) % count) for source in range(count)]
    return lax.ppermute(value, axis, pairs)


def silu_grad(value):
    sigma = jax.nn.sigmoid(value)
    return sigma * (1.0 + value * (1.0 - sigma))


def tables(routes, gates, experts, slot_cap):
    tok_rows, top_count = routes.shape
    flat = routes.reshape(tok_rows * top_count)
    onehot = (flat[:, None] == jnp.arange(experts, dtype=jnp.int32)[None, :]).astype(jnp.int32)
    before = jnp.cumsum(onehot, axis=0) - onehot
    slots = jnp.sum(before * onehot, axis=1)
    places = flat * slot_cap + slots
    columns = jnp.arange(experts * slot_cap, dtype=jnp.int32)
    hits = (
        (places[:, None] == columns[None, :])
        .astype(jnp.float32)
        .reshape(tok_rows, top_count, experts * slot_cap)
    )
    plain = jnp.sum(hits, axis=1)
    gated = jnp.sum(hits * gates[:, :, None], axis=1)
    return (plain, gated)


def gather_rows(plain, values):
    return lax.dot_general(
        plain.astype(jnp.bfloat16),
        values,
        (((0,), (0,)), ((), ())),
        preferred_element_type=jnp.float32,
    ).astype(jnp.bfloat16)


def send_rows(stacked, experts, slot_cap):
    count, _, model_width = stacked.shape
    copies = jnp.repeat(stacked.reshape(count, experts, 1, slot_cap, model_width), GROUP, axis=2)
    copies = copies.reshape(count, experts * GROUP, slot_cap, model_width)
    received = lax.all_to_all(copies, "expert", split_axis=1, concat_axis=1, tiled=True)
    return received.reshape(count, -1, model_width)


def send_back(parts, experts, slot_cap):
    count, _, model_width = parts.shape
    arranged = parts.reshape(count, experts * GROUP, slot_cap, model_width)
    received = lax.all_to_all(arranged, "expert", split_axis=1, concat_axis=1, tiled=True)
    summed = jnp.sum(
        received.reshape(count, experts, GROUP, slot_cap, model_width), axis=2, dtype=jnp.float32
    )
    return summed.reshape(count, experts * slot_cap, model_width)


def expert_forward(rows, up_proj, down_proj):
    pre = jnp.dot(rows, up_proj, preferred_element_type=jnp.float32)
    act = jax.nn.silu(pre).astype(jnp.bfloat16)
    return jnp.dot(act, down_proj, preferred_element_type=jnp.float32).astype(jnp.bfloat16)


def expert_backward(rows, grad_rows, up_proj, down_proj):
    pre = jnp.dot(rows, up_proj, preferred_element_type=jnp.float32)
    act = jax.nn.silu(pre).astype(jnp.bfloat16)
    dact = lax.dot_general(
        grad_rows, down_proj, (((1,), (1,)), ((), ())), preferred_element_type=jnp.float32
    )
    dpre = (dact * silu_grad(pre)).astype(jnp.bfloat16)
    dpart = lax.dot_general(
        dpre, up_proj, (((1,), (1,)), ((), ())), preferred_element_type=jnp.float32
    ).astype(jnp.bfloat16)
    grad_up = lax.dot_general(
        rows, dpre, (((0,), (0,)), ((), ())), preferred_element_type=jnp.float32
    )
    grad_down = lax.dot_general(
        act, grad_rows, (((0,), (0,)), ((), ())), preferred_element_type=jnp.float32
    )
    return (dpart, grad_up, grad_down)


def local(
    fwd_acts, fwd_routes, fwd_gates, back_acts, back_routes, back_gates, back_grads, w_up, w_down
):
    devices = lax.axis_size("expert")
    experts = devices // GROUP
    tok_rows = fwd_acts.shape[1]
    top_count = fwd_routes.shape[2]
    slot_cap = GROUP * (5 * tok_rows * top_count // (4 * devices))
    up_proj = w_up[0, 0]
    down_proj = w_down[0, 0]
    fwd_input = fwd_acts[0]
    back_input = back_acts[0]
    out_grad = back_grads[0]
    plain_f, gated_f = tables(fwd_routes[0], fwd_gates[0], experts, slot_cap)
    plain_b, gated_b = tables(back_routes[0], back_gates[0], experts, slot_cap)
    buffer_f = gather_rows(plain_f, fwd_input)
    buffer_x = gather_rows(plain_b, back_input)
    buffer_g = lax.dot_general(
        gated_b, out_grad.astype(jnp.float32), (((0,), (0,)), ((), ())), precision=HIGH
    ).astype(jnp.bfloat16)
    got_f = send_rows(buffer_f[None], experts, slot_cap)
    part = expert_forward(got_f[0], up_proj, down_proj)
    summed_f = send_back(part[None], experts, slot_cap)[0]
    got_b = send_rows(jnp.stack([buffer_x, buffer_g]), experts, slot_cap)
    dpart, grad_up, grad_down = expert_backward(got_b[0], got_b[1], up_proj, down_proj)
    summed_b = send_back(dpart[None], experts, slot_cap)[0]
    merged = jnp.dot(gated_f, summed_f, precision=HIGH)
    section_out = (fwd_input.astype(jnp.float32) + merged).astype(jnp.bfloat16)
    spread_back = jnp.dot(plain_b, summed_b, precision=HIGH)
    section_grad = (out_grad.astype(jnp.float32) + spread_back).astype(jnp.bfloat16)
    fwd_next = passed_along(section_out[None], "pipe", 1)
    back_next = passed_along(section_grad[None], "pipe", -1)
    return (fwd_next, back_next, grad_up[None, None], grad_down[None, None])


def solution(mesh):
    in_specs = (
        P("pipe", "expert", None),
        P("pipe", "expert", None),
        P("pipe", "expert", None),
        P("pipe", "expert", None),
        P("pipe", "expert", None),
        P("pipe", "expert", None),
        P("pipe", "expert", None),
        P("pipe", "expert", None, None),
        P("pipe", "expert", None, None),
    )
    out_specs = (
        P("pipe", "expert", None),
        P("pipe", "expert", None),
        P("pipe", "expert", None, None),
        P("pipe", "expert", None, None),
    )
    return jax.shard_map(local, mesh=mesh, in_specs=in_specs, out_specs=out_specs, check_vma=False)
```

profile of v0, /device:TPU:14, one launch (start us, length us, event | category | flops | bytes accessed | tf_op | source)
XLA Modules:
  0.0 557.6 jit_solution(5994944724591656761)
XLA Ops:
  0.6 0.0 copy-start
  0.6 0.9 copy.40
  1.5 0.1 eq.58
  1.7 0.1 fusion.28
  1.8 0.2 reduce_window_sum.17
  2.0 0.2 select_reduce_fusion.3
  2.1 0.1 reduce_sum.77
  2.3 0.1 copy.41
  2.4 0.7 bitcast_add_fusion.1
  3.1 1.4 convert_reduce_fusion.3
  4.5 1.5 convolution_convert_fusion.4
  6.0 2.4 broadcast_in_dim.26
  8.4 6.4 %all-to-all-start = ((bf16[1,16,40,3584]{3,2,0,1:T(8,128)(2,1)}), bf16[1,16,40,3584]{3,2,0,1:T(8,128)(2,1)}, u32[]{:S(2)}, u32[]{:S(2)}) async-start(bf16[1,16,40,3584]{3,2,0,1:T(8,128)(2,1)} %bitcast.86), calls=%async_computation | async-start | bytes 9175040 | tf_op jit(solution)/shard_map/all_to_all | solution.py:54
  14.8 0.0 copy-done.13
  14.8 0.0 copy-start.4
  14.8 0.1 copy.43
  14.9 0.1 eq.65
  15.0 0.1 fusion.27
  15.1 0.2 reduce_window_sum.18
  15.3 0.2 select_reduce_fusion.2
  15.5 0.1 reduce_sum.82
  15.6 0.1 copy.44
  15.7 0.1 select_reduce_fusion
  15.8 0.5 convolution_convert_fusion.3
  16.3 1.1 convolution_convert_fusion.2
  17.4 0.2 maximum_bitcast_fusion
  17.7 1.6 copy.45
  19.2 96.3 %all-to-all-done = bf16[1,16,40,3584]{3,2,0,1:T(8,128)(2,1)} async-done(((bf16[1,16,40,3584]{3,2,0,1:T(8,128)(2,1)}), bf16[1,16,40,3584]{3,2,0,1:T(8,128)(2,1)}, u32[]{:S(2)}, u32[]{:S(2)}) %all-to-all-start) | async-done | bytes 4587552 | tf_op jit(solution)/shard_map/all_to_all | solution.py:54
  115.5 6.2 %broadcast_in_dim.29 = bf16[2,4,1,4,40,3584]{5,4,0,3,1,2:T(8,128)(2,1)} broadcast(bf16[2,4,40,3584]{3,2,0,1:T(8,128)(2,1)} %copy.45), dimensions={0,1,4,5} | broadcast | bytes 11468800 | tf_op jit(solution)/shard_map/broadcast_in_dim | solution.py:52
  121.7 5.1 all-to-all-start.2
  126.8 9.9 %convolution_convert_fusion.1 = bf16[640,3584]{1,0:T(8,128)(2,1)} fusion(bf16[1,1,256,3584]{3,2,1,0:T(8,128)(2,1)} %param.17, bf16[640,3584]{1,0:T(8,128)(2,1)} %bitcast.5, bf16[1,1,3584,256]{3,2,1,0:T(8,128)(2,1)S(1)} %copy-done), kind=kOutput, calls=%fused_computation.3 | convolution fusion | flops 2351923200 | bytes 12845056 | tf_op jit(solution)/shard_map/dot_general | solution.py:71
  136.7 189.1 %all-to-all-done.2 = bf16[2,16,40,3584]{3,2,0,1:T(8,128)(2,1)} async-done(((bf16[2,16,40,3584]{3,2,0,1:T(8,128)(2,1)}), bf16[2,16,40,3584]{3,2,0,1:T(8,128)(2,1)}, u32[]{:S(2)}, u32[]{:S(2)}) %all-to-all-start.2) | async-done | bytes 9175072 | tf_op jit(solution)/shard_map/all_to_all | solution.py:54
  325.8 5.1 all-to-all-start.1
  330.9 4.3 fusion.33
  335.2 0.0 copy-start.15
  335.2 1.3 fusion.8
  336.5 0.0 copy-start.5
  336.6 1.0 copy-done.1
  337.6 0.5 copy-done.15
  338.1 1.4 fusion.15
  339.5 0.0 copy-start.7
  339.5 0.7 copy-done.7
  340.2 3.5 convolution_convert_fusion
  343.7 87.9 %all-to-all-done.1 = bf16[1,16,40,3584]{3,2,0,1:T(8,128)(2,1)} async-done(((bf16[1,16,40,3584]{3,2,0,1:T(8,128)(2,1)}), bf16[1,16,40,3584]{3,2,0,1:T(8,128)(2,1)}, u32[]{:S(2)}, u32[]{:S(2)}) %all-to-all-start.1) | async-done | bytes 4587552 | tf_op jit(solution)/shard_map/all_to_all | solution.py:61
  431.6 5.1 all-to-all-start.3
  436.7 0.0 copy-start.3
  436.7 0.0 copy-start.12
  436.7 0.0 slice-start.3
  436.7 3.5 convert_reduce_fusion.1
  440.2 0.0 copy-start.8
  440.2 2.1 fusion.3
  442.3 0.5 collective-permute-start
  442.9 0.0 slice-start
  442.9 3.5 convolution_bitcast_fusion.1
  446.4 91.0 %all-to-all-done.3 = bf16[1,16,40,3584]{3,2,0,1:T(8,128)(2,1)} async-done(((bf16[1,16,40,3584]{3,2,0,1:T(8,128)(2,1)}), bf16[1,16,40,3584]{3,2,0,1:T(8,128)(2,1)}, u32[]{:S(2)}, u32[]{:S(2)}) %all-to-all-start.3) | async-done | bytes 4587552 | tf_op jit(solution)/shard_map/all_to_all | solution.py:61
  537.4 3.5 convert_reduce_fusion
  540.9 0.0 copy-start.6
  540.9 1.3 fusion.2
  542.3 0.6 collective-permute-start.1
  542.9 3.5 convolution_bitcast_fusion
  546.4 0.0 collective-permute-done
  546.4 8.7 %collective-permute-done.1 = bf16[1,64,3584]{2,1,0:T(8,128)(2,1)S(1)} collective-permute-done((bf16[1,64,3584]{2,1,0:T(8,128)(2,1)S(1)}, bf16[1,64,3584]{2,1,0:T(8,128)(2,1)S(1)}, u32[]{:S(2)}, u32[]{:S(2)}) %collective-permute-start.1) | collective-permute-done | bytes 458784 | tf_op jit(solution)/shard_map/ppermute | solution.py:15
  555.1 1.8 copy.49
  556.9 0.8 copy.50
  (28 shorter events, 0.1 us)
Async XLA Ops:
  0.6 126.1 %copy-start = (bf16[1,1,3584,256]{3,2,1,0:T(8,128)(2,1)S(1)}, bf16[1,1,3584,256]{3,2,1,0:T(8,128)(2,1)}, u32[]{:S(2)}) copy-start(bf16[1,1,3584,256]{3,2,1,0:T(8,128)(2,1)} %param.16) | copy-start | bytes 5505028
  8.4 6.4 %copy-start.13 = (s32[1,64,2]{1,2,0:T(2,128)S(1)}, s32[1,64,2]{1,2,0:T(2,128)}, u32[]{:S(2)}) copy-start(s32[1,64,2]{1,2,0:T(2,128)} %param.13) | copy-start | bytes 1540
  8.4 7.3 %copy-start.14 = (f32[1,64,2]{1,2,0:T(2,128)S(1)}, f32[1,64,2]{1,2,0:T(2,128)}, u32[]{:S(2)}) copy-start(f32[1,64,2]{1,2,0:T(2,128)} %param.14) | copy-start | bytes 1540
  8.4 7.4 %copy-start.11 = (bf16[1,64,3584]{2,1,0:T(8,128)(2,1)S(1)}, bf16[1,64,3584]{2,1,0:T(8,128)(2,1)}, u32[]{:S(2)}) copy-start(bf16[1,64,3584]{2,1,0:T(8,128)(2,1)} %param.12) | copy-start | bytes 1376260
  8.4 107.1 %all-to-all-start = ((bf16[1,16,40,3584]{3,2,0,1:T(8,128)(2,1)}), bf16[1,16,40,3584]{3,2,0,1:T(8,128)(2,1)}, u32[]{:S(2)}, u32[]{:S(2)}) async-start(bf16[1,16,40,3584]{3,2,0,1:T(8,128)(2,1)} %bitcast.86), calls=%async_computation | async-start | bytes 9175040 | tf_op jit(solution)/shard_map/all_to_all | solution.py:54
  14.8 1.5 copy-start.4
  15.8 1.6 copy-start.9
  121.7 204.1 %all-to-all-start.2 = ((bf16[2,16,40,3584]{3,2,0,1:T(8,128)(2,1)}), bf16[2,16,40,3584]{3,2,0,1:T(8,128)(2,1)}, u32[]{:S(2)}, u32[]{:S(2)}) async-start(bf16[2,16,40,3584]{3,2,0,1:T(8,128)(2,1)} %bitcast.80), calls=%async_computation.2 | async-start | bytes 18350080 | tf_op jit(solution)/shard_map/all_to_all | solution.py:54
  325.8 105.8 %all-to-all-start.1 = ((bf16[1,16,40,3584]{3,2,0,1:T(8,128)(2,1)}), bf16[1,16,40,3584]{3,2,0,1:T(8,128)(2,1)}, u32[]{:S(2)}, u32[]{:S(2)}) async-start(bf16[1,16,40,3584]{3,2,0,1:T(8,128)(2,1)} %bitcast.95), calls=%async_computation.1 | async-start | bytes 9175040 | tf_op jit(solution)/shard_map/all_to_all | solution.py:61
  335.2 2.4 copy-start.1
  335.2 4.3 copy-start.2
  335.2 2.9 copy-start.15
  336.5 1.0 copy-start.5
  339.5 0.7 copy-start.7
  431.6 105.8 %all-to-all-start.3 = ((bf16[1,16,40,3584]{3,2,0,1:T(8,128)(2,1)}), bf16[1,16,40,3584]{3,2,0,1:T(8,128)(2,1)}, u32[]{:S(2)}, u32[]{:S(2)}) async-start(bf16[1,16,40,3584]{3,2,0,1:T(8,128)(2,1)} %bitcast.85), calls=%async_computation.3 | async-start | bytes 9175040 | tf_op jit(solution)/shard_map/all_to_all | solution.py:61
  436.7 6.2 %slice-start.2 = ((s8[4587520]{0:T(1024)(128)(4,1)}), s8[4194304]{0:T(1024)(128)(4,1)S(1)}, s32[]{:S(2)}) async-start(s8[4587520]{0:T(1024)(128)(4,1)} %bitcast.90), calls=%async_computation.6 | async-start | bytes 8388608
  436.7 3.5 copy-start.3
  436.7 3.5 copy-start.12
  436.7 6.2 %slice-start.3 = ((s8[4587520]{0:T(1024)(128)(4,1)}), s8[393216]{0:T(1024)(128)(4,1)S(1)}, s32[]{:S(2)}) async-start(s8[4587520]{0:T(1024)(128)(4,1)} %bitcast.90), calls=%async_computation.7 | async-start | bytes 786432
  440.2 2.7 copy-start.8
  442.3 104.0 %collective-permute-start = (bf16[1,64,3584]{2,1,0:T(8,128)(2,1)}, bf16[1,64,3584]{2,1,0:T(8,128)(2,1)}, u32[]{:S(2)}, u32[]{:S(2)}) collective-permute-start(bf16[1,64,3584]{2,1,0:T(8,128)(2,1)} %fusion.3), channel_id=1, source_target_pairs={{0,16},{16,0},{1,17},{17,1},{2,18},{18,2},{3,19},{19,3},{4,20},{20... | collective-permute-start | bytes 1376264 | tf_op jit(solution)/shard_map/ppermute | solution.py:15
  442.9 100.0 %slice-start = ((s8[4587520]{0:T(1024)(128)(4,1)}), s8[393216]{0:T(1024)(128)(4,1)S(1)}, s32[]{:S(2)}) async-start(s8[4587520]{0:T(1024)(128)(4,1)} %bitcast.82), calls=%async_computation.4 | async-start | bytes 786432
  537.4 3.5 copy-start.10
  537.4 5.5 slice-start.1
  540.9 2.0 copy-start.6
  542.3 12.8 %collective-permute-start.1 = (bf16[1,64,3584]{2,1,0:T(8,128)(2,1)S(1)}, bf16[1,64,3584]{2,1,0:T(8,128)(2,1)S(1)}, u32[]{:S(2)}, u32[]{:S(2)}) collective-permute-start(bf16[1,64,3584]{2,1,0:T(8,128)(2,1)S(1)} %fusion.2), channel_id=1, source_target_pairs={{0,16},{16,0},{1,17},{17,1},{2,18},{18,2},{3,19},{19,3},{4,20},{20... | collective-permute-start | bytes 1376264 | tf_op jit(solution)/shard_map/ppermute | solution.py:15
where the time goes:
time: 558 us
  waiting for transfers between devices  473 us (85%)
  matrix products  29.6 us (5%)
  starting transfers between devices  22.7 us (4%)
  local copies, waits for them, and re-layouts  21.1 us (4%)
  other arithmetic  10.3 us (2%)
    all_to_all x2, waiting for transfers between devices, send_rows(): lax.all_to_all(copies, 'expert', split_axis=1, concat_axis=1, tiled=True)  285 us
    all_to_all x2, waiting for transfers between devices, send_back(): lax.all_to_all(arranged, 'expert', split_axis=1, concat_axis=1, tiled=True)  179 us
    all_to_all x2, starting transfers between devices, send_rows(): lax.all_to_all(copies, 'expert', split_axis=1, concat_axis=1, tiled=True)  11.4 us
  transfers between devices with their start and end apart: 6, of which 5 were waited for; matrix products, arithmetic and copies ran while one was open for 8% of the time, Pallas kernels for 0%

commit v1 on v0

v1 whole, which is shorter than its diff:
```python
import jax
import jax.numpy as jnp
from jax import lax
from jax.sharding import PartitionSpec as P

GROUP = 4
F32 = jnp.float32
BF16 = jnp.bfloat16


def after(value, *before):
    return lax.optimization_barrier((value, *before))[0]


def dot(left, right, contract):
    return lax.dot_general(left, right, ((contract[:1], contract[1:]), ((), ())), preferred_element_type=F32)


def local(
    fwd_acts, fwd_routes, fwd_gates, back_acts, back_routes, back_gates, back_grads, w_up, w_down
):
    devices = lax.axis_size("expert")
    sections = lax.axis_size("pipe")
    experts = devices // GROUP
    tok_rows, width = fwd_acts.shape[1:]
    top_count = fwd_routes.shape[2]
    cap = GROUP * (5 * tok_rows * top_count // (4 * devices))
    mine = lax.axis_index("expert") // GROUP

    def send(value, planes=0, flip=0, pipes=0):
        pairs = []
        for section in range(sections):
            for place in range(devices):
                target = (place // GROUP + planes) % experts * GROUP + (place % GROUP) ^ flip
                goal = (section + pipes) % sections * devices + target
                pairs.append((section * devices + place, goal))
        return lax.ppermute(value, ("pipe", "expert"), pairs)

    def tables(routes):
        nearby = (routes - mine) % experts
        flat = nearby.reshape(tok_rows * top_count)
        onehot = (flat[:, None] == jnp.arange(experts, dtype=jnp.int32)[None, :]).astype(jnp.int32)
        before = jnp.cumsum(onehot, axis=0) - onehot
        slots = jnp.sum(before * onehot, axis=1)
        places = (flat * cap + slots).reshape(tok_rows, top_count)
        columns = jnp.arange(experts * cap, dtype=jnp.int32)
        return (places[:, :, None] == columns).astype(BF16)

    def gather(hits, values):
        plain = jnp.sum(hits, axis=1)
        return [
            dot(plain[:, k * cap:(k + 1) * cap], values, (0, 0)).astype(BF16) for k in range(experts)
        ]

    fwd_input, back_input, out_grad = fwd_acts[0], back_acts[0], back_grads[0]
    up_own, down_own = w_up[0, 0], w_down[0, 0]

    up_y = send(up_own, flip=2)
    down_y = send(down_own, flip=2)
    up_c = send(up_own, flip=1)
    down_c = send(down_own, flip=1)
    up_d = send(up_y, flip=1)
    down_d = send(down_y, flip=1)

    hits_f = tables(fwd_routes[0])
    hits_b = tables(back_routes[0])
    gates_b = jnp.sum(hits_b.astype(F32) * back_gates[0][:, :, None], axis=(0, 1))

    f = gather(hits_f, fwd_input)
    got_f = [f[0]] + [send(f[k], planes=k) for k in range(1, experts)]
    x = gather(hits_b, back_input)
    got_x = [x[0]] + [send(after(x[k], got_f[k]), planes=k) for k in range(1, experts)]
    g = gather(hits_b, out_grad)
    g = [
        (g[k].astype(F32) * gates_b[k * cap:(k + 1) * cap, None]).astype(BF16) for k in range(experts)
    ]
    got_g = [g[0]] + [send(after(g[k], got_x[k]), planes=k) for k in range(1, experts)]

    res_f = send(fwd_input, pipes=1)
    res_hits_f = send(fwd_routes[0], pipes=1)
    res_gates = send(fwd_gates[0], pipes=1)
    res_b = send(out_grad, pipes=-1)
    res_hits_b = send(back_routes[0], pipes=-1)

    rows_f = jnp.concatenate(got_f, axis=0)
    rows_x = jnp.concatenate(got_x, axis=0)
    rows_g = jnp.concatenate(got_g, axis=0)

    up = jnp.concatenate([up_own, up_c, up_y, up_d], axis=1)
    down = jnp.concatenate([down_own, down_c, down_y, down_d], axis=0)

    act_f = jax.nn.silu(dot(rows_f, up, (1, 0))).astype(BF16)
    out_f = dot(act_f, down, (1, 0)).astype(BF16)

    pre = dot(rows_x, up, (1, 0))
    sigma = jax.nn.sigmoid(pre)
    act = (pre * sigma).astype(BF16)
    dact = dot(rows_g, down, (1, 1))
    dpre = (dact * sigma * (1.0 + pre * (1.0 - sigma))).astype(BF16)
    out_b = dot(dpre, up, (1, 1)).astype(BF16)

    hidden = up_own.shape[1]

    ret_f = [send(out_f[k * cap:(k + 1) * cap], planes=-k, pipes=1) for k in range(experts)]
    ret_b = [
        send(after(out_b[k * cap:(k + 1) * cap], ret_f[k]), planes=-k, pipes=-1)
        for k in range(experts)
    ]

    both = jnp.concatenate([act.reshape(-1, GROUP, hidden), dpre.reshape(-1, GROUP, hidden)], axis=2)
    both_all = [both[:, 0]] + [send(both[:, m], flip=m) for m in range(1, GROUP)]
    x_y = send(after(rows_x, up_y), flip=2)
    g_y = send(after(rows_g, down_y), flip=2)
    x_c, g_c = send(rows_x, flip=1), send(rows_g, flip=1)
    x_d, g_d = send(x_y, flip=1), send(g_y, flip=1)
    x_all = jnp.concatenate([rows_x, x_c, x_y, x_d], axis=0)
    g_all = jnp.concatenate([rows_g, g_c, g_y, g_d], axis=0)
    hid_all = jnp.concatenate(both_all, axis=0)
    grad_up = dot(x_all, hid_all[:, hidden:], (0, 0))
    grad_down = dot(hid_all[:, :hidden], g_all, (0, 0))

    def combine(residual, hits, gates, parts):
        total = residual.astype(F32)
        for choice in range(top_count):
            picked = dot(hits[:, choice], jnp.concatenate(parts, axis=0), (1, 0))
            total = total + (picked if gates is None else gates[:, choice:choice + 1] * picked)
        return total.astype(BF16)

    fwd_next = combine(res_f, tables(res_hits_f), res_gates, ret_f)
    back_next = combine(res_b, tables(res_hits_b), None, ret_b)
    return (fwd_next[None], back_next[None], grad_up[None, None], grad_down[None, None])


def solution(mesh):
    rows = P("pipe", "expert", None)
    slices = P("pipe", "expert", None, None)
    return jax.shard_map(
        local,
        mesh=mesh,
        in_specs=(rows,) * 7 + (slices,) * 2,
        out_specs=(rows, rows, slices, slices),
        check_vma=False,
    )
```

time: 558 us -> 252 us (0.45)
  the two profiles are of different devices: /device:TPU:14 before, /device:TPU:0 now
where the time goes in v1:
time: 252 us; the launch traced here: 251 us
  waiting for transfers between devices  118 us (47%)
  starting transfers between devices  57 us (23%)
  matrix products  52.8 us (21%)
  local copies, waits for them, and re-layouts  17.5 us (7%)
  other arithmetic  4.84 us (2%)
    ppermute x37, waiting for transfers between devices, send(): return lax.ppermute(value, ('pipe', 'expert'), pairs)  118 us
    ppermute x37, starting transfers between devices, send(): return lax.ppermute(value, ('pipe', 'expert'), pairs)  57 us
    dot_general x22, matrix products, dot(): lax.dot_general(left, right, ((contract[:1], contract[1:]), ((), ())), pr...  52.8 us
    unnamed x59, local copies, waits for them, and re-layouts  12.8 us
  transfers between devices with their start and end apart: 37, of which 10 were waited for; matrix products, arithmetic and copies ran while one was open for 28% of the time, Pallas kernels for 0%

profile of v1, /device:TPU:0, one launch (start us, length us, event | category | flops | bytes accessed | tf_op | source)
XLA Modules:
  0.0 251.2 jit_solution(17532516961349557828)
XLA Ops:
  0.7 3.0 %collective-permute-start.10 = (bf16[256,3584]{1,0:T(8,128)(2,1)}, bf16[256,3584]{1,0:T(8,128)(2,1)}, u32[]{:S(2)}, u32[]{:S(2)}) collective-permute-start(bf16[256,3584]{1,0:T(8,128)(2,1)} %bitcast.97), channel_id=1, source_target_pairs={{0,2},{1,3},{2,0},{3,1},{4,6},{5,7},{6,4},{7,5},{8,10},{9,11},{10,... | collective-permute-start | bytes 5505032 | tf_op jit(solution)/shard_map/ppermute | solution.py:37
  3.7 0.7 broadcast_subtract_fusion.1
  5.3 0.7 fusion.60
  6.1 1.4 convolution_convert_fusion.10
  7.5 3.7 %collective-permute-start.5 = (bf16[40,3584]{1,0:T(8,128)(2,1)S(1)}, bf16[40,3584]{1,0:T(8,128)(2,1)}, u32[]{:S(2)}, u32[]{:S(2)}) collective-permute-start(bf16[40,3584]{1,0:T(8,128)(2,1)S(1)} %convolution_convert_fusion.10), channel_id=1, source_target_pairs={{0,12},{1,13},{2,14},{3,15},{4,0},{5,1},{6,2},{7,3},{8,4},{9,5},{1... | collective-permute-start | bytes 860168 | tf_op jit(solution)/shard_map/ppermute | solution.py:37
  11.1 1.3 convolution_convert_fusion.11
  12.6 1.6 collective-permute-start.17
  15.0 1.0 convolution_convert_fusion.13
  17.7 1.0 constant_dynamic-update-slice_fusion.14
  18.9 1.1 fusion.2
  20.0 1.1 fusion.5
  21.0 1.1 fusion.8
  22.1 1.1 constant_dynamic-update-slice_fusion.21
  23.2 1.1 convolution_convert_fusion.7
  24.3 0.9 collective-permute-start.3
  27.7 1.5 collective-permute-start.1
  29.2 7.6 %collective-permute-done.4 = bf16[40,3584]{1,0:T(8,128)(2,1)} collective-permute-done((bf16[40,3584]{1,0:T(8,128)(2,1)S(1)}, bf16[40,3584]{1,0:T(8,128)(2,1)}, u32[]{:S(2)}, u32[]{:S(2)}) %collective-permute-start.4) | collective-permute-done | bytes 286752 | tf_op jit(solution)/shard_map/ppermute | solution.py:37
  36.8 8.2 %collective-permute-start.20 = (bf16[40,3584]{1,0:T(8,128)(2,1)S(1)}, bf16[40,3584]{1,0:T(8,128)(2,1)S(1)}, u32[]{:S(2)}, u32[]{:S(2)}) collective-permute-start(bf16[40,3584]{1,0:T(8,128)(2,1)S(1)} %convolution_convert_fusion.5), channel_id=1, source_target_pairs={{0,8},{1,9},{2,10},{3,11},{4,12},{5,13},{6,14},{7,15},{8,0},{9,1},... | collective-permute-start | bytes 860168 | tf_op jit(solution)/shard_map/ppermute | solution.py:37
  45.0 1.4 collective-permute-start.18
  46.6 2.5 collective-permute-start.23
  49.0 16.3 %collective-permute-done.20 = bf16[40,3584]{1,0:T(8,128)(2,1)S(1)} collective-permute-done((bf16[40,3584]{1,0:T(8,128)(2,1)S(1)}, bf16[40,3584]{1,0:T(8,128)(2,1)S(1)}, u32[]{:S(2)}, u32[]{:S(2)}) %collective-permute-start.20) | collective-permute-done | bytes 286752 | tf_op jit(solution)/shard_map/ppermute | solution.py:37
  65.3 12.2 %collective-permute-start.19 = (bf16[40,3584]{1,0:T(8,128)(2,1)}, bf16[40,3584]{1,0:T(8,128)(2,1)S(1)}, u32[]{:S(2)}, u32[]{:S(2)}) collective-permute-start(bf16[40,3584]{1,0:T(8,128)(2,1)} %fusion.8), channel_id=1, source_target_pairs={{0,4},{1,5},{2,6},{3,7},{4,8},{5,9},{6,10},{7,11},{8,12},{9,13},{1... | collective-permute-start | bytes 860168 | tf_op jit(solution)/shard_map/ppermute | solution.py:37
  77.5 0.7 constant_dynamic-update-slice_fusion.13
  78.3 0.7 constant_dynamic-update-slice_fusion.12
  79.1 0.7 constant_dynamic-update-slice_fusion.11
  79.9 9.1 %collective-permute-done.21 = bf16[40,3584]{1,0:T(8,128)(2,1)S(1)} collective-permute-done((bf16[40,3584]{1,0:T(8,128)(2,1)}, bf16[40,3584]{1,0:T(8,128)(2,1)S(1)}, u32[]{:S(2)}, u32[]{:S(2)}) %collective-permute-start.21) | collective-permute-done | bytes 286752 | tf_op jit(solution)/shard_map/ppermute | solution.py:37
  89.0 1.1 pad_maximum_fusion.6
  91.1 0.7 constant_dynamic-update-slice_fusion.20
  91.8 0.7 constant_dynamic-update-slice_fusion.19
  92.6 0.7 constant_dynamic-update-slice_fusion.18
  93.3 1.6 collective-permute-start.35
  95.1 23.7 %collective-permute-done.29 = bf16[160,3584]{1,0:T(8,128)(2,1)S(1)} collective-permute-done((bf16[160,3584]{1,0:T(8,128)(2,1)S(1)}, bf16[160,3584]{1,0:T(8,128)(2,1)S(1)}, u32[]{:S(2)}, u32[]{:S(2)}) %collective-permute-start.29) | collective-permute-done | bytes 1146912 | tf_op jit(solution)/shard_map/ppermute | solution.py:37
  118.7 1.2 constant_dynamic-update-slice_fusion.10
  119.9 1.1 constant_dynamic-update-slice_fusion.17
  121.0 1.1 constant_dynamic-update-slice_fusion.9
  122.1 20.3 %collective-permute-done.35 = bf16[160,3584]{1,0:T(8,128)(2,1)S(1)} collective-permute-done((bf16[160,3584]{1,0:T(8,128)(2,1)S(1)}, bf16[160,3584]{1,0:T(8,128)(2,1)S(1)}, u32[]{:S(2)}, u32[]{:S(2)}) %collective-permute-start.35) | collective-permute-done | bytes 1146912 | tf_op jit(solution)/shard_map/ppermute | solution.py:37
  142.4 1.5 collective-permute-start
  143.9 1.1 constant_dynamic-update-slice_fusion.16
  145.0 1.2 copy-done.12
  146.2 1.2 copy-done.14
  147.5 1.2 copy-done.16
  148.7 15.2 %convolution_convert_fusion.1 = bf16[160,3584]{1,0:T(8,128)(2,1)} fusion(bf16[256,3584]{1,0:T(8,128)(2,1)} %copy-done.16, bf16[256,3584]{1,0:T(8,128)(2,1)} %collective-permute-done.10, bf16[256,3584]{1,0:T(8,128)(2,1)} %copy-done.12, bf16[256,3584]{1,0:T(8,128)(2,1)} %bitcast.98, bf16[40,3584]{1,0:T(8,128)(2,1)} %collective-permute-done.5, ...), kind=kOutput, calls=%fused_computation.5 | convolution fusion | flops 2413510656 | bytes 16973824 | tf_op jit(solution)/shard_map/dot_general | solution.py:16
  163.9 1.4 fusion.83
  165.4 1.1 collective-permute-start.12
  166.4 5.0 %multiply_convert_fusion = (bf16[160,1024]{1,0:T(8,128)(2,1)S(1)}, f32[160,1024]{1,0:T(8,128)S(1)}) fusion(bf16[3584,256]{1,0:T(8,128)(2,1)} %collective-permute-done.8, bf16[3584,256]{1,0:T(8,128)(2,1)} %collective-permute-done.7, bf16[3584,256]{1,0:T(8,128)(2,1)S(1)} %copy-done.15, bf16[3584,256]{1,0:T(8,128)(2,1)} %bitcast.5, ...), kind=kOutput, calls=%fused_computation.46 | convolution fusion | flops 1209171968 | bytes 9469952 | tf_op jit(solution)/shard_map/dot_general | solution.py:16
  171.5 4.0 %fusion.13 = bf16[160,1024]{1,0:T(8,128)(2,1)S(1)} fusion(bf16[256,3584]{1,0:T(8,128)(2,1)S(1)} %copy-done.17, bf16[256,3584]{1,0:T(8,128)(2,1)} %collective-permute-done.10, bf16[256,3584]{1,0:T(8,128)(2,1)S(1)} %copy-done.13, bf16[256,3584]{1,0:T(8,128)(2,1)S(1)} %bitcast.100, f32[160,1024]{1,0:T(8,128)S(1)} %get-tuple-element.49, ...), kind=kOutput, calls=%fused_computation.32 | convolution fusion | flops 1209827328 | bytes 9469952 | tf_op jit(solution)/shard_map/dot_general | solution.py:16
  176.3 1.3 collective-permute-start.31
  177.6 4.5 %convolution_convert_fusion = bf16[160,3584]{1,0:T(8,128)(2,1)S(1)} fusion(bf16[160,1024]{1,0:T(8,128)(2,1)S(1)} %fusion.13, bf16[3584,256]{1,0:T(8,128)(2,1)} %collective-permute-done.8, bf16[3584,256]{1,0:T(8,128)(2,1)} %collective-permute-done.7, bf16[3584,256]{1,0:T(8,128)(2,1)S(1)} %copy-done.15, bf16[3584,256]{1,0:T(8,128)(2,1)} %bitcast.5), kind=kOutput, calls=%fused_computation.4 | convolution fusion | flops 1204338688 | bytes 8814592 | tf_op jit(solution)/shard_map/dot_general | solution.py:16
  182.2 1.1 collective-permute-start.16
  183.3 0.8 collective-permute-done.32
  184.8 3.8 %collective-permute-start.13 = (bf16[40,3584]{1,0:T(8,128)(2,1)S(1)}, bf16[40,3584]{1,0:T(8,128)(2,1)S(1)}, u32[]{:S(2)}, u32[]{:S(2)}) collective-permute-start(bf16[40,3584]{1,0:T(8,128)(2,1)S(1)} %get-tuple-element.34), channel_id=1, source_target_pairs={{0,28},{1,29},{2,30},{3,31},{4,16},{5,17},{6,18},{7,19},{8,20},{9,... | collective-permute-start | bytes 860168 | tf_op jit(solution)/shard_map/ppermute | solution.py:37
  188.6 6.7 %collective-permute-done.13 = bf16[40,3584]{1,0:T(8,128)(2,1)S(1)} collective-permute-done((bf16[40,3584]{1,0:T(8,128)(2,1)S(1)}, bf16[40,3584]{1,0:T(8,128)(2,1)S(1)}, u32[]{:S(2)}, u32[]{:S(2)}) %collective-permute-start.13) | collective-permute-done | bytes 286752 | tf_op jit(solution)/shard_map/ppermute | solution.py:37
  195.3 2.6 %collective-permute-start.14 = (bf16[40,3584]{1,0:T(8,128)(2,1)S(1)}, bf16[40,3584]{1,0:T(8,128)(2,1)S(1)}, u32[]{:S(2)}, u32[]{:S(2)}) collective-permute-start(bf16[40,3584]{1,0:T(8,128)(2,1)S(1)} %get-tuple-element.33), channel_id=1, source_target_pairs={{0,24},{1,25},{2,26},{3,27},{4,28},{5,29},{6,30},{7,31},{8,16},{9,... | collective-permute-start | bytes 860168 | tf_op jit(solution)/shard_map/ppermute | solution.py:37
  198.0 13.7 %collective-permute-done.14 = bf16[40,3584]{1,0:T(8,128)(2,1)S(1)} collective-permute-done((bf16[40,3584]{1,0:T(8,128)(2,1)S(1)}, bf16[40,3584]{1,0:T(8,128)(2,1)S(1)}, u32[]{:S(2)}, u32[]{:S(2)}) %collective-permute-start.14) | collective-permute-done | bytes 286752 | tf_op jit(solution)/shard_map/ppermute | solution.py:37
  212.1 10.1 %collective-permute-done.15 = bf16[40,3584]{1,0:T(8,128)(2,1)S(1)} collective-permute-done((bf16[40,3584]{1,0:T(8,128)(2,1)S(1)}, bf16[40,3584]{1,0:T(8,128)(2,1)S(1)}, u32[]{:S(2)}, u32[]{:S(2)}) %collective-permute-start.15) | collective-permute-done | bytes 286752 | tf_op jit(solution)/shard_map/ppermute | solution.py:37
  222.2 1.2 collective-permute-start.24
  223.8 2.9 %collective-permute-start.25 = (bf16[40,3584]{1,0:T(8,128)(2,1)S(1)}, bf16[40,3584]{1,0:T(8,128)(2,1)S(1)}, u32[]{:S(2)}, u32[]{:S(2)}) collective-permute-start(bf16[40,3584]{1,0:T(8,128)(2,1)S(1)} %get-tuple-element.23), channel_id=1, source_target_pairs={{0,28},{1,29},{2,30},{3,31},{4,16},{5,17},{6,18},{7,19},{8,20},{9,... | collective-permute-start | bytes 860168 | tf_op jit(solution)/shard_map/ppermute | solution.py:37
  226.7 2.1 fusion.26
  228.9 3.5 %convolution_bitcast_fusion.1 = f32[1,1,3584,256]{3,2,1,0:T(8,128)} fusion(bf16[640,3584]{1,0:T(8,128)(2,1)S(1)} %constant_dynamic-update-slice_fusion.8, bf16[640,512]{1,0:T(8,128)(2,1)S(1)} %pad_maximum_fusion.8), kind=kOutput, calls=%fused_computation.3 | convolution fusion | flops 1174405120 | bytes 8585216 | tf_op jit(solution)/shard_map/dot_general | solution.py:16
  232.4 0.8 collective-permute-start.27
  233.2 1.1 constant_dynamic-update-slice_fusion.15
  234.3 5.8 %convolution_bitcast_fusion = f32[1,1,256,3584]{3,2,1,0:T(8,128)} fusion(bf16[640,3584]{1,0:T(8,128)(2,1)} %constant_dynamic-update-slice_fusion.15, bf16[640,512]{1,0:T(8,128)(2,1)S(1)} %pad_maximum_fusion.8), kind=kOutput, calls=%fused_computation.2 | convolution fusion | flops 1174405120 | bytes 8585216 | tf_op jit(solution)/shard_map/dot_general | solution.py:16
  240.1 9.6 %collective-permute-done.26 = bf16[40,3584]{1,0:T(8,128)(2,1)S(1)} collective-permute-done((bf16[40,3584]{1,0:T(8,128)(2,1)S(1)}, bf16[40,3584]{1,0:T(8,128)(2,1)S(1)}, u32[]{:S(2)}, u32[]{:S(2)}) %collective-permute-start.26) | collective-permute-done | bytes 286752 | tf_op jit(solution)/shard_map/ppermute | solution.py:37
  250.1 1.1 fusion.27
  (147 shorter events, 10.7 us)
Async XLA Ops:
  0.6 16.4 %copy-start = (bf16[1,64,3584]{2,1,0:T(8,128)(2,1)S(1)}, bf16[1,64,3584]{2,1,0:T(8,128)(2,1)}, u32[]{:S(2)}) copy-start(bf16[1,64,3584]{2,1,0:T(8,128)(2,1)} %param.12) | copy-start | bytes 1376260
  0.6 14.0 %copy-start.1 = (bf16[1,64,3584]{2,1,0:T(8,128)(2,1)S(1)}, bf16[1,64,3584]{2,1,0:T(8,128)(2,1)}, u32[]{:S(2)}) copy-start(bf16[1,64,3584]{2,1,0:T(8,128)(2,1)} %param.9) | copy-start | bytes 1376260
  0.7 15.3 %copy-start.8 = (s32[1,64,2]{1,2,0:T(2,128)S(1)}, s32[1,64,2]{1,2,0:T(2,128)}, u32[]{:S(2)}) copy-start(s32[1,64,2]{1,2,0:T(2,128)} %param.13) | copy-start | bytes 1540
  0.7 92.6 %collective-permute-start.10 = (bf16[256,3584]{1,0:T(8,128)(2,1)}, bf16[256,3584]{1,0:T(8,128)(2,1)}, u32[]{:S(2)}, u32[]{:S(2)}) collective-permute-start(bf16[256,3584]{1,0:T(8,128)(2,1)} %bitcast.97), channel_id=1, source_target_pairs={{0,2},{1,3},{2,0},{3,1},{4,6},{5,7},{6,4},{7,5},{8,10},{9,11},{10,... | collective-permute-start | bytes 5505032 | tf_op jit(solution)/shard_map/ppermute | solution.py:37
  7.5 20.2 %collective-permute-start.5 = (bf16[40,3584]{1,0:T(8,128)(2,1)S(1)}, bf16[40,3584]{1,0:T(8,128)(2,1)}, u32[]{:S(2)}, u32[]{:S(2)}) collective-permute-start(bf16[40,3584]{1,0:T(8,128)(2,1)S(1)} %convolution_convert_fusion.10), channel_id=1, source_target_pairs={{0,12},{1,13},{2,14},{3,15},{4,0},{5,1},{6,2},{7,3},{8,4},{9,5},{1... | collective-permute-start | bytes 860168 | tf_op jit(solution)/shard_map/ppermute | solution.py:37
  12.5 6.3 %copy-start.9 = (f32[1,64,2]{1,2,0:T(2,128)S(1)}, f32[1,64,2]{1,2,0:T(2,128)}, u32[]{:S(2)}) copy-start(f32[1,64,2]{1,2,0:T(2,128)} %param.14) | copy-start | bytes 1540
  12.5 6.4 %copy-start.2 = (bf16[1,64,3584]{2,1,0:T(8,128)(2,1)S(1)}, bf16[1,64,3584]{2,1,0:T(8,128)(2,1)}, u32[]{:S(2)}) copy-start(bf16[1,64,3584]{2,1,0:T(8,128)(2,1)} %param.15) | copy-start | bytes 1376260
  12.5 24.3 %collective-permute-start.4 = (bf16[40,3584]{1,0:T(8,128)(2,1)S(1)}, bf16[40,3584]{1,0:T(8,128)(2,1)}, u32[]{:S(2)}, u32[]{:S(2)}) collective-permute-start(bf16[40,3584]{1,0:T(8,128)(2,1)S(1)} %convolution_convert_fusion.11), channel_id=1, source_target_pairs={{0,8},{1,9},{2,10},{3,11},{4,12},{5,13},{6,14},{7,15},{8,0},{9,1},... | collective-permute-start | bytes 860168 | tf_op jit(solution)/shard_map/ppermute | solution.py:37
  12.6 11.7 %collective-permute-start.17 = (s32[64,2]{0,1:T(2,128)}, s32[64,2]{0,1:T(2,128)S(1)}, u32[]{:S(2)}, u32[]{:S(2)}) collective-permute-start(s32[64,2]{0,1:T(2,128)} %bitcast.94), channel_id=1, source_target_pairs={{0,16},{1,17},{2,18},{3,19},{4,20},{5,21},{6,22},{7,23},{8,24},{9,... | collective-permute-start | bytes 1544 | tf_op jit(solution)/shard_map/ppermute | solution.py:37
  14.1 11.1 %collective-permute-start.2 = (s32[64,2]{0,1:T(2,128)}, s32[64,2]{0,1:T(2,128)S(1)}, u32[]{:S(2)}, u32[]{:S(2)}) collective-permute-start(s32[64,2]{0,1:T(2,128)} %bitcast.95), channel_id=1, source_target_pairs={{0,16},{1,17},{2,18},{3,19},{4,20},{5,21},{6,22},{7,23},{8,24},{9,... | collective-permute-start | bytes 1544 | tf_op jit(solution)/shard_map/ppermute | solution.py:37
  18.9 8.8 %copy-start.18 = (f32[1,64,2]{1,2,0:T(2,128)S(1)}, f32[1,64,2]{1,2,0:T(2,128)}, u32[]{:S(2)}) copy-start(f32[1,64,2]{1,2,0:T(2,128)} %param.11) | copy-start | bytes 1540
  24.3 12.6 %collective-permute-start.3 = (bf16[40,3584]{1,0:T(8,128)(2,1)S(1)}, bf16[40,3584]{1,0:T(8,128)(2,1)}, u32[]{:S(2)}, u32[]{:S(2)}) collective-permute-start(bf16[40,3584]{1,0:T(8,128)(2,1)S(1)} %convolution_convert_fusion.12), channel_id=1, source_target_pairs={{0,4},{1,5},{2,6},{3,7},{4,8},{5,9},{6,10},{7,11},{8,12},{9,13},{1... | collective-permute-start | bytes 860168 | tf_op jit(solution)/shard_map/ppermute | solution.py:37
  25.2 65.4 %collective-permute-start.7 = (bf16[3584,256]{1,0:T(8,128)(2,1)}, bf16[3584,256]{1,0:T(8,128)(2,1)}, u32[]{:S(2)}, u32[]{:S(2)}) collective-permute-start(bf16[3584,256]{1,0:T(8,128)(2,1)} %bitcast.5), channel_id=1, source_target_pairs={{0,2},{1,3},{2,0},{3,1},{4,6},{5,7},{6,4},{7,5},{8,10},{9,11},{10,... | collective-permute-start | bytes 5505032 | tf_op jit(solution)/shard_map/ppermute | solution.py:37
  27.5 52.3 %copy-start.10 = (bf16[1,1,256,3584]{3,2,1,0:T(8,128)(2,1)S(1)}, bf16[1,1,256,3584]{3,2,1,0:T(8,128)(2,1)}, u32[]{:S(2)}) copy-start(bf16[1,1,256,3584]{3,2,1,0:T(8,128)(2,1)} %param.17) | copy-start | bytes 5505028
  27.7 17.3 %collective-permute-start.1 = (f32[64,2]{0,1:T(2,128)S(1)}, f32[64,2]{0,1:T(2,128)S(1)}, u32[]{:S(2)}, u32[]{:S(2)}) collective-permute-start(f32[64,2]{0,1:T(2,128)S(1)} %bitcast.101), channel_id=1, source_target_pairs={{0,16},{1,17},{2,18},{3,19},{4,20},{5,21},{6,22},{7,23},{8,24},{9,... | collective-permute-start | bytes 1544 | tf_op jit(solution)/shard_map/ppermute | solution.py:37
  36.8 9.7 %collective-permute-start.22 = (bf16[40,3584]{1,0:T(8,128)(2,1)S(1)}, bf16[40,3584]{1,0:T(8,128)(2,1)S(1)}, u32[]{:S(2)}, u32[]{:S(2)}) collective-permute-start(bf16[40,3584]{1,0:T(8,128)(2,1)S(1)} %convolution_convert_fusion.3), channel_id=1, source_target_pairs={{0,12},{1,13},{2,14},{3,15},{4,0},{5,1},{6,2},{7,3},{8,4},{9,5},{1... | collective-permute-start | bytes 860168 | tf_op jit(solution)/shard_map/ppermute | solution.py:37
  36.8 28.5 %collective-permute-start.20 = (bf16[40,3584]{1,0:T(8,128)(2,1)S(1)}, bf16[40,3584]{1,0:T(8,128)(2,1)S(1)}, u32[]{:S(2)}, u32[]{:S(2)}) collective-permute-start(bf16[40,3584]{1,0:T(8,128)(2,1)S(1)} %convolution_convert_fusion.5), channel_id=1, source_target_pairs={{0,8},{1,9},{2,10},{3,11},{4,12},{5,13},{6,14},{7,15},{8,0},{9,1},... | collective-permute-start | bytes 860168 | tf_op jit(solution)/shard_map/ppermute | solution.py:37
  45.0 20.3 %collective-permute-start.18 = (bf16[40,3584]{1,0:T(8,128)(2,1)}, bf16[40,3584]{1,0:T(8,128)(2,1)S(1)}, u32[]{:S(2)}, u32[]{:S(2)}) collective-permute-start(bf16[40,3584]{1,0:T(8,128)(2,1)} %convolution_convert_fusion.7), channel_id=1, source_target_pairs={{0,4},{1,5},{2,6},{3,7},{4,8},{5,9},{6,10},{7,11},{8,12},{9,13},{1... | collective-permute-start | bytes 860168 | tf_op jit(solution)/shard_map/ppermute | solution.py:37
  46.6 33.3 %collective-permute-start.23 = (bf16[40,3584]{1,0:T(8,128)(2,1)}, bf16[40,3584]{1,0:T(8,128)(2,1)S(1)}, u32[]{:S(2)}, u32[]{:S(2)}) collective-permute-start(bf16[40,3584]{1,0:T(8,128)(2,1)} %fusion.2), channel_id=1, source_target_pairs={{0,12},{1,13},{2,14},{3,15},{4,0},{5,1},{6,2},{7,3},{8,4},{9,5},{1... | collective-permute-start | bytes 860168 | tf_op jit(solution)/shard_map/ppermute | solution.py:37
  65.3 23.6 %collective-permute-start.21 = (bf16[40,3584]{1,0:T(8,128)(2,1)}, bf16[40,3584]{1,0:T(8,128)(2,1)S(1)}, u32[]{:S(2)}, u32[]{:S(2)}) collective-permute-start(bf16[40,3584]{1,0:T(8,128)(2,1)} %fusion.5), channel_id=1, source_target_pairs={{0,8},{1,9},{2,10},{3,11},{4,12},{5,13},{6,14},{7,15},{8,0},{9,1},... | collective-permute-start | bytes 860168 | tf_op jit(solution)/shard_map/ppermute | solution.py:37
  65.3 23.6 %collective-permute-start.19 = (bf16[40,3584]{1,0:T(8,128)(2,1)}, bf16[40,3584]{1,0:T(8,128)(2,1)S(1)}, u32[]{:S(2)}, u32[]{:S(2)}) collective-permute-start(bf16[40,3584]{1,0:T(8,128)(2,1)} %fusion.8), channel_id=1, source_target_pairs={{0,4},{1,5},{2,6},{3,7},{4,8},{5,9},{6,10},{7,11},{8,12},{9,13},{1... | collective-permute-start | bytes 860168 | tf_op jit(solution)/shard_map/ppermute | solution.py:37
  79.9 65.1 %collective-permute-start.9 = (bf16[256,3584]{1,0:T(8,128)(2,1)S(1)}, bf16[256,3584]{1,0:T(8,128)(2,1)S(1)}, u32[]{:S(2)}, u32[]{:S(2)}) collective-permute-start(bf16[256,3584]{1,0:T(8,128)(2,1)S(1)} %bitcast.99), channel_id=1, source_target_pairs={{0,1},{1,0},{2,3},{3,2},{4,5},{5,4},{6,7},{7,6},{8,9},{9,8},{10,11... | collective-permute-start | bytes 5505032 | tf_op jit(solution)/shard_map/ppermute | solution.py:37
  89.0 4.3 %collective-permute-start.28 = (bf16[160,3584]{1,0:T(8,128)(2,1)S(1)}, bf16[160,3584]{1,0:T(8,128)(2,1)S(1)}, u32[]{:S(2)}, u32[]{:S(2)}) collective-permute-start(bf16[160,3584]{1,0:T(8,128)(2,1)S(1)} %pad_maximum_fusion.7), channel_id=1, source_target_pairs={{0,1},{1,0},{2,3},{3,2},{4,5},{5,4},{6,7},{7,6},{8,9},{9,8},{10,11... | collective-permute-start | bytes 3440648 | tf_op jit(solution)/shard_map/ppermute | solution.py:37
  90.0 4.9 %collective-permute-start.34 = (bf16[160,3584]{1,0:T(8,128)(2,1)S(1)}, bf16[160,3584]{1,0:T(8,128)(2,1)S(1)}, u32[]{:S(2)}, u32[]{:S(2)}) collective-permute-start(bf16[160,3584]{1,0:T(8,128)(2,1)S(1)} %pad_maximum_fusion.6), channel_id=1, source_target_pairs={{0,1},{1,0},{2,3},{3,2},{4,5},{5,4},{6,7},{7,6},{8,9},{9,8},{10,11... | collective-permute-start | bytes 3440648 | tf_op jit(solution)/shard_map/ppermute | solution.py:37
  90.6 28.1 %collective-permute-start.29 = (bf16[160,3584]{1,0:T(8,128)(2,1)S(1)}, bf16[160,3584]{1,0:T(8,128)(2,1)S(1)}, u32[]{:S(2)}, u32[]{:S(2)}) collective-permute-start(bf16[160,3584]{1,0:T(8,128)(2,1)S(1)} %pad_maximum_fusion.7), channel_id=1, source_target_pairs={{0,2},{1,3},{2,0},{3,1},{4,6},{5,7},{6,4},{7,5},{8,10},{9,11},{10,... | collective-permute-start | bytes 3440648 | tf_op jit(solution)/shard_map/ppermute | solution.py:37
  93.3 52.9 %collective-permute-start.6 = (bf16[3584,256]{1,0:T(8,128)(2,1)}, bf16[3584,256]{1,0:T(8,128)(2,1)S(1)}, u32[]{:S(2)}, u32[]{:S(2)}) collective-permute-start(bf16[3584,256]{1,0:T(8,128)(2,1)} %bitcast.5), channel_id=1, source_target_pairs={{0,1},{1,0},{2,3},{3,2},{4,5},{5,4},{6,7},{7,6},{8,9},{9,8},{10,11... | collective-permute-start | bytes 5505032 | tf_op jit(solution)/shard_map/ppermute | solution.py:37
  93.3 49.1 %collective-permute-start.35 = (bf16[160,3584]{1,0:T(8,128)(2,1)S(1)}, bf16[160,3584]{1,0:T(8,128)(2,1)S(1)}, u32[]{:S(2)}, u32[]{:S(2)}) collective-permute-start(bf16[160,3584]{1,0:T(8,128)(2,1)S(1)} %pad_maximum_fusion.6), channel_id=1, source_target_pairs={{0,2},{1,3},{2,0},{3,1},{4,6},{5,7},{6,4},{7,5},{8,10},{9,11},{10,... | collective-permute-start | bytes 3440648 | tf_op jit(solution)/shard_map/ppermute | solution.py:37
  94.9 52.6 %collective-permute-start.11 = (bf16[256,3584]{1,0:T(8,128)(2,1)}, bf16[256,3584]{1,0:T(8,128)(2,1)S(1)}, u32[]{:S(2)}, u32[]{:S(2)}) collective-permute-start(bf16[256,3584]{1,0:T(8,128)(2,1)} %collective-permute-done.10), channel_id=1, source_target_pairs={{0,1},{1,0},{2,3},{3,2},{4,5},{5,4},{6,7},{7,6},{8,9},{9,8},{10,11... | collective-permute-start | bytes 5505032 | tf_op jit(solution)/shard_map/ppermute | solution.py:37
  118.7 2.3 copy-start.4
  118.7 30.0 %collective-permute-start.8 = (bf16[3584,256]{1,0:T(8,128)(2,1)}, bf16[3584,256]{1,0:T(8,128)(2,1)}, u32[]{:S(2)}, u32[]{:S(2)}) collective-permute-start(bf16[3584,256]{1,0:T(8,128)(2,1)} %collective-permute-done.7), channel_id=1, source_target_pairs={{0,1},{1,0},{2,3},{3,2},{4,5},{5,4},{6,7},{7,6},{8,9},{9,8},{10,11... | collective-permute-start | bytes 5505032 | tf_op jit(solution)/shard_map/ppermute | solution.py:37
  142.4 1.5 copy-start.6
  142.4 81.3 %collective-permute-start = (bf16[64,3584]{1,0:T(8,128)(2,1)S(1)}, bf16[64,3584]{1,0:T(8,128)(2,1)}, u32[]{:S(2)}, u32[]{:S(2)}) collective-permute-start(bf16[64,3584]{1,0:T(8,128)(2,1)S(1)} %bitcast.88), channel_id=1, source_target_pairs={{0,16},{1,17},{2,18},{3,19},{4,20},{5,21},{6,22},{7,23},{8,24},{9,... | collective-permute-start | bytes 1376264 | tf_op jit(solution)/shard_map/ppermute | solution.py:37
  145.0 1.2 copy-start.12
  146.2 1.2 copy-start.14
  147.5 1.2 copy-start.16
  163.9 2.6 %copy-start.15 = (bf16[3584,256]{1,0:T(8,128)(2,1)S(1)}, bf16[3584,256]{1,0:T(8,128)(2,1)}, u32[]{:S(2)}) copy-start(bf16[3584,256]{1,0:T(8,128)(2,1)} %copy-done.14) | copy-start | bytes 5505028
  165.3 6.2 %copy-start.3 = (bf16[40,3584]{1,0:T(8,128)(2,1)S(1)}, bf16[40,3584]{1,0:T(8,128)(2,1)}, u32[]{:S(2)}) copy-start(bf16[40,3584]{1,0:T(8,128)(2,1)} %get-tuple-element.51) | copy-start | bytes 860164
  165.3 6.2 %copy-start.11 = (bf16[1,1,256,3584]{3,2,1,0:T(8,128)(2,1)S(1)}, bf16[1,1,256,3584]{3,2,1,0:T(8,128)(2,1)}, u32[]{:S(2)}) copy-start(bf16[1,1,256,3584]{3,2,1,0:T(8,128)(2,1)} %param.17) | copy-start | bytes 5505028
  165.3 6.2 %copy-start.13 = (bf16[256,3584]{1,0:T(8,128)(2,1)S(1)}, bf16[256,3584]{1,0:T(8,128)(2,1)}, u32[]{:S(2)}) copy-start(bf16[256,3584]{1,0:T(8,128)(2,1)} %copy-done.12) | copy-start | bytes 5505028
  165.3 6.2 %copy-start.17 = (bf16[256,3584]{1,0:T(8,128)(2,1)S(1)}, bf16[256,3584]{1,0:T(8,128)(2,1)}, u32[]{:S(2)}) copy-start(bf16[256,3584]{1,0:T(8,128)(2,1)} %copy-done.16) | copy-start | bytes 5505028
  165.4 19.5 %collective-permute-start.12 = (bf16[40,3584]{1,0:T(8,128)(2,1)S(1)}, bf16[40,3584]{1,0:T(8,128)(2,1)S(1)}, u32[]{:S(2)}, u32[]{:S(2)}) collective-permute-start(bf16[40,3584]{1,0:T(8,128)(2,1)S(1)} %get-tuple-element.35), channel_id=1, source_target_pairs={{0,16},{1,17},{2,18},{3,19},{4,20},{5,21},{6,22},{7,23},{8,24},{9,... | collective-permute-start | bytes 860168 | tf_op jit(solution)/shard_map/ppermute | solution.py:37
  175.6 53.3 %slice-start = ((s8[4587520]{0:T(1024)(128)(4,1)}), s8[4194304]{0:T(1024)(128)(4,1)S(1)}, s32[]{:S(2)}) async-start(s8[4587520]{0:T(1024)(128)(4,1)} %bitcast.92), calls=%async_computation | async-start | bytes 8388608
  175.7 6.5 %collective-permute-start.33 = (bf16[160,512]{1,0:T(8,128)(2,1)S(1)}, bf16[160,512]{1,0:T(8,128)(2,1)S(1)}, u32[]{:S(2)}, u32[]{:S(2)}) collective-permute-start(bf16[160,512]{1,0:T(8,128)(2,1)S(1)} %get-tuple-element.37), channel_id=1, source_target_pairs={{0,3},{1,2},{2,1},{3,0},{4,7},{5,6},{6,5},{7,4},{8,11},{9,10},{10,... | collective-permute-start | bytes 491528 | tf_op jit(solution)/shard_map/ppermute | solution.py:37
  175.7 8.3 %collective-permute-start.32 = (bf16[160,512]{1,0:T(8,128)(2,1)S(1)}, bf16[160,512]{1,0:T(8,128)(2,1)S(1)}, u32[]{:S(2)}, u32[]{:S(2)}) collective-permute-start(bf16[160,512]{1,0:T(8,128)(2,1)S(1)} %get-tuple-element.38), channel_id=1, source_target_pairs={{0,2},{1,3},{2,0},{3,1},{4,6},{5,7},{6,4},{7,5},{8,10},{9,11},{10,... | collective-permute-start | bytes 491528 | tf_op jit(solution)/shard_map/ppermute | solution.py:37
  176.3 52.5 %slice-start.1 = ((s8[4587520]{0:T(1024)(128)(4,1)}), s8[393216]{0:T(1024)(128)(4,1)S(1)}, s32[]{:S(2)}) async-start(s8[4587520]{0:T(1024)(128)(4,1)} %bitcast.92), calls=%async_computation.1 | async-start | bytes 786432
  176.3 8.4 %collective-permute-start.31 = (bf16[160,512]{1,0:T(8,128)(2,1)S(1)}, bf16[160,512]{1,0:T(8,128)(2,1)S(1)}, u32[]{:S(2)}, u32[]{:S(2)}) collective-permute-start(bf16[160,512]{1,0:T(8,128)(2,1)S(1)} %get-tuple-element.39), channel_id=1, source_target_pairs={{0,1},{1,0},{2,3},{3,2},{4,5},{5,4},{6,7},{7,6},{8,9},{9,8},{10,11... | collective-permute-start | bytes 491528 | tf_op jit(solution)/shard_map/ppermute | solution.py:37
  182.1 2.0 copy-start.5
  182.1 2.6 %copy-start.7 = (bf16[160,3584]{1,0:T(8,128)(2,1)S(1)}, bf16[160,3584]{1,0:T(8,128)(2,1)}, u32[]{:S(2)}) copy-start(bf16[160,3584]{1,0:T(8,128)(2,1)} %copy-done.6) | copy-start | bytes 3440644
  182.2 67.9 %collective-permute-start.16 = (bf16[64,3584]{1,0:T(8,128)(2,1)S(1)}, bf16[64,3584]{1,0:T(8,128)(2,1)S(1)}, u32[]{:S(2)}, u32[]{:S(2)}) collective-permute-start(bf16[64,3584]{1,0:T(8,128)(2,1)S(1)} %bitcast.89), channel_id=1, source_target_pairs={{0,16},{1,17},{2,18},{3,19},{4,20},{5,21},{6,22},{7,23},{8,24},{9,... | collective-permute-start | bytes 1376264 | tf_op jit(solution)/shard_map/ppermute | solution.py:37
  184.0 44.8 %collective-permute-start.30 = (bf16[160,3584]{1,0:T(8,128)(2,1)S(1)}, bf16[160,3584]{1,0:T(8,128)(2,1)S(1)}, u32[]{:S(2)}, u32[]{:S(2)}) collective-permute-start(bf16[160,3584]{1,0:T(8,128)(2,1)S(1)} %copy-done.5), channel_id=1, source_target_pairs={{0,1},{1,0},{2,3},{3,2},{4,5},{5,4},{6,7},{7,6},{8,9},{9,8},{10,11... | collective-permute-start | bytes 3440648 | tf_op jit(solution)/shard_map/ppermute | solution.py:37
  184.7 47.7 %collective-permute-start.36 = (bf16[160,3584]{1,0:T(8,128)(2,1)S(1)}, bf16[160,3584]{1,0:T(8,128)(2,1)S(1)}, u32[]{:S(2)}, u32[]{:S(2)}) collective-permute-start(bf16[160,3584]{1,0:T(8,128)(2,1)S(1)} %copy-done.7), channel_id=1, source_target_pairs={{0,1},{1,0},{2,3},{3,2},{4,5},{5,4},{6,7},{7,6},{8,9},{9,8},{10,11... | collective-permute-start | bytes 3440648 | tf_op jit(solution)/shard_map/ppermute | solution.py:37
  184.8 10.5 %collective-permute-start.13 = (bf16[40,3584]{1,0:T(8,128)(2,1)S(1)}, bf16[40,3584]{1,0:T(8,128)(2,1)S(1)}, u32[]{:S(2)}, u32[]{:S(2)}) collective-permute-start(bf16[40,3584]{1,0:T(8,128)(2,1)S(1)} %get-tuple-element.34), channel_id=1, source_target_pairs={{0,28},{1,29},{2,30},{3,31},{4,16},{5,17},{6,18},{7,19},{8,20},{9,... | collective-permute-start | bytes 860168 | tf_op jit(solution)/shard_map/ppermute | solution.py:37
  195.3 16.3 %collective-permute-start.14 = (bf16[40,3584]{1,0:T(8,128)(2,1)S(1)}, bf16[40,3584]{1,0:T(8,128)(2,1)S(1)}, u32[]{:S(2)}, u32[]{:S(2)}) collective-permute-start(bf16[40,3584]{1,0:T(8,128)(2,1)S(1)} %get-tuple-element.33), channel_id=1, source_target_pairs={{0,24},{1,25},{2,26},{3,27},{4,28},{5,29},{6,30},{7,31},{8,16},{9,... | collective-permute-start | bytes 860168 | tf_op jit(solution)/shard_map/ppermute | solution.py:37
  211.7 10.5 %collective-permute-start.15 = (bf16[40,3584]{1,0:T(8,128)(2,1)S(1)}, bf16[40,3584]{1,0:T(8,128)(2,1)S(1)}, u32[]{:S(2)}, u32[]{:S(2)}) collective-permute-start(bf16[40,3584]{1,0:T(8,128)(2,1)S(1)} %get-tuple-element.32), channel_id=1, source_target_pairs={{0,20},{1,21},{2,22},{3,23},{4,24},{5,25},{6,26},{7,27},{8,28},{9,... | collective-permute-start | bytes 860168 | tf_op jit(solution)/shard_map/ppermute | solution.py:37
  222.2 17.9 %collective-permute-start.24 = (bf16[40,3584]{1,0:T(8,128)(2,1)S(1)}, bf16[40,3584]{1,0:T(8,128)(2,1)S(1)}, u32[]{:S(2)}, u32[]{:S(2)}) collective-permute-start(bf16[40,3584]{1,0:T(8,128)(2,1)S(1)} %get-tuple-element.22), channel_id=1, source_target_pairs={{0,16},{1,17},{2,18},{3,19},{4,20},{5,21},{6,22},{7,23},{8,24},{9,... | collective-permute-start | bytes 860168 | tf_op jit(solution)/shard_map/ppermute | solution.py:37
  223.8 16.3 %collective-permute-start.25 = (bf16[40,3584]{1,0:T(8,128)(2,1)S(1)}, bf16[40,3584]{1,0:T(8,128)(2,1)S(1)}, u32[]{:S(2)}, u32[]{:S(2)}) collective-permute-start(bf16[40,3584]{1,0:T(8,128)(2,1)S(1)} %get-tuple-element.23), channel_id=1, source_target_pairs={{0,28},{1,29},{2,30},{3,31},{4,16},{5,17},{6,18},{7,19},{8,20},{9,... | collective-permute-start | bytes 860168 | tf_op jit(solution)/shard_map/ppermute | solution.py:37
  228.8 20.9 %collective-permute-start.26 = (bf16[40,3584]{1,0:T(8,128)(2,1)S(1)}, bf16[40,3584]{1,0:T(8,128)(2,1)S(1)}, u32[]{:S(2)}, u32[]{:S(2)}) collective-permute-start(bf16[40,3584]{1,0:T(8,128)(2,1)S(1)} %get-tuple-element.24), channel_id=1, source_target_pairs={{0,24},{1,25},{2,26},{3,27},{4,28},{5,29},{6,30},{7,31},{8,16},{9,... | collective-permute-start | bytes 860168 | tf_op jit(solution)/shard_map/ppermute | solution.py:37
  232.4 17.4 %collective-permute-start.27 = (bf16[40,3584]{1,0:T(8,128)(2,1)S(1)}, bf16[40,3584]{1,0:T(8,128)(2,1)S(1)}, u32[]{:S(2)}, u32[]{:S(2)}) collective-permute-start(bf16[40,3584]{1,0:T(8,128)(2,1)S(1)} %get-tuple-element.25), channel_id=1, source_target_pairs={{0,20},{1,21},{2,22},{3,23},{4,24},{5,25},{6,26},{7,27},{8,28},{9,... | collective-permute-start | bytes 860168 | tf_op jit(solution)/shard_map/ppermute | solution.py:37

commit v2 on v1

v2 whole, which is shorter than its diff:
```python
import jax
import jax.numpy as jnp
from jax import lax
from jax.experimental import pallas as pl
from jax.experimental.pallas import tpu as pltpu
from jax.sharding import PartitionSpec as P

GROUP = 4
LANES = 128
F32 = jnp.float32
BF16 = jnp.bfloat16
VMEM = pl.BlockSpec(memory_space=pltpu.VMEM)
SMEM = pl.BlockSpec(memory_space=pltpu.SMEM)
ANY = pl.BlockSpec(memory_space=pl.ANY)
LIMIT = pltpu.CompilerParams(vmem_limit_bytes=12 * 2**20)


def after(values, *before):
    values = tuple(values)
    return lax.optimization_barrier((values, before))[0]


def dot(left, right, contract):
    return lax.dot_general(left, right, ((contract[:1], contract[1:]), ((), ())), preferred_element_type=F32)


def shape(*dims, dtype=BF16):
    return jax.ShapeDtypeStruct(dims, dtype)


def cost(gflops, mib):
    return pl.CostEstimate(flops=int(gflops * 1e9), bytes_accessed=mib * 2**20, transcendentals=0)


def build_kernel(
    experts, cap, mine_ref, fr_ref, fg_ref, br_ref, bg_ref, f_any, x_any, g_any, *refs
):
    outs, refs = refs[:experts], refs[experts:]
    table_f, table_b, f_ref, x_ref, g_ref, sems = refs
    copies = [
        pltpu.make_async_copy(src, dst, sems.at[i])
        for i, (src, dst) in enumerate(((f_any, f_ref), (x_any, x_ref), (g_any, g_ref)))
    ]
    for copy in copies:
        copy.start()
    tok_rows = f_ref.shape[0]
    wide = table_b.shape[2]
    mine = mine_ref[0]
    row = lax.broadcasted_iota(jnp.int32, (tok_rows, tok_rows), 0)
    col = lax.broadcasted_iota(jnp.int32, (tok_rows, tok_rows), 1)
    earlier = (row < col).astype(F32).astype(BF16)
    same = (row == col).astype(F32).astype(BF16)
    slot = lax.broadcasted_iota(jnp.int32, (cap, tok_rows), 0).astype(F32)
    at = [lax.rem(mine + k, experts) for k in range(experts)]

    def placed(routes, gates):
        named = [((routes[0:1] == e) | (routes[1:2] == e)).astype(F32) for e in at]
        gate = [jnp.where(routes[0:1] == e, gates[0:1], gates[1:2]) for e in at]
        rows = -(-experts // 16) * 16
        padded = jnp.concatenate(named + [jnp.zeros((rows - experts, tok_rows), F32)], axis=0)
        prefix = dot(padded.astype(BF16), earlier, (1, 0))
        hits = [jnp.where(prefix[k:k + 1] == slot, named[k], 0.0) for k in range(experts)]
        return hits, [hits[k] * gate[k] for k in range(experts)]

    def by_token(slots):
        rest = jnp.zeros((wide - experts * cap, tok_rows), F32)
        full = jnp.concatenate(slots + [rest], axis=0)
        return dot(same, full.astype(BF16), (1, 1)).astype(BF16)

    hits_f, gated_f = placed(fr_ref[...], fg_ref[...])
    hits_b, gated_b = placed(br_ref[...], bg_ref[...])
    for copy in copies:
        copy.wait()
    for k in range(experts):
        hits = hits_b[k].astype(BF16)
        rows_f = dot(hits_f[k].astype(BF16), f_ref[...], (1, 0))
        rows_x = dot(hits, x_ref[...], (1, 0))
        rows_g = dot(hits, g_ref[...], (1, 0)) * jnp.sum(gated_b[k], axis=1, keepdims=True)
        rows = jnp.concatenate([rows_f, rows_x, rows_g], axis=0)
        outs[k][...] = rows.astype(BF16)
    table_f[0] = by_token(gated_f)
    table_f[1] = by_token([part - part.astype(BF16).astype(F32) for part in gated_f])
    table_b[0] = by_token(hits_b)


def pack_kernel(side, up, down, packed):
    packed[:side] = down[...]
    for j in range(0, up.shape[0], side):
        packed[side:, j:j + side] = up[j:j + side]


def up_blocks(ref, side):
    width = max(ref.shape)
    if ref.shape[0] == width:
        return [ref[j:j + side] for j in range(0, width, side)]
    return [ref[side:, j:j + side] for j in range(0, width, side)]


def first_layer(rows_f, rows_x, rows_g, up, down):
    count, side = rows_f.shape[0], down.shape[0]
    rows = jnp.concatenate([rows_f[...], rows_x[...]], axis=0)
    if up.shape[1] == side:
        pre = dot(rows, up[...], (1, 0))
    else:
        pre = sum(
            dot(rows[:, j * side:(j + 1) * side], block, (1, 0))
            for j, block in enumerate(up_blocks(up, side))
        )
    sigma = 1.0 / (1.0 + jnp.exp(-pre))
    acts = (pre * sigma).astype(BF16)
    pre, sigma = pre[count:], sigma[count:]
    dact = dot(rows_g[...], down[...], (1, 1))
    dpre = (dact * (sigma * (1.0 + pre * (1.0 - sigma)))).astype(BF16)
    return acts[:count], acts[count:], dpre


def local(
    fwd_acts, fwd_routes, fwd_gates, back_acts, back_routes, back_gates, back_grads, w_up, w_down
):
    devices = lax.axis_size("expert")
    sections = lax.axis_size("pipe")
    experts = devices // GROUP
    tok_rows, width = fwd_acts.shape[1:]
    cap = GROUP * (5 * tok_rows * fwd_routes.shape[2] // (4 * devices))
    mine = lax.axis_index("expert") // GROUP
    hidden = w_up.shape[3]
    count = experts * cap
    wide = -(-count // LANES) * LANES
    tile = width // 7

    def send(value, planes=0, flip=0, pipes=0):
        pairs = []
        for section in range(sections):
            for place in range(devices):
                target = (place // GROUP + planes) % experts * GROUP + (place % GROUP ^ flip)
                goal = (section + pipes) % sections * devices + target
                pairs.append((section * devices + place, goal))
        return lax.ppermute(value, ("pipe", "expert"), pairs)

    fwd_input, back_input, out_grad = fwd_acts[0], back_acts[0], back_grads[0]
    up_own, down_own = w_up[0, 0], w_down[0, 0]
    away = range(1, experts)

    def both_ways(forth, back, planes=0):
        if sections == 2:
            parts = send(jnp.concatenate([forth, back], axis=0), planes=planes, pipes=1)
            return parts[:forth.shape[0]], parts[forth.shape[0]:]
        return send(forth, planes=planes, pipes=1), send(back, planes=planes, pipes=-1)

    up_c, down_c = send(up_own, flip=1), send(down_own, flip=1)
    packed_own = pl.pallas_call(
        lambda *refs: pack_kernel(hidden, *refs),
        out_shape=shape(2 * hidden, width),
        in_specs=[VMEM] * 2,
        out_specs=VMEM,
        name="pack",
        compiler_params=LIMIT,
        cost_estimate=cost(0, 8),
    )(up_own, down_own)
    built = pl.pallas_call(
        lambda *refs: build_kernel(experts, cap, *refs),
        out_shape=[shape(3 * cap, width)] * experts
        + [shape(2, tok_rows, wide), shape(1, tok_rows, wide)],
        in_specs=[SMEM] + [VMEM] * 4 + [ANY] * 3,
        out_specs=[VMEM] * (experts + 2),
        scratch_shapes=[pltpu.VMEM((tok_rows, width), BF16)] * 3 + [pltpu.SemaphoreType.DMA((3,))],
        name="build",
        compiler_params=LIMIT,
        cost_estimate=cost(1, 5),
    )(
        mine.reshape(1), fwd_routes[0].T, fwd_gates[0].T, back_routes[0].T, back_gates[0].T,
        fwd_input, back_input, out_grad,
    )
    table_f, table_b = built[experts:]

    tables = table_f.transpose(1, 0, 2).reshape(tok_rows, 2 * wide), jnp.concatenate([table_b[0]] * 2, axis=1)
    base_f = jnp.concatenate([fwd_input, tables[0]], axis=1)
    base_b = jnp.concatenate([out_grad, tables[1]], axis=1)
    *rows_out, packed_own, base_f, base_b = after([*built[1:experts], packed_own, base_f, base_b], up_c, down_c)
    got = [built[0]] + [send(rows_out[k - 1], planes=k) for k in away]
    packed_y = send(packed_own, flip=2)
    base_f, base_b = both_ways(base_f, base_b)
    packed_d = send(packed_y, flip=1)

    rows_f, rows_x, rows_g = (
        jnp.concatenate([part[i * cap:(i + 1) * cap] for part in got], axis=0) for i in range(3)
    )
    (rows_f,) = after([rows_f], base_f, base_b)

    def own_kernel(rows_f, rows_x, rows_g, *refs):
        weights, outs = refs[:4], refs[4:]
        for q in range(2):
            for out, value in zip(outs, first_layer(rows_f, rows_x, rows_g, *weights[2 * q:2 * q + 2])):
                out[:, q * hidden:(q + 1) * hidden] = value

    act_f01, act_b01, dpre01 = pl.pallas_call(
        own_kernel,
        out_shape=[shape(count, 2 * hidden)] * 3,
        in_specs=[VMEM] * 7,
        out_specs=[VMEM] * 3,
        name="own",
        compiler_params=LIMIT,
        cost_estimate=cost(2, 12),
    )(rows_f, rows_x, rows_g, up_own, down_own, up_c, down_c)

    def near_kernel(rows_f, rows_x, rows_g, weights, *outs):
        for out, value in zip(outs, first_layer(rows_f, rows_x, rows_g, weights, weights.at[:hidden])):
            out[...] = value

    act_f2, act_b2, dpre2 = pl.pallas_call(
        near_kernel,
        out_shape=[shape(count, hidden)] * 3,
        in_specs=[VMEM] * 4,
        out_specs=[VMEM] * 3,
        name="near",
        compiler_params=LIMIT,
        cost_estimate=cost(1, 6),
    )(rows_f, rows_x, rows_g, packed_y)

    def back_kernel(rows_f, rows_x, rows_g, act_b01, act_b2, dpre01, dpre2, up_own, up_c, packed_y, packed_d, *outs):
        out, act_f, sent, hid_own, hid_c = outs
        acts = first_layer(rows_f, rows_x, rows_g, packed_d, packed_d.at[:hidden])
        act_f[...] = acts[0]
        act_b = [act_b01[:, :hidden], act_b01[:, hidden:], act_b2[...], acts[1]]
        dpre = [dpre01[:, :hidden], dpre01[:, hidden:], dpre2[...], acts[2]]
        blocks = [up_blocks(ref, hidden) for ref in (up_own, up_c, packed_y, packed_d)]
        for j in range(width // hidden):
            out[:, j * hidden:(j + 1) * hidden] = sum(
                dot(dpre[q], blocks[q][j], (1, 1)) for q in range(GROUP)
            ).astype(BF16)
        sent[:, :width] = rows_g[...]
        for q in range(GROUP):
            target, low = [(hid_own, 0), (hid_c, 0), (sent, width), (sent, width + 2 * hidden)][q]
            target[:, low:low + hidden] = act_b[q]
            target[:, low + hidden:low + 2 * hidden] = dpre[q]

    out_b, act_f3, sent, hid_own, hid_c = pl.pallas_call(
        back_kernel,
        out_shape=[
            shape(count, width), shape(count, hidden), shape(count, width + 4 * hidden),
            shape(count, 2 * hidden), shape(count, 2 * hidden),
        ],
        in_specs=[VMEM] * 11,
        out_specs=[VMEM] * 5,
        name="back",
        compiler_params=LIMIT,
        cost_estimate=cost(2.4, 16),
    )(rows_f, rows_x, rows_g, act_b01, act_b2, dpre01, dpre2, up_own, up_c, packed_y, packed_d)

    def forward_kernel(act01, act2, act3, down_own, down_c, packed_y, packed_d, out):
        acts = [act01[:, :hidden], act01[:, hidden:], act2[...], act3[...]]
        for start in range(0, width, tile):
            span = slice(start, start + tile)
            out[:, span] = sum(
                dot(acts[q], weights[:hidden, span], (1, 0))
                for q, weights in enumerate((down_own, down_c, packed_y, packed_d))
            ).astype(BF16)

    rows_late = after([rows_x, rows_g], packed_d)
    x_c, g_c = send(rows_late[0], flip=1), send(rows_late[1], flip=1)
    out_f = pl.pallas_call(
        forward_kernel,
        out_shape=shape(count, width),
        in_specs=[VMEM] * 7,
        out_specs=VMEM,
        name="forward",
        compiler_params=LIMIT,
        cost_estimate=cost(1.3, 12),
    )(*after([act_f01], out_b, x_c, g_c), act_f2, act_f3, down_own, down_c, packed_y, packed_d)

    ret_f, ret_b = zip(*[
        both_ways(out_f[k * cap:(k + 1) * cap], out_b[k * cap:(k + 1) * cap], -k) for k in range(experts)
    ])

    x_y = send(*after([rows_x], packed_y), flip=2)
    sent_y = send(*after([sent], x_y, out_f), flip=2)
    x_late, hid_late = after([x_y, hid_c], sent_y)
    x_d, hid_c = send(x_late, flip=1), send(hid_late, flip=1)
    sent_d = send(sent_y, flip=1)
    hid_y, hid_d = sent_y[:, width:width + 2 * hidden], sent_d[:, width + 2 * hidden:]
    x_all = jnp.concatenate([rows_x, x_c, x_y, x_d], axis=0)
    g_all = jnp.concatenate([rows_g, g_c, sent_y[:, :width], sent_d[:, :width]], axis=0)
    hid_all = jnp.concatenate([hid_own, hid_c, hid_y, hid_d], axis=0)
    grad_up = dot(x_all, hid_all[:, hidden:], (0, 0))
    grad_down = dot(hid_all[:, :hidden], g_all, (0, 0))

    def combine(pieces, base, *parts):
        def kernel(base, *refs):
            parts, out = refs[:-1], refs[-1]
            table = base[:, width:]
            for start in range(0, width, tile):
                span = slice(start, start + tile)
                total = base[:, span].astype(F32)
                for k, part in enumerate(parts):
                    for piece in range(pieces):
                        low = piece * wide + k * cap
                        total = total + dot(table[:, low:low + cap], part[:, span], (1, 0))
                out[:, span] = total.astype(BF16)

        return pl.pallas_call(
            kernel,
            out_shape=shape(tok_rows, width),
            in_specs=[VMEM] * (1 + len(parts)),
            out_specs=VMEM,
            name="combine",
            compiler_params=LIMIT,
            cost_estimate=cost(0.1, 2),
        )(base, *parts)

    base_f, base_b = after([base_f, base_b], grad_up, grad_down)
    fwd_next = combine(2, base_f, *ret_f)
    back_next = combine(1, base_b, *ret_b)
    return (fwd_next[None], back_next[None], grad_up[None, None], grad_down[None, None])


def solution(mesh):
    rows = P("pipe", "expert", None)
    slices = P("pipe", "expert", None, None)
    return jax.shard_map(
        local,
        mesh=mesh,
        in_specs=(rows,) * 7 + (slices,) * 2,
        out_specs=(rows, rows, slices, slices),
        check_vma=False,
    )
```

time: 252 us -> 177 us (0.70)
  matrix products: 52.8 us -> 6.93 us
  starting transfers between devices: 57 us -> 23.7 us
  Pallas kernels: 0 us -> 17.6 us
  local copies, waits for them, and re-layouts: 17.5 us -> 8.01 us
  other arithmetic: 4.84 us -> 0.65 us
    dot_general x22 -> x2, matrix products: 52.8 us -> 6.93 us  [dot(): lax.dot_general(left, right, ((contract[:1], contract[1:]), ((), ())), pr...]
    ppermute x37 -> x19, starting transfers between devices: 57 us -> 23.7 us  [send(): return lax.ppermute(value, ('pipe', 'expert'), pairs)]
    pallas_call x0 -> x8, Pallas kernels: none -> 17.6 us  [the longest x1 5.2 us: local(): pl.pallas_call(back_kernel, out_shape=[shape(count, width), shape(count,...]
    unnamed x59 -> x34, local copies, waits for them, and re-layouts: 12.8 us -> 7.42 us
    ppermute x37 -> x19, waiting for transfers between devices: 118 us -> 117 us  [send(): return lax.ppermute(value, ('pipe', 'expert'), pairs)]
  transfers between devices with their start and end apart: 37 -> 19, of which waited for: 10 -> 8; matrix products, arithmetic and copies ran while one was open for 28% -> 1% of each run, Pallas kernels for 0% -> 8%
where the time goes in v2:
time: 177 us; the launch traced here: 175 us
  waiting for transfers between devices  117 us (66%)
  starting transfers between devices  23.7 us (13%)
  Pallas kernels  17.6 us (10%)
  local copies, waits for them, and re-layouts  8.01 us (5%)
  matrix products  6.93 us (4%)
    ppermute x19, waiting for transfers between devices, send(): return lax.ppermute(value, ('pipe', 'expert'), pairs)  117 us
    ppermute x19, starting transfers between devices, send(): return lax.ppermute(value, ('pipe', 'expert'), pairs)  23.7 us
    unnamed x34, local copies, waits for them, and re-layouts  7.42 us
    dot_general x2, matrix products, dot(): lax.dot_general(left, right, ((contract[:1], contract[1:]), ((), ())), pr...  6.93 us
    pallas_call x1, Pallas kernels, local(): pl.pallas_call(back_kernel, out_shape=[shape(count, width), shape(count,...  5.2 us
    pallas_call x1, Pallas kernels, local(): pl.pallas_call(own_kernel, out_shape=[shape(count, 2 * hidden)] * 3, in_s...  3.91 us
  transfers between devices with their start and end apart: 19, of which 8 were waited for; matrix products, arithmetic and copies ran while one was open for 1% of the time, Pallas kernels for 8%

profile of v2, /device:TPU:0, one launch (start us, length us, event | category | flops | bytes accessed | tf_op | source)
XLA Modules:
  0.0 175.0 jit_solution(12456000924159075574)
XLA Ops:
  0.6 0.5 collective-permute-start
  1.2 0.1 collective-permute-start.1
  1.2 1.5 copy-done
  2.7 1.5 copy-done.2
  4.3 0.2 pack.1
  4.5 0.0 copy-start.4
  4.5 1.8 %copy-done.4 = bf16[512,3584]{1,0:T(8,128)(2,1)} copy-done((bf16[512,3584]{1,0:T(8,128)(2,1)}, bf16[512,3584]{1,0:T(8,128)(2,1)S(1)}, u32[]{:S(2)}) %copy-start.4) | copy-done | bytes 3670040
  6.4 2.3 %build.1 = (bf16[120,3584]{1,0:T(8,128)(2,1)S(1)}, bf16[120,3584]{1,0:T(8,128)(2,1)S(1)}, bf16[120,3584]{1,0:T(8,128)(2,1)S(1)}, bf16[120,3584]{1,0:T(8,128)(2,1...) custom-call(s32[1]{0:T(128)} %bitcast.refs_0_, s32[2,64]{1,0:T(2,128)S(1)} %bitcast.43, ...), custom_call_target="tpu_custom_call" | custom-call | flops 1000000000 | bytes 5242880 | tf_op jit(solution)/shard_map/build/pallas_call | solution.py:160
  8.7 0.1 pad_maximum_fusion.9
  8.8 0.0 collective-permute-done.refs_2_.up_c
  8.9 0.0 collective-permute-done.1.refs_3_.down_c
  8.9 3.0 %collective-permute-start.6 = (bf16[512,3584]{1,0:T(8,128)(2,1)S(1)}, bf16[512,3584]{1,0:T(8,128)(2,1)S(1)}, u32[]{:S(2)}, u32[]{:S(2)}) collective-permute-start(bf16[512,3584]{1,0:T(8,128)(2,1)S(1)} %copy-done.5), channel_id=1, source_target_pairs={{0,2},{1,3},{2,0},{3,1},{4,6},{5,7},{6,4},{7,5},{8,10},{9,11},{10,... | collective-permute-start | bytes 11010056 | tf_op jit(solution)/shard_map/ppermute | solution.py:138
  11.9 1.6 collective-permute-start.3
  13.5 0.1 constant_dynamic-update-slice_fusion.11
  13.6 2.7 %collective-permute-start.4 = (bf16[120,3584]{1,0:T(8,128)(2,1)S(1)}, bf16[120,3584]{1,0:T(8,128)(2,1)S(1)}, u32[]{:S(2)}, u32[]{:S(2)}) collective-permute-start(bf16[120,3584]{1,0:T(8,128)(2,1)S(1)} %get-tuple-element.46), channel_id=1, source_target_pairs={{0,8},{1,9},{2,10},{3,11},{4,12},{5,13},{6,14},{7,15},{8,0},{9,1},... | collective-permute-start | bytes 2580488 | tf_op jit(solution)/shard_map/ppermute | solution.py:138
  16.2 1.3 collective-permute-start.5
  17.6 0.1 pad_maximum_fusion.3
  17.6 1.6 collective-permute-start.2
  19.2 16.6 %collective-permute-done.3 = bf16[120,3584]{1,0:T(8,128)(2,1)S(1)} collective-permute-done((bf16[120,3584]{1,0:T(8,128)(2,1)S(1)}, bf16[120,3584]{1,0:T(8,128)(2,1)S(1)}, u32[]{:S(2)}, u32[]{:S(2)}) %collective-permute-start.3) | collective-permute-done | bytes 860192 | tf_op jit(solution)/shard_map/ppermute | solution.py:138
  35.8 0.1 constant_dynamic-update-slice_fusion.10
  35.9 55.5 %collective-permute-done.6.weights.packed_y = bf16[512,3584]{1,0:T(8,128)(2,1)S(1)} collective-permute-done((bf16[512,3584]{1,0:T(8,128)(2,1)S(1)}, bf16[512,3584]{1,0:T(8,128)(2,1)S(1)}, u32[]{:S(2)}, u32[]{:S(2)}) %collective-permute-start.6) | collective-permute-done | bytes 3670048 | tf_op jit(solution)/shard_map/ppermute | solution.py:138
  91.5 0.0 collective-permute-start.7
  91.5 0.1 constant_dynamic-update-slice_fusion.9
  91.6 0.1 constant_dynamic-update-slice_fusion.8
  91.7 0.1 pad_maximum_fusion.2.rows_f
  91.8 0.1 pad_maximum_fusion.1.rows_g
  91.9 0.0 copy-start.1
  91.9 0.0 copy-start.3
  91.9 0.1 pad_maximum_fusion.rows_x
  92.0 0.1 fusion.6
  92.1 1.3 copy-done.1
  93.4 0.6 copy-done.3
  94.0 3.9 %own.1 = (bf16[160,512]{1,0:T(8,128)(2,1)S(1)}, bf16[160,512]{1,0:T(8,128)(2,1)S(1)}, bf16[160,512]{1,0:T(8,128)(2,1)S(1)}) custom-call(bf16[160,3584]{1,0:T(8,128)(2,1)S(1)} %pad_maximum_fusion.2.rows_f, bf16[160,3584]{1,0:T(8,128)(2,1)S(1)} %pad_maximum_fusion.rows_x, bf16[160,3584]{1,0:T(8,128)(2,1)S(1)} %pad_maximum_fusion.1.rows_g, ...), custom_call_target="tpu_custom_call" | custom-call | flops 2000000000 | bytes 12582912 | tf_op jit(solution)/shard_map/own/pallas_call | solution.py:196
  97.9 1.8 %collective-permute-start.9 = (bf16[160,3584]{1,0:T(8,128)(2,1)S(1)}, bf16[160,3584]{1,0:T(8,128)(2,1)S(1)}, u32[]{:S(2)}, u32[]{:S(2)}) collective-permute-start(bf16[160,3584]{1,0:T(8,128)(2,1)S(1)} %pad_maximum_fusion.rows_x), channel_id=1, source_target_pairs={{0,2},{1,3},{2,0},{3,1},{4,6},{5,7},{6,4},{7,5},{8,10},{9,11},{10,... | collective-permute-start | bytes 3440648 | tf_op jit(solution)/shard_map/ppermute | solution.py:138
  99.7 1.3 near.1
  101.0 0.3 collective-permute-start.10
  101.3 0.3 collective-permute-start.8
  101.6 5.2 %back.1 = (bf16[160,3584]{1,0:T(8,128)(2,1)S(1)}, bf16[160,256]{1,0:T(8,128)(2,1)S(1)}, bf16[160,4608]{1,0:T(8,128)(2,1)S(1)}, bf16[160,512]{1,0:T(8,128)(2,1)S(1)}, bf16[160,512]{1,0:T(8,128)(2,1)S(1)}) custom-call(bf16[160,3584]{1,0:T(8,128)(2,1)S(1)} %pad_maximum_fusion.2.rows_f, bf16[160,3584]{1,0:T(8,128)(2,1)S(1)} %pad_maximum_fusion.rows_x, ...), custom_call_target="tpu_custom_call" | custom-call | flops 2400000000 | bytes 16777216 | tf_op jit(solution)/shard_map/back/pallas_call | solution.py:237
  106.8 0.1 fusion.5
  106.9 1.4 forward.1
  108.3 0.1 fusion.4
  108.4 2.5 %collective-permute-start.18 = (bf16[80,3584]{1,0:T(8,128)(2,1)S(1)}, bf16[80,3584]{1,0:T(8,128)(2,1)S(1)}, u32[]{:S(2)}, u32[]{:S(2)}) collective-permute-start(bf16[80,3584]{1,0:T(8,128)(2,1)S(1)} %pad_maximum_fusion.8), channel_id=1, source_target_pairs={{0,20},{1,21},{2,22},{3,23},{4,24},{5,25},{6,26},{7,27},{8,28},{9,... | collective-permute-start | bytes 1720328 | tf_op jit(solution)/shard_map/ppermute | solution.py:138
  111.0 2.6 %collective-permute-start.17 = (bf16[80,3584]{1,0:T(8,128)(2,1)S(1)}, bf16[80,3584]{1,0:T(8,128)(2,1)S(1)}, u32[]{:S(2)}, u32[]{:S(2)}) collective-permute-start(bf16[80,3584]{1,0:T(8,128)(2,1)S(1)} %pad_maximum_fusion.7), channel_id=1, source_target_pairs={{0,24},{1,25},{2,26},{3,27},{4,28},{5,29},{6,30},{7,31},{8,16},{9,... | collective-permute-start | bytes 1720328 | tf_op jit(solution)/shard_map/ppermute | solution.py:138
  113.7 2.5 %collective-permute-start.16 = (bf16[80,3584]{1,0:T(8,128)(2,1)S(1)}, bf16[80,3584]{1,0:T(8,128)(2,1)S(1)}, u32[]{:S(2)}, u32[]{:S(2)}) collective-permute-start(bf16[80,3584]{1,0:T(8,128)(2,1)S(1)} %pad_maximum_fusion.6), channel_id=1, source_target_pairs={{0,28},{1,29},{2,30},{3,31},{4,16},{5,17},{6,18},{7,19},{8,20},{9,... | collective-permute-start | bytes 1720328 | tf_op jit(solution)/shard_map/ppermute | solution.py:138
  116.2 0.6 collective-permute-start.15
  116.8 8.8 %collective-permute-done.9 = bf16[160,3584]{1,0:T(8,128)(2,1)S(1)} collective-permute-done((bf16[160,3584]{1,0:T(8,128)(2,1)S(1)}, bf16[160,3584]{1,0:T(8,128)(2,1)S(1)}, u32[]{:S(2)}, u32[]{:S(2)}) %collective-permute-start.9) | collective-permute-done | bytes 1146912 | tf_op jit(solution)/shard_map/ppermute | solution.py:138
  125.6 1.7 collective-permute-start.11
  127.4 0.1 constant_dynamic-update-slice_fusion.7
  127.4 0.1 constant_dynamic-update-slice_fusion.2
  127.5 0.1 constant_dynamic-update-slice_fusion.1
  127.7 23.5 %collective-permute-done.17 = bf16[80,3584]{1,0:T(8,128)(2,1)S(1)} collective-permute-done((bf16[80,3584]{1,0:T(8,128)(2,1)S(1)}, bf16[80,3584]{1,0:T(8,128)(2,1)S(1)}, u32[]{:S(2)}, u32[]{:S(2)}) %collective-permute-start.17) | collective-permute-done | bytes 573472 | tf_op jit(solution)/shard_map/ppermute | solution.py:138
  151.2 8.3 %collective-permute-done.11 = bf16[160,4608]{1,0:T(8,128)(2,1)S(1)} collective-permute-done((bf16[160,4608]{1,0:T(8,128)(2,1)S(1)}, bf16[160,4608]{1,0:T(8,128)(2,1)S(1)}, u32[]{:S(2)}, u32[]{:S(2)}) %collective-permute-start.11) | collective-permute-done | bytes 1474592 | tf_op jit(solution)/shard_map/ppermute | solution.py:138
  159.5 0.5 collective-permute-start.14
  160.0 3.2 %collective-permute-done.15 = bf16[80,3584]{1,0:T(8,128)(2,1)S(1)} collective-permute-done((bf16[80,3584]{1,0:T(8,128)(2,1)S(1)}, bf16[80,3584]{1,0:T(8,128)(2,1)S(1)}, u32[]{:S(2)}, u32[]{:S(2)}) %collective-permute-start.15) | collective-permute-done | bytes 573472 | tf_op jit(solution)/shard_map/ppermute | solution.py:138
  163.3 0.1 collective-permute-start.13
  163.4 0.1 slice_dynamic-update-slice_fusion.1
  163.5 0.1 constant_dynamic-update-slice_fusion
  163.5 0.9 collective-permute-done.14
  164.4 0.1 slice_dynamic-update-slice_fusion
  164.5 0.2 collective-permute-done.13
  164.8 3.5 %fusion = f32[256,3584]{1,0:T(8,128)} fusion(bf16[640,3584]{1,0:T(8,128)(2,1)S(1)} %slice_dynamic-update-slice_fusion, bf16[640,512]{1,0:T(8,128)(2,1)S(1)} %pad_maximum_fusion.4), kind=kOutput, calls=%fused_computation.13 | convolution fusion | flops 1174405120 | bytes 8585216 | tf_op jit(solution)/shard_map/dot_general | solution.py:24
  168.2 3.5 %fusion.2 = f32[3584,256]{1,0:T(8,128)} fusion(bf16[640,3584]{1,0:T(8,128)(2,1)S(1)} %constant_dynamic-update-slice_fusion, bf16[640,512]{1,0:T(8,128)(2,1)S(1)} %pad_maximum_fusion.4), kind=kOutput, calls=%fused_computation.15 | convolution fusion | flops 1174405120 | bytes 8585216 | tf_op jit(solution)/shard_map/dot_general | solution.py:24
  171.7 1.4 combine.3
  173.1 1.9 %combine.2 = bf16[64,3584]{1,0:T(8,128)(2,1)} custom-call(bf16[64,4096]{1,0:T(8,128)(2,1)S(1)} %get-tuple-element.68.base, bf16[40,3584]{1,0:T(8,128)(2,1)S(1)} %get-tuple-element.107.refs_0_, bf16[40,3584]{1,0:T(8,128)(2,1)S(1)} %get-tuple-element.105.refs_1_, bf16[40,3584]{1,0:T(8,128)(2,1)S(1)} %get-tuple-element.103.refs_2_, ...), custom_call_target="tpu_custom_call" | custom-call | flops 100000000 | bytes 2097152 | tf_op jit(solution)/shard_map/combine/pallas_call | solution.py:300
  (40 shorter events, 0.4 us)
Async XLA Ops:
  0.6 8.2 %collective-permute-start = (bf16[3584,256]{1,0:T(8,128)(2,1)}, bf16[3584,256]{1,0:T(8,128)(2,1)}, u32[]{:S(2)}, u32[]{:S(2)}) collective-permute-start(bf16[3584,256]{1,0:T(8,128)(2,1)} %bitcast.28), channel_id=1, source_target_pairs={{0,1},{1,0},{2,3},{3,2},{4,5},{5,4},{6,7},{7,6},{8,9},{9,8},{10,11... | collective-permute-start | bytes 5505032 | tf_op jit(solution)/shard_map/ppermute | solution.py:138
  1.2 7.7 %collective-permute-start.1 = (bf16[256,3584]{1,0:T(8,128)(2,1)}, bf16[256,3584]{1,0:T(8,128)(2,1)S(1)}, u32[]{:S(2)}, u32[]{:S(2)}) collective-permute-start(bf16[256,3584]{1,0:T(8,128)(2,1)} %bitcast.32), channel_id=1, source_target_pairs={{0,1},{1,0},{2,3},{3,2},{4,5},{5,4},{6,7},{7,6},{8,9},{9,8},{10,11... | collective-permute-start | bytes 5505032 | tf_op jit(solution)/shard_map/ppermute | solution.py:138
  1.2 1.5 copy-start
  2.7 1.5 copy-start.2
  4.2 2.1 %copy-start.6 = (bf16[1,64,3584]{2,1,0:T(8,128)(2,1)S(1)}, bf16[1,64,3584]{2,1,0:T(8,128)(2,1)}, u32[]{:S(2)}) copy-start(bf16[1,64,3584]{2,1,0:T(8,128)(2,1)} %param.9) | copy-start | bytes 1376260
  4.2 2.1 %copy-start.7 = (bf16[1,64,3584]{2,1,0:T(8,128)(2,1)S(1)}, bf16[1,64,3584]{2,1,0:T(8,128)(2,1)}, u32[]{:S(2)}) copy-start(bf16[1,64,3584]{2,1,0:T(8,128)(2,1)} %param.15) | copy-start | bytes 1376260
  4.2 2.1 %copy-start.8 = (bf16[1,64,3584]{2,1,0:T(8,128)(2,1)S(1)}, bf16[1,64,3584]{2,1,0:T(8,128)(2,1)}, u32[]{:S(2)}) copy-start(bf16[1,64,3584]{2,1,0:T(8,128)(2,1)} %param.12) | copy-start | bytes 1376260
  4.2 2.1 %copy-start.9 = (s32[1,64,2]{1,2,0:T(2,128)S(1)}, s32[1,64,2]{1,2,0:T(2,128)}, u32[]{:S(2)}) copy-start(s32[1,64,2]{1,2,0:T(2,128)} %param.10) | copy-start | bytes 1540
  4.2 2.1 %copy-start.10 = (f32[1,64,2]{1,2,0:T(2,128)S(1)}, f32[1,64,2]{1,2,0:T(2,128)}, u32[]{:S(2)}) copy-start(f32[1,64,2]{1,2,0:T(2,128)} %param.11) | copy-start | bytes 1540
  4.3 2.1 %copy-start.11 = (s32[1,64,2]{1,2,0:T(2,128)S(1)}, s32[1,64,2]{1,2,0:T(2,128)}, u32[]{:S(2)}) copy-start(s32[1,64,2]{1,2,0:T(2,128)} %param.13) | copy-start | bytes 1540
  4.3 2.1 %copy-start.12 = (f32[1,64,2]{1,2,0:T(2,128)S(1)}, f32[1,64,2]{1,2,0:T(2,128)}, u32[]{:S(2)}) copy-start(f32[1,64,2]{1,2,0:T(2,128)} %param.14) | copy-start | bytes 1540
  4.5 1.8 %copy-start.4 = (bf16[512,3584]{1,0:T(8,128)(2,1)}, bf16[512,3584]{1,0:T(8,128)(2,1)S(1)}, u32[]{:S(2)}) copy-start(bf16[512,3584]{1,0:T(8,128)(2,1)S(1)} %pack.1) | copy-start | bytes 11010052
  6.4 2.5 %copy-start.5 = (bf16[512,3584]{1,0:T(8,128)(2,1)S(1)}, bf16[512,3584]{1,0:T(8,128)(2,1)}, u32[]{:S(2)}) copy-start(bf16[512,3584]{1,0:T(8,128)(2,1)} %copy-done.4) | copy-start | bytes 11010052
  8.9 82.6 %collective-permute-start.6 = (bf16[512,3584]{1,0:T(8,128)(2,1)S(1)}, bf16[512,3584]{1,0:T(8,128)(2,1)S(1)}, u32[]{:S(2)}, u32[]{:S(2)}) collective-permute-start(bf16[512,3584]{1,0:T(8,128)(2,1)S(1)} %copy-done.5), channel_id=1, source_target_pairs={{0,2},{1,3},{2,0},{3,1},{4,6},{5,7},{6,4},{7,5},{8,10},{9,11},{10,... | collective-permute-start | bytes 11010056 | tf_op jit(solution)/shard_map/ppermute | solution.py:138
  11.9 23.9 %collective-permute-start.3 = (bf16[120,3584]{1,0:T(8,128)(2,1)S(1)}, bf16[120,3584]{1,0:T(8,128)(2,1)S(1)}, u32[]{:S(2)}, u32[]{:S(2)}) collective-permute-start(bf16[120,3584]{1,0:T(8,128)(2,1)S(1)} %get-tuple-element.45), channel_id=1, source_target_pairs={{0,4},{1,5},{2,6},{3,7},{4,8},{5,9},{6,10},{7,11},{8,12},{9,13},{1... | collective-permute-start | bytes 2580488 | tf_op jit(solution)/shard_map/ppermute | solution.py:138
  13.6 77.9 %collective-permute-start.4 = (bf16[120,3584]{1,0:T(8,128)(2,1)S(1)}, bf16[120,3584]{1,0:T(8,128)(2,1)S(1)}, u32[]{:S(2)}, u32[]{:S(2)}) collective-permute-start(bf16[120,3584]{1,0:T(8,128)(2,1)S(1)} %get-tuple-element.46), channel_id=1, source_target_pairs={{0,8},{1,9},{2,10},{3,11},{4,12},{5,13},{6,14},{7,15},{8,0},{9,1},... | collective-permute-start | bytes 2580488 | tf_op jit(solution)/shard_map/ppermute | solution.py:138
  16.2 75.4 %collective-permute-start.5 = (bf16[120,3584]{1,0:T(8,128)(2,1)S(1)}, bf16[120,3584]{1,0:T(8,128)(2,1)S(1)}, u32[]{:S(2)}, u32[]{:S(2)}) collective-permute-start(bf16[120,3584]{1,0:T(8,128)(2,1)S(1)} %get-tuple-element.47), channel_id=1, source_target_pairs={{0,12},{1,13},{2,14},{3,15},{4,0},{5,1},{6,2},{7,3},{8,4},{9,5},{1... | collective-permute-start | bytes 2580488 | tf_op jit(solution)/shard_map/ppermute | solution.py:138
  17.6 74.4 %collective-permute-start.2 = (bf16[128,4096]{1,0:T(8,128)(2,1)S(1)}, bf16[128,4096]{1,0:T(8,128)(2,1)S(1)}, u32[]{:S(2)}, u32[]{:S(2)}) collective-permute-start(bf16[128,4096]{1,0:T(8,128)(2,1)S(1)} %pad_maximum_fusion.3), channel_id=1, source_target_pairs={{0,16},{1,17},{2,18},{3,19},{4,20},{5,21},{6,22},{7,23},{8,24},{9,... | collective-permute-start | bytes 3145736 | tf_op jit(solution)/shard_map/ppermute | solution.py:138
  91.5 9.5 %collective-permute-start.7 = (bf16[512,3584]{1,0:T(8,128)(2,1)S(1)}, bf16[512,3584]{1,0:T(8,128)(2,1)S(1)}, u32[]{:S(2)}, u32[]{:S(2)}) collective-permute-start(bf16[512,3584]{1,0:T(8,128)(2,1)S(1)} %collective-permute-done.6.weights.packed_y), channel_id=1, source_target_pairs={{0,1},{1,0},{2,3},{3,2},{4,5},{5,4},{6,7},{7,6},{8,9},{9,8},{10,11... | collective-permute-start | bytes 11010056 | tf_op jit(solution)/shard_map/ppermute | solution.py:138
  91.9 1.5 copy-start.1
  91.9 2.0 %copy-start.3 = (bf16[1,1,256,3584]{3,2,1,0:T(8,128)(2,1)S(1)}, bf16[1,1,256,3584]{3,2,1,0:T(8,128)(2,1)}, u32[]{:S(2)}) copy-start(bf16[1,1,256,3584]{3,2,1,0:T(8,128)(2,1)} %param.17) | copy-start | bytes 5505028
  97.9 27.7 %collective-permute-start.9 = (bf16[160,3584]{1,0:T(8,128)(2,1)S(1)}, bf16[160,3584]{1,0:T(8,128)(2,1)S(1)}, u32[]{:S(2)}, u32[]{:S(2)}) collective-permute-start(bf16[160,3584]{1,0:T(8,128)(2,1)S(1)} %pad_maximum_fusion.rows_x), channel_id=1, source_target_pairs={{0,2},{1,3},{2,0},{3,1},{4,6},{5,7},{6,4},{7,5},{8,10},{9,11},{10,... | collective-permute-start | bytes 3440648 | tf_op jit(solution)/shard_map/ppermute | solution.py:138
  101.0 5.9 %collective-permute-start.10 = (bf16[160,3584]{1,0:T(8,128)(2,1)S(1)}, bf16[160,3584]{1,0:T(8,128)(2,1)S(1)}, u32[]{:S(2)}, u32[]{:S(2)}) collective-permute-start(bf16[160,3584]{1,0:T(8,128)(2,1)S(1)} %pad_maximum_fusion.1.rows_g), channel_id=1, source_target_pairs={{0,1},{1,0},{2,3},{3,2},{4,5},{5,4},{6,7},{7,6},{8,9},{9,8},{10,11... | collective-permute-start | bytes 3440648 | tf_op jit(solution)/shard_map/ppermute | solution.py:138
  101.3 5.6 %collective-permute-start.8 = (bf16[160,3584]{1,0:T(8,128)(2,1)S(1)}, bf16[160,3584]{1,0:T(8,128)(2,1)S(1)}, u32[]{:S(2)}, u32[]{:S(2)}) collective-permute-start(bf16[160,3584]{1,0:T(8,128)(2,1)S(1)} %pad_maximum_fusion.rows_x), channel_id=1, source_target_pairs={{0,1},{1,0},{2,3},{3,2},{4,5},{5,4},{6,7},{7,6},{8,9},{9,8},{10,11... | collective-permute-start | bytes 3440648 | tf_op jit(solution)/shard_map/ppermute | solution.py:138
  108.4 19.2 %collective-permute-start.18 = (bf16[80,3584]{1,0:T(8,128)(2,1)S(1)}, bf16[80,3584]{1,0:T(8,128)(2,1)S(1)}, u32[]{:S(2)}, u32[]{:S(2)}) collective-permute-start(bf16[80,3584]{1,0:T(8,128)(2,1)S(1)} %pad_maximum_fusion.8), channel_id=1, source_target_pairs={{0,20},{1,21},{2,22},{3,23},{4,24},{5,25},{6,26},{7,27},{8,28},{9,... | collective-permute-start | bytes 1720328 | tf_op jit(solution)/shard_map/ppermute | solution.py:138
  111.0 40.1 %collective-permute-start.17 = (bf16[80,3584]{1,0:T(8,128)(2,1)S(1)}, bf16[80,3584]{1,0:T(8,128)(2,1)S(1)}, u32[]{:S(2)}, u32[]{:S(2)}) collective-permute-start(bf16[80,3584]{1,0:T(8,128)(2,1)S(1)} %pad_maximum_fusion.7), channel_id=1, source_target_pairs={{0,24},{1,25},{2,26},{3,27},{4,28},{5,29},{6,30},{7,31},{8,16},{9,... | collective-permute-start | bytes 1720328 | tf_op jit(solution)/shard_map/ppermute | solution.py:138
  113.7 37.5 %collective-permute-start.16 = (bf16[80,3584]{1,0:T(8,128)(2,1)S(1)}, bf16[80,3584]{1,0:T(8,128)(2,1)S(1)}, u32[]{:S(2)}, u32[]{:S(2)}) collective-permute-start(bf16[80,3584]{1,0:T(8,128)(2,1)S(1)} %pad_maximum_fusion.6), channel_id=1, source_target_pairs={{0,28},{1,29},{2,30},{3,31},{4,16},{5,17},{6,18},{7,19},{8,20},{9,... | collective-permute-start | bytes 1720328 | tf_op jit(solution)/shard_map/ppermute | solution.py:138
  116.2 47.0 %collective-permute-start.15 = (bf16[80,3584]{1,0:T(8,128)(2,1)S(1)}, bf16[80,3584]{1,0:T(8,128)(2,1)S(1)}, u32[]{:S(2)}, u32[]{:S(2)}) collective-permute-start(bf16[80,3584]{1,0:T(8,128)(2,1)S(1)} %pad_maximum_fusion.5), channel_id=1, source_target_pairs={{0,16},{1,17},{2,18},{3,19},{4,20},{5,21},{6,22},{7,23},{8,24},{9,... | collective-permute-start | bytes 1720328 | tf_op jit(solution)/shard_map/ppermute | solution.py:138
  125.6 33.9 %collective-permute-start.11 = (bf16[160,4608]{1,0:T(8,128)(2,1)S(1)}, bf16[160,4608]{1,0:T(8,128)(2,1)S(1)}, u32[]{:S(2)}, u32[]{:S(2)}) collective-permute-start(bf16[160,4608]{1,0:T(8,128)(2,1)S(1)} %get-tuple-element.64), channel_id=1, source_target_pairs={{0,2},{1,3},{2,0},{3,1},{4,6},{5,7},{6,4},{7,5},{8,10},{9,11},{10,... | collective-permute-start | bytes 4423688 | tf_op jit(solution)/shard_map/ppermute | solution.py:138
  159.5 3.9 %collective-permute-start.12 = (bf16[160,3584]{1,0:T(8,128)(2,1)S(1)}, bf16[160,3584]{1,0:T(8,128)(2,1)S(1)}, u32[]{:S(2)}, u32[]{:S(2)}) collective-permute-start(bf16[160,3584]{1,0:T(8,128)(2,1)S(1)} %collective-permute-done.9), channel_id=1, source_target_pairs={{0,1},{1,0},{2,3},{3,2},{4,5},{5,4},{6,7},{7,6},{8,9},{9,8},{10,11... | collective-permute-start | bytes 3440648 | tf_op jit(solution)/shard_map/ppermute | solution.py:138
  159.5 4.9 %collective-permute-start.14 = (bf16[160,4608]{1,0:T(8,128)(2,1)S(1)}, bf16[160,4608]{1,0:T(8,128)(2,1)S(1)}, u32[]{:S(2)}, u32[]{:S(2)}) collective-permute-start(bf16[160,4608]{1,0:T(8,128)(2,1)S(1)} %collective-permute-done.11), channel_id=1, source_target_pairs={{0,1},{1,0},{2,3},{3,2},{4,5},{5,4},{6,7},{7,6},{8,9},{9,8},{10,11... | collective-permute-start | bytes 4423688 | tf_op jit(solution)/shard_map/ppermute | solution.py:138
  163.3 1.5 collective-permute-start.13

commit v3 on v1

v3 whole, which is shorter than its diff:
```python
import jax
import jax.numpy as jnp
from jax import lax
from jax.experimental import pallas as pl
from jax.experimental.pallas import tpu as pltpu
from jax.sharding import PartitionSpec as P

GROUP = 4
LANES = 128
F32 = jnp.float32
BF16 = jnp.bfloat16
VMEM = pl.BlockSpec(memory_space=pltpu.VMEM)
SMEM = pl.BlockSpec(memory_space=pltpu.SMEM)
HBM = pl.BlockSpec(memory_space=pltpu.HBM)


def after(values, *before):
    return list(lax.optimization_barrier((tuple(values), before))[0])


def dot(left, right, contract):
    return lax.dot_general(left, right, ((contract[:1], contract[1:]), ((), ())), preferred_element_type=F32)


def shape(*dims, dtype=BF16):
    return jax.ShapeDtypeStruct(dims, dtype)


def cost(gflops, mib):
    return pl.CostEstimate(flops=int(gflops * 1e9), bytes_accessed=int(mib * 2**20), transcendentals=0)


def start_copies(pairs, sems):
    copies = [pltpu.make_async_copy(src, dst, sems.at[i]) for i, (src, dst) in enumerate(pairs)]
    for copy in copies:
        copy.start()
    return copies


def build_kernel(
    experts, cap, joined, mine_ref, fr_ref, fg_ref, br_ref, bg_ref, f_any, x_any, g_any, *refs
):
    outs, tables, (f_ref, x_ref, g_ref, sems) = refs[:experts], refs[experts:-4], refs[-4:]
    copies = start_copies(((f_any, f_ref), (x_any, x_ref), (g_any, g_ref)), sems)
    tok_rows = f_ref.shape[0]
    wide = tables[0].shape[1] // 2
    mine = mine_ref[0]
    row = lax.broadcasted_iota(jnp.int32, (tok_rows, tok_rows), 0)
    col = lax.broadcasted_iota(jnp.int32, (tok_rows, tok_rows), 1)
    earlier = (row < col).astype(F32).astype(BF16)
    same = (row == col).astype(F32).astype(BF16)
    slot = lax.broadcasted_iota(jnp.int32, (cap, tok_rows), 0).astype(F32)
    at = [lax.rem(mine + k, experts) for k in range(experts)]

    def placed(routes, gates):
        named = [((routes[0:1] == e) | (routes[1:2] == e)).astype(F32) for e in at]
        gate = [jnp.where(routes[0:1] == e, gates[0:1], gates[1:2]) for e in at]
        rows = -(-experts // 16) * 16
        padded = jnp.concatenate(named + [jnp.zeros((rows - experts, tok_rows), F32)], axis=0)
        prefix = dot(padded.astype(BF16), earlier, (1, 0))
        hits = [jnp.where(prefix[k:k + 1] == slot, named[k], 0.0) for k in range(experts)]
        return hits, [hits[k] * gate[k] for k in range(experts)]

    def by_token(slots):
        filled = sum(part.shape[0] for part in slots)
        full = jnp.concatenate(slots + [jnp.zeros((wide - filled, tok_rows), F32)], axis=0)
        return dot(same, full.astype(BF16), (1, 1)).astype(BF16)

    hits_f, gated_f = placed(fr_ref[...], fg_ref[...])
    hits_b, gated_b = placed(br_ref[...], bg_ref[...])
    rest_f = [part - part.astype(BF16).astype(F32) for part in gated_f]
    empty = jnp.zeros((cap, tok_rows), F32)
    for copy in copies:
        copy.wait()
    for k in range(experts):
        hits = hits_b[k].astype(BF16)
        rows_f = dot(hits_f[k].astype(BF16), f_ref[...], (1, 0))
        rows_x = dot(hits, x_ref[...], (1, 0))
        rows_g = dot(hits, g_ref[...], (1, 0)) * jnp.sum(gated_b[k], axis=1, keepdims=True)
        outs[k][...] = jnp.concatenate([rows_f, rows_x, rows_g], axis=0).astype(BF16)

    if joined:
        slots_f = [[part for k in range(experts) for part in (parts[k], empty)] for parts in (gated_f, rest_f)]
        slots_b = [part for k in range(experts) for part in (empty, hits_b[k])]
        tops = ((tables[0], 0, slots_f), (tables[0], tok_rows, [slots_b, None]))
    else:
        tops = ((tables[0], 0, [gated_f, rest_f]), (tables[1], 0, [hits_b, None]))
    for table, low, slots in tops:
        for i, part in enumerate(slots):
            value = jnp.zeros((tok_rows, wide), BF16) if part is None else by_token(part)
            table[low:low + tok_rows, i * wide:(i + 1) * wide] = value


def silu_slope(pre):
    sigma = 1.0 / (1.0 + jnp.exp(-pre))
    return pre * sigma, sigma * (1.0 + pre * (1.0 - sigma))


def hidden_units(rows_f, rows_x, rows_g, weights):
    count = rows_f.shape[0]
    up, down = weights
    pre = dot(jnp.concatenate([rows_f[...], rows_x[...]], axis=0), up[...], (1, 0))
    act, slope = silu_slope(pre)
    dact = dot(rows_g[...], down[...], (1, 1))
    return act[:count].astype(BF16), (dact * slope[count:]).astype(BF16)


def own_kernel(rows_f, rows_x, rows_g, up, down, up_c, down_c, act_f, dpre):
    side = down.shape[0]
    for q, weights in enumerate(((up, down), (up_c, down_c))):
        cols = slice(q * side, (q + 1) * side)
        act_f[:, cols], dpre[:, cols] = hidden_units(rows_f, rows_x, rows_g, weights)


def near_kernel(rows_f, rows_x, rows_g, act_f, dpre, up, down, up_c, down_c, up_y, down_y, part_f, part_b):
    side = down.shape[0]
    last_act, last_dpre = hidden_units(rows_f, rows_x, rows_g, (up_y, down_y))
    acts = [act_f[:, :side], act_f[:, side:], last_act]
    dpres = [dpre[:, :side], dpre[:, side:], last_dpre]
    for j in range(0, part_f.shape[1], side):
        cols = slice(j, j + side)
        part_f[:, cols] = sum(dot(a, w[:, cols], (1, 0)) for a, w in zip(acts, (down, down_c, down_y)))
        part_b[:, cols] = sum(dot(d, w[cols, :], (1, 1)) for d, w in zip(dpres, (up, up_c, up_y)))


def far_kernel(cap, joined, rows_f, rows_x, rows_g, part_f, part_b, up, down, *outs):
    side = down.shape[0]
    act_f, dpre = hidden_units(rows_f, rows_x, rows_g, (up, down))
    experts = rows_f.shape[0] // cap
    for j in range(0, part_f.shape[1], side):
        cols = slice(j, j + side)
        out_f = part_f[:, cols] + dot(act_f, down[:, cols], (1, 0))
        out_b = part_b[:, cols] + dot(dpre, up[cols, :], (1, 1))
        for k in range(experts):
            rows = slice(k * cap, (k + 1) * cap)
            if joined:
                outs[k][:, cols] = jnp.concatenate([out_f[rows], out_b[rows]], axis=0).astype(BF16)
            else:
                outs[k][:, cols] = out_f[rows].astype(BF16)
                outs[experts + k][:, cols] = out_b[rows].astype(BF16)


def grads_kernel(xg_own, xg_c, xg_y, xg_d, own_up, own_down, grad_up, grad_down, up, down, sems):
    count = xg_own.shape[0] // 2
    side, width = down.shape
    all_x = [piece.at[:count] for piece in (xg_own, xg_c, xg_y, xg_d)]
    all_g = [piece.at[count:] for piece in (xg_own, xg_c, xg_y, xg_d)]
    acts, dpres = [], []
    for rows_x, rows_g in zip(all_x, all_g):
        act, slope = silu_slope(dot(rows_x[...], own_up[...], (1, 0)))
        acts.append(act.astype(BF16))
        dact = dot(rows_g[...], own_down[...], (1, 1))
        dpres.append((dact * slope).astype(BF16))
    act, dpre = jnp.concatenate(acts, axis=0), jnp.concatenate(dpres, axis=0)
    tile = 2 * side
    copies = []
    for t, low in enumerate(range(0, width, tile)):
        cols = slice(low, low + tile)
        up[cols, :] = dot(jnp.concatenate([rows[:, cols] for rows in all_x], axis=0), dpre, (0, 0))
        down[:, cols] = dot(act, jnp.concatenate([rows[:, cols] for rows in all_g], axis=0), (0, 0))
        span = pl.ds(low, tile)
        copies.append(pltpu.make_async_copy(up.at[span], grad_up.at[span], sems.at[0, t]))
        copies.append(pltpu.make_async_copy(down.at[:, span], grad_down.at[:, span], sems.at[1, t]))
        copies[-2].start()
        copies[-1].start()
    for copy in copies:
        copy.wait()


def combine_kernel(experts, count, tables, *refs):
    base, refs = refs[:count], refs[count:]
    whole, late, outs = refs[:experts], refs[experts:2 * experts - 1], refs[2 * experts - 1:]
    tokens, width = tables.shape[0], whole[0].shape[1]
    wide = tables.shape[1] // 2
    each = whole[0].shape[0]
    table = jnp.concatenate([tables[:, :wide], tables[:, wide:]], axis=0)
    pieces = [(0, whole[0])]
    for k in range(1, experts):
        pieces += [(k * each, whole[k]), (k * each + whole[k].shape[0], late[k - 1])]
    tile = width // 7
    for low in range(0, width, tile):
        cols = slice(low, low + tile)
        picked = sum(dot(table[:, at:at + part.shape[0]], part[:, cols], (1, 0)) for at, part in pieces)
        picked = picked[:tokens] + picked[tokens:]
        rows = tokens // count
        for i, out in enumerate(outs):
            out[:, cols] = (base[i][:, cols].astype(F32) + picked[i * rows:(i + 1) * rows]).astype(BF16)


def local(
    fwd_acts, fwd_routes, fwd_gates, back_acts, back_routes, back_gates, back_grads, w_up, w_down
):
    devices = lax.axis_size("expert")
    sections = lax.axis_size("pipe")
    experts = devices // GROUP
    tok_rows, width = fwd_acts.shape[1:]
    cap = GROUP * (5 * tok_rows * fwd_routes.shape[2] // (4 * devices))
    mine = lax.axis_index("expert") // GROUP
    hidden = w_up.shape[3]
    count = experts * cap
    joined = sections == 2
    each = 2 * cap if joined else cap
    wide = -(-experts * each // LANES) * LANES

    def send(value, planes=0, flip=0, pipes=0):
        pairs = []
        for section in range(sections):
            for place in range(devices):
                target = (place // GROUP + planes) % experts * GROUP + (place % GROUP ^ flip)
                goal = (section + pipes) % sections * devices + target
                pairs.append((section * devices + place, goal))
        return lax.ppermute(value, ("pipe", "expert"), pairs)

    def call(kernel, name, out_shape, inputs, estimate, limit=8, **more):
        return pl.pallas_call(
            kernel,
            out_shape=out_shape,
            in_specs=more.pop("in_specs", [VMEM] * len(inputs)),
            out_specs=more.pop("out_specs", [VMEM] * len(out_shape)),
            name=name,
            compiler_params=pltpu.CompilerParams(vmem_limit_bytes=limit * 2**20),
            cost_estimate=estimate,
            **more,
        )(*inputs)

    fwd_input, back_input, out_grad = fwd_acts[0], back_acts[0], back_grads[0]
    away = range(1, experts)

    up_own, down_own = w_up[0, 0], w_down[0, 0]
    up_c, down_c = send(up_own, flip=1), send(down_own, flip=1)
    up_y, down_y = send(up_own, flip=2), send(down_own, flip=2)
    res_f = send(fwd_input, pipes=1)
    tables = [shape(2 * tok_rows, 2 * wide)] if joined else [shape(tok_rows, 2 * wide)] * 2
    built = call(
        lambda *refs: build_kernel(experts, cap, joined, *refs),
        "build",
        [shape(3 * cap, width)] * experts + tables,
        (
            mine.reshape(1), fwd_routes[0].T, fwd_gates[0].T, back_routes[0].T, back_gates[0].T,
            fwd_input, back_input, out_grad,
        ),
        cost(100, 0.1),
        limit=56,
        in_specs=[SMEM] + [VMEM] * 4 + [HBM] * 3,
        scratch_shapes=[pltpu.VMEM((tok_rows, width), BF16)] * 3 + [pltpu.SemaphoreType.DMA((3,))],
    )
    rows_out, tables = built[:experts], built[experts:]
    got = [rows_out[0]] + after(rows_out[1:], up_c, down_c)
    got[-1:] = after(got[-1:], res_f)
    got[1:] = [send(part, planes=k) for k, part in enumerate(got[1:], 1)]
    up_d, down_d = send(up_y, flip=1), send(down_y, flip=1)
    out_grad, *tables = after([out_grad, *tables], up_d)
    res_b = send(out_grad, pipes=-1)
    tables = [send(table, pipes=1 - 2 * i) for i, table in enumerate(tables)]

    rows_f, rows_x, rows_g = (
        jnp.concatenate([part[i * cap:(i + 1) * cap] for part in got], axis=0) for i in range(3)
    )
    rows_xg = jnp.concatenate([rows_x, rows_g], axis=0)
    rows = rows_f, rows_x, rows_g = rows_f, rows_x, rows_g
    act_f, dpre = call(
        own_kernel, "own", [shape(count, 2 * hidden)] * 2, (*rows, up_own, down_own, up_c, down_c), cost(2, 12)
    )
    part_f, part_b = call(
        near_kernel,
        "near",
        [shape(count, width, dtype=F32)] * 2,
        (*rows, act_f, dpre, up_own, down_own, up_c, down_c, up_y, down_y),
        cost(3, 18),
    )
    outs = call(
        lambda *refs: far_kernel(cap, joined, *refs),
        "far",
        [shape(each, width)] * experts if joined else [shape(cap, width)] * (2 * experts),
        (*after(rows, res_b, *tables), part_f, part_b, up_d, down_d),
        cost(2, 10),
    )

    split = 4 * each // 5 // 16 * 16
    ways = range(2 * experts if not joined else experts)
    early = [outs[i] if i % experts == 0 else outs[i][:split] for i in ways]
    late = [None if i % experts == 0 else outs[i][split:] for i in ways]

    def back(value, i):
        return send(value, planes=-(i % experts), pipes=1 if i < experts else -1)

    ret = [back(early[i], i) for i in ways]
    ret_late = after([part for part in late if part is not None], *ret)
    ret_late = [back(part, i) for part, i in zip(ret_late, [i for i in ways if i % experts])]

    xg_y = send(*after([rows_xg], up_y, down_y), flip=2)
    xg_c = send(*after([rows_xg], up_d, down_d), flip=1)
    xg_d = send(*after([xg_y], *ret), flip=1)
    tiles = width // (2 * hidden)
    grad_up, grad_down = call(
        grads_kernel,
        "grads",
        [shape(width, hidden, dtype=F32), shape(hidden, width, dtype=F32)],
        (rows_xg, xg_c, xg_y, xg_d, up_own, down_own),
        cost(0.01, 0.1),
        limit=16,
        out_specs=[HBM] * 2,
        scratch_shapes=[
            pltpu.VMEM((width, hidden), F32), pltpu.VMEM((hidden, width), F32), pltpu.SemaphoreType.DMA((2, tiles)),
        ],
    )

    tables = after(tables, grad_up, grad_down)
    results = []
    bases = [(res_f, res_b)] if joined else [(res_f,), (res_b,)]
    for i, (base, table) in enumerate(zip(bases, tables)):
        parts = (*ret[i * experts:(i + 1) * experts], *ret_late[i * (experts - 1):(i + 1) * (experts - 1)])
        results += call(
            lambda *refs: combine_kernel(experts, len(base), *refs),
            "combine", [shape(tok_rows, width)] * (2 if joined else 1), (table, *base, *parts), cost(0.2, 4),
        )
    fwd_next, back_next = results
    return (fwd_next[None], back_next[None], grad_up[None, None], grad_down[None, None])


def solution(mesh):
    rows = P("pipe", "expert", None)
    slices = P("pipe", "expert", None, None)
    return jax.shard_map(
        local,
        mesh=mesh,
        in_specs=(rows,) * 7 + (slices,) * 2,
        out_specs=(rows, rows, slices, slices),
        check_vma=False,
    )
```

time: 252 us -> 173 us (0.69)
  matrix products: 52.8 us -> 0 us
  Pallas kernels: 0 us -> 29.5 us
  starting transfers between devices: 57 us -> 30.2 us
  local copies, waits for them, and re-layouts: 17.5 us -> 3.38 us
  waiting for transfers between devices: 118 us -> 109 us
  other arithmetic: 4.84 us -> 0.34 us
    dot_general x22 -> x0, matrix products: 52.8 us -> none  [dot(): lax.dot_general(left, right, ((contract[:1], contract[1:]), ((), ())), pr...]
    pallas_call x0 -> x6, Pallas kernels: none -> 29.5 us  [call(): pl.pallas_call(kernel, out_shape=out_shape, in_specs=more.pop('in_specs',...]
    ppermute x37 -> x22, starting transfers between devices: 57 us -> 30.2 us  [send(): return lax.ppermute(value, ('pipe', 'expert'), pairs)]
    unnamed x59 -> x11, local copies, waits for them, and re-layouts: 12.8 us -> 1.77 us
    ppermute x37 -> x22, waiting for transfers between devices: 118 us -> 109 us  [send(): return lax.ppermute(value, ('pipe', 'expert'), pairs)]
  transfers between devices with their start and end apart: 37 -> 22, of which waited for: 10 -> 8; matrix products, arithmetic and copies ran while one was open for 28% -> 2% of each run, Pallas kernels for 0% -> 15%
where the time goes in v3:
time: 173 us
  waiting for transfers between devices  109 us (63%)
  starting transfers between devices  30.2 us (17%)
  Pallas kernels  29.5 us (17%)
  local copies, waits for them, and re-layouts  3.38 us (2%)
    ppermute x22, waiting for transfers between devices, send(): return lax.ppermute(value, ('pipe', 'expert'), pairs)  109 us
    ppermute x22, starting transfers between devices, send(): return lax.ppermute(value, ('pipe', 'expert'), pairs)  30.2 us
    pallas_call x6, Pallas kernels, call(): pl.pallas_call(kernel, out_shape=out_shape, in_specs=more.pop('in_specs',...  29.5 us
  transfers between devices with their start and end apart: 22, of which 8 were waited for; matrix products, arithmetic and copies ran while one was open for 2% of the time, Pallas kernels for 15%

profile of v3, /device:TPU:0, one launch (start us, length us, event | category | flops | bytes accessed | tf_op | source)
XLA Modules:
  0.0 172.8 jit_solution(7236015595830134949)
XLA Ops:
  0.6 0.5 collective-permute-start.3
  1.2 2.6 %collective-permute-start = (bf16[3584,256]{1,0:T(8,128)(2,1)}, bf16[3584,256]{1,0:T(8,128)(2,1)}, u32[]{:S(2)}, u32[]{:S(2)}) collective-permute-start(bf16[3584,256]{1,0:T(8,128)(2,1)} %bitcast.23), channel_id=1, source_target_pairs={{0,2},{1,3},{2,0},{3,1},{4,6},{5,7},{6,4},{7,5},{8,10},{9,11},{10,... | collective-permute-start | bytes 5505032 | tf_op jit(solution)/shard_map/ppermute | solution.py:212
  3.7 0.2 collective-permute-start.4
  3.9 0.3 collective-permute-start.9
  4.2 1.7 %collective-permute-start.7 = (bf16[64,3584]{1,0:T(8,128)(2,1)}, bf16[64,3584]{1,0:T(8,128)(2,1)S(1)}, u32[]{:S(2)}, u32[]{:S(2)}) collective-permute-start(bf16[64,3584]{1,0:T(8,128)(2,1)} %bitcast.35), channel_id=1, source_target_pairs={{0,16},{1,17},{2,18},{3,19},{4,20},{5,21},{6,22},{7,23},{8,24},{9,... | collective-permute-start | bytes 1376264 | tf_op jit(solution)/shard_map/ppermute | solution.py:212
  5.9 4.3 %build.1 = (bf16[120,3584]{1,0:T(8,128)(2,1)}, bf16[120,3584]{1,0:T(8,128)(2,1)}, bf16[120,3584]{1,0:T(8,128)(2,1)}, bf16[120,3584]{1,0:T(8,128)(2,1)}, bf16[128,768]{1,0:T(8,128)(2,1)}) custom-call(s32[1]{0:T(128)} %bitcast.1.refs_0_, s32[2,64]{1,0:T(2,128)} %bitcast.41, f32[2,64]{1,0:T(2,128)} %bitcast.42, s32[2,64]{1,0:T(2,128)} %bitcast.43, ...), custom_call_target="tpu_custom_call" | custom-call | flops 99999997952 | bytes 104857 | tf_op jit(solution)/shard_map/build/pallas_call | solution.py:215
  10.2 0.0 collective-permute-done.3.up_c
  10.2 0.0 collective-permute-done.4.down_c
  10.2 1.6 collective-permute-start.5
  11.8 1.2 fusion
  13.1 2.7 %collective-permute-start.6 = (bf16[120,3584]{1,0:T(8,128)(2,1)}, bf16[120,3584]{1,0:T(8,128)(2,1)S(1)}, u32[]{:S(2)}, u32[]{:S(2)}) collective-permute-start(bf16[120,3584]{1,0:T(8,128)(2,1)} %get-tuple-element.44), channel_id=1, source_target_pairs={{0,8},{1,9},{2,10},{3,11},{4,12},{5,13},{6,14},{7,15},{8,0},{9,1},... | collective-permute-start | bytes 2580488 | tf_op jit(solution)/shard_map/ppermute | solution.py:212
  15.7 1.2 collective-permute-done.7.refs_1_
  16.9 3.8 %collective-permute-start.8 = (bf16[120,3584]{1,0:T(8,128)(2,1)}, bf16[120,3584]{1,0:T(8,128)(2,1)S(1)}, u32[]{:S(2)}, u32[]{:S(2)}) collective-permute-start(bf16[120,3584]{1,0:T(8,128)(2,1)} %get-tuple-element.46), channel_id=1, source_target_pairs={{0,12},{1,13},{2,14},{3,15},{4,0},{5,1},{6,2},{7,3},{8,4},{9,5},{1... | collective-permute-start | bytes 2580488 | tf_op jit(solution)/shard_map/ppermute | solution.py:212
  20.7 24.2 %collective-permute-done.up_y = bf16[3584,256]{1,0:T(8,128)(2,1)} collective-permute-done((bf16[3584,256]{1,0:T(8,128)(2,1)}, bf16[3584,256]{1,0:T(8,128)(2,1)}, u32[]{:S(2)}, u32[]{:S(2)}) %collective-permute-start) | collective-permute-done | bytes 1835040 | tf_op jit(solution)/shard_map/ppermute | solution.py:212
  44.9 0.0 collective-permute-start.1
  44.9 39.1 %collective-permute-done.9.down_y = bf16[256,3584]{1,0:T(8,128)(2,1)} collective-permute-done((bf16[256,3584]{1,0:T(8,128)(2,1)}, bf16[256,3584]{1,0:T(8,128)(2,1)}, u32[]{:S(2)}, u32[]{:S(2)}) %collective-permute-start.9) | collective-permute-done | bytes 1835040 | tf_op jit(solution)/shard_map/ppermute | solution.py:212
  84.0 0.0 collective-permute-start.10
  84.0 0.0 collective-permute-done.5
  84.0 0.1 fusion.1
  84.1 0.0 collective-permute-done.6
  84.1 0.1 fusion.2
  84.2 0.0 collective-permute-done.8
  84.2 0.1 fusion.3
  84.3 1.0 constant_dynamic-update-slice_fusion.3
  85.4 1.8 %collective-permute-start.12 = (bf16[320,3584]{1,0:T(8,128)(2,1)S(1)}, bf16[320,3584]{1,0:T(8,128)(2,1)S(1)}, u32[]{:S(2)}, u32[]{:S(2)}) collective-permute-start(bf16[320,3584]{1,0:T(8,128)(2,1)S(1)} %constant_dynamic-update-slice_fusion.xg_own), channel_id=1, source_target_pairs={{0,2},{1,3},{2,0},{3,1},{4,6},{5,7},{6,4},{7,5},{8,10},{9,11},{10,... | collective-permute-start | bytes 6881288 | tf_op jit(solution)/shard_map/ppermute | solution.py:212
  87.2 0.1 pad_maximum_fusion.2.rows_g.refs_2_
  87.3 0.0 copy-start.2
  87.3 0.0 copy-start
  87.3 0.0 copy-start.1
  87.3 0.2 pad_maximum_fusion
  87.6 0.0 collective-permute-done.1.refs_5_
  87.6 0.7 copy-done.2
  88.3 1.5 collective-permute-start.13
  89.8 0.0 copy-done
  89.8 0.0 copy-done.1
  89.8 3.9 %own.1 = (bf16[160,512]{1,0:T(8,128)(2,1)S(1)}, bf16[160,512]{1,0:T(8,128)(2,1)S(1)}) custom-call(bf16[160,3584]{1,0:T(8,128)(2,1)S(1)} %get-tuple-element.50.rows_f.refs_0_, bf16[160,3584]{1,0:T(8,128)(2,1)S(1)} %get-tuple-element.51.rows_x.refs_1_, bf16[160,3584]{1,0:T(8,128)(2,1)S(1)} %pad_maximum_fusion.2.rows_g.refs_2_, bf16[3584,256]{1,0:T(8,128)(2,1)S(1)} %bitcast.24, ...), custom_call_target="tpu_custom_call" | custom-call | flops 2000000000 | bytes 12582912 | tf_op jit(solution)/shard_map/own/pallas_call | solution.py:215
  93.8 0.0 copy-done.3
  93.8 1.3 collective-permute-start.2
  95.0 6.6 %near.1 = (f32[160,3584]{1,0:T(8,128)S(1)}, f32[160,3584]{1,0:T(8,128)S(1)}) custom-call(bf16[160,3584]{1,0:T(8,128)(2,1)S(1)} %get-tuple-element.50.rows_f.refs_0_, bf16[160,3584]{1,0:T(8,128)(2,1)S(1)} %get-tuple-element.51.rows_x.refs_1_, bf16[160,3584]{1,0:T(8,128)(2,1)S(1)} %pad_maximum_fusion.2.rows_g.refs_2_, ...), custom_call_target="tpu_custom_call" | custom-call | flops 3000000000 | bytes 18874368 | tf_op jit(solution)/shard_map/near/pallas_call | solution.py:215
  101.6 3.6 %collective-permute-done.2.refs_0_ = bf16[128,768]{1,0:T(8,128)(2,1)S(1)} collective-permute-done((bf16[128,768]{1,0:T(8,128)(2,1)S(1)}, bf16[128,768]{1,0:T(8,128)(2,1)S(1)}, u32[]{:S(2)}, u32[]{:S(2)}) %collective-permute-start.2) | collective-permute-done | bytes 196640 | tf_op jit(solution)/shard_map/ppermute | solution.py:212
  105.2 0.0 collective-permute-done.13.refs_2_
  105.2 0.0 collective-permute-done.10.refs_6_
  105.2 2.4 %far.1 = (bf16[80,3584]{1,0:T(8,128)(2,1)S(1)}, bf16[80,3584]{1,0:T(8,128)(2,1)S(1)}, bf16[80,3584]{1,0:T(8,128)(2,1)S(1)}, bf16[80,3584]{1,0:T(8,128)(2,1)S(1)}) custom-call(bf16[160,3584]{1,0:T(8,128)(2,1)S(1)} %get-tuple-element.50.rows_f.refs_0_, bf16[160,3584]{1,0:T(8,128)(2,1)S(1)} %get-tuple-element.51.rows_x.refs_1_, ...), custom_call_target="tpu_custom_call" | custom-call | flops 2000000000 | bytes 10485760 | tf_op jit(solution)/shard_map/far/pallas_call | solution.py:215
  107.6 1.6 collective-permute-start.14
  109.2 4.1 %collective-permute-start.15 = (bf16[64,3584]{1,0:T(8,128)(2,1)S(1)}, bf16[64,3584]{1,0:T(8,128)(2,1)S(1)}, u32[]{:S(2)}, u32[]{:S(2)}) collective-permute-start(bf16[64,3584]{1,0:T(8,128)(2,1)S(1)} %slice.66), channel_id=1, source_target_pairs={{0,28},{1,29},{2,30},{3,31},{4,16},{5,17},{6,18},{7,19},{8,20},{9,... | collective-permute-start | bytes 1376264 | tf_op jit(solution)/shard_map/ppermute | solution.py:212
  113.4 1.5 collective-permute-start.16
  114.9 0.6 collective-permute-start.17
  115.5 8.9 %collective-permute-done.15.refs_4_ = bf16[64,3584]{1,0:T(8,128)(2,1)S(1)} collective-permute-done((bf16[64,3584]{1,0:T(8,128)(2,1)S(1)}, bf16[64,3584]{1,0:T(8,128)(2,1)S(1)}, u32[]{:S(2)}, u32[]{:S(2)}) %collective-permute-start.15) | collective-permute-done | bytes 458784 | tf_op jit(solution)/shard_map/ppermute | solution.py:212
  124.4 0.0 collective-permute-start.11
  124.4 28.9 %collective-permute-done.16.refs_5_ = bf16[64,3584]{1,0:T(8,128)(2,1)S(1)} collective-permute-done((bf16[64,3584]{1,0:T(8,128)(2,1)S(1)}, bf16[64,3584]{1,0:T(8,128)(2,1)S(1)}, u32[]{:S(2)}, u32[]{:S(2)}) %collective-permute-start.16) | collective-permute-done | bytes 458784 | tf_op jit(solution)/shard_map/ppermute | solution.py:212
  153.4 0.0 collective-permute-done.17.refs_6_
  153.4 0.0 collective-permute-done.14.refs_3_
  153.4 0.0 collective-permute-done.12.xg_y
  153.4 0.1 collective-permute-start.18
  153.5 1.3 collective-permute-start.19
  154.8 2.7 %collective-permute-start.20 = (bf16[16,3584]{1,0:T(8,128)(2,1)S(1)}, bf16[16,3584]{1,0:T(8,128)(2,1)S(1)}, u32[]{:S(2)}, u32[]{:S(2)}) collective-permute-start(bf16[16,3584]{1,0:T(8,128)(2,1)S(1)} %slice.70), channel_id=1, source_target_pairs={{0,24},{1,25},{2,26},{3,27},{4,28},{5,29},{6,30},{7,31},{8,16},{9,... | collective-permute-start | bytes 344072 | tf_op jit(solution)/shard_map/ppermute | solution.py:212
  157.5 0.3 collective-permute-start.21
  157.8 0.0 collective-permute-done.11.xg_c
  157.8 0.1 collective-permute-done.18.xg_d
  157.9 7.9 %grads.1 = (f32[3584,256]{1,0:T(8,128)}, f32[256,3584]{1,0:T(8,128)}) custom-call(bf16[320,3584]{1,0:T(8,128)(2,1)S(1)} %constant_dynamic-update-slice_fusion.xg_own, bf16[320,3584]{1,0:T(8,128)(2,1)S(1)} %collective-permute-done.11.xg_c, bf16[320,3584]{1,0:T(8,128)(2,1)S(1)} %collective-permute-done.12.xg_y, ...), custom_call_target="tpu_custom_call" | custom-call | flops 10000000 | bytes 104857 | tf_op jit(solution)/shard_map/grads/pallas_call | solution.py:215
  165.8 0.0 collective-permute-done.19.refs_7_
  165.8 2.6 %collective-permute-done.20.refs_8_ = bf16[16,3584]{1,0:T(8,128)(2,1)S(1)} collective-permute-done((bf16[16,3584]{1,0:T(8,128)(2,1)S(1)}, bf16[16,3584]{1,0:T(8,128)(2,1)S(1)}, u32[]{:S(2)}, u32[]{:S(2)}) %collective-permute-start.20) | collective-permute-done | bytes 114720 | tf_op jit(solution)/shard_map/ppermute | solution.py:212
  168.4 0.0 collective-permute-done.21.refs_9_
  168.4 4.4 %combine.1 = (bf16[64,3584]{1,0:T(8,128)(2,1)}, bf16[64,3584]{1,0:T(8,128)(2,1)}) custom-call(bf16[128,768]{1,0:T(8,128)(2,1)S(1)} %collective-permute-done.2.refs_0_, bf16[64,3584]{1,0:T(8,128)(2,1)S(1)} %collective-permute-done.7.refs_1_, bf16[64,3584]{1,0:T(8,128)(2,1)S(1)} %collective-permute-done.13.refs_2_, ...), custom_call_target="tpu_custom_call" | custom-call | flops 200000000 | bytes 4194304 | tf_op jit(solution)/shard_map/combine/pallas_call | solution.py:215
  (10 shorter events, 0.2 us)
Async XLA Ops:
  0.6 9.6 %collective-permute-start.3 = (bf16[3584,256]{1,0:T(8,128)(2,1)}, bf16[3584,256]{1,0:T(8,128)(2,1)S(1)}, u32[]{:S(2)}, u32[]{:S(2)}) collective-permute-start(bf16[3584,256]{1,0:T(8,128)(2,1)} %bitcast.22), channel_id=1, source_target_pairs={{0,1},{1,0},{2,3},{3,2},{4,5},{5,4},{6,7},{7,6},{8,9},{9,8},{10,11... | collective-permute-start | bytes 5505032 | tf_op jit(solution)/shard_map/ppermute | solution.py:212
  1.2 43.8 %collective-permute-start = (bf16[3584,256]{1,0:T(8,128)(2,1)}, bf16[3584,256]{1,0:T(8,128)(2,1)}, u32[]{:S(2)}, u32[]{:S(2)}) collective-permute-start(bf16[3584,256]{1,0:T(8,128)(2,1)} %bitcast.23), channel_id=1, source_target_pairs={{0,2},{1,3},{2,0},{3,1},{4,6},{5,7},{6,4},{7,5},{8,10},{9,11},{10,... | collective-permute-start | bytes 5505032 | tf_op jit(solution)/shard_map/ppermute | solution.py:212
  3.7 6.5 %collective-permute-start.4 = (bf16[256,3584]{1,0:T(8,128)(2,1)}, bf16[256,3584]{1,0:T(8,128)(2,1)}, u32[]{:S(2)}, u32[]{:S(2)}) collective-permute-start(bf16[256,3584]{1,0:T(8,128)(2,1)} %bitcast.27), channel_id=1, source_target_pairs={{0,1},{1,0},{2,3},{3,2},{4,5},{5,4},{6,7},{7,6},{8,9},{9,8},{10,11... | collective-permute-start | bytes 5505032 | tf_op jit(solution)/shard_map/ppermute | solution.py:212
  3.9 80.1 %collective-permute-start.9 = (bf16[256,3584]{1,0:T(8,128)(2,1)}, bf16[256,3584]{1,0:T(8,128)(2,1)}, u32[]{:S(2)}, u32[]{:S(2)}) collective-permute-start(bf16[256,3584]{1,0:T(8,128)(2,1)} %bitcast.28), channel_id=1, source_target_pairs={{0,2},{1,3},{2,0},{3,1},{4,6},{5,7},{6,4},{7,5},{8,10},{9,11},{10,... | collective-permute-start | bytes 5505032 | tf_op jit(solution)/shard_map/ppermute | solution.py:212
  4.2 12.7 %collective-permute-start.7 = (bf16[64,3584]{1,0:T(8,128)(2,1)}, bf16[64,3584]{1,0:T(8,128)(2,1)S(1)}, u32[]{:S(2)}, u32[]{:S(2)}) collective-permute-start(bf16[64,3584]{1,0:T(8,128)(2,1)} %bitcast.35), channel_id=1, source_target_pairs={{0,16},{1,17},{2,18},{3,19},{4,20},{5,21},{6,22},{7,23},{8,24},{9,... | collective-permute-start | bytes 1376264 | tf_op jit(solution)/shard_map/ppermute | solution.py:212
  10.2 73.8 %collective-permute-start.5 = (bf16[120,3584]{1,0:T(8,128)(2,1)}, bf16[120,3584]{1,0:T(8,128)(2,1)S(1)}, u32[]{:S(2)}, u32[]{:S(2)}) collective-permute-start(bf16[120,3584]{1,0:T(8,128)(2,1)} %get-tuple-element.43), channel_id=1, source_target_pairs={{0,4},{1,5},{2,6},{3,7},{4,8},{5,9},{6,10},{7,11},{8,12},{9,13},{1... | collective-permute-start | bytes 2580488 | tf_op jit(solution)/shard_map/ppermute | solution.py:212
  13.1 71.0 %collective-permute-start.6 = (bf16[120,3584]{1,0:T(8,128)(2,1)}, bf16[120,3584]{1,0:T(8,128)(2,1)S(1)}, u32[]{:S(2)}, u32[]{:S(2)}) collective-permute-start(bf16[120,3584]{1,0:T(8,128)(2,1)} %get-tuple-element.44), channel_id=1, source_target_pairs={{0,8},{1,9},{2,10},{3,11},{4,12},{5,13},{6,14},{7,15},{8,0},{9,1},... | collective-permute-start | bytes 2580488 | tf_op jit(solution)/shard_map/ppermute | solution.py:212
  16.9 67.3 %collective-permute-start.8 = (bf16[120,3584]{1,0:T(8,128)(2,1)}, bf16[120,3584]{1,0:T(8,128)(2,1)S(1)}, u32[]{:S(2)}, u32[]{:S(2)}) collective-permute-start(bf16[120,3584]{1,0:T(8,128)(2,1)} %get-tuple-element.46), channel_id=1, source_target_pairs={{0,12},{1,13},{2,14},{3,15},{4,0},{5,1},{6,2},{7,3},{8,4},{9,5},{1... | collective-permute-start | bytes 2580488 | tf_op jit(solution)/shard_map/ppermute | solution.py:212
  44.9 42.7 %collective-permute-start.1 = (bf16[3584,256]{1,0:T(8,128)(2,1)}, bf16[3584,256]{1,0:T(8,128)(2,1)S(1)}, u32[]{:S(2)}, u32[]{:S(2)}) collective-permute-start(bf16[3584,256]{1,0:T(8,128)(2,1)} %collective-permute-done.up_y), channel_id=1, source_target_pairs={{0,1},{1,0},{2,3},{3,2},{4,5},{5,4},{6,7},{7,6},{8,9},{9,8},{10,11... | collective-permute-start | bytes 5505032 | tf_op jit(solution)/shard_map/ppermute | solution.py:212
  84.0 21.2 %collective-permute-start.10 = (bf16[256,3584]{1,0:T(8,128)(2,1)}, bf16[256,3584]{1,0:T(8,128)(2,1)S(1)}, u32[]{:S(2)}, u32[]{:S(2)}) collective-permute-start(bf16[256,3584]{1,0:T(8,128)(2,1)} %collective-permute-done.9.down_y), channel_id=1, source_target_pairs={{0,1},{1,0},{2,3},{3,2},{4,5},{5,4},{6,7},{7,6},{8,9},{9,8},{10,11... | collective-permute-start | bytes 5505032 | tf_op jit(solution)/shard_map/ppermute | solution.py:212
  85.4 68.0 %collective-permute-start.12 = (bf16[320,3584]{1,0:T(8,128)(2,1)S(1)}, bf16[320,3584]{1,0:T(8,128)(2,1)S(1)}, u32[]{:S(2)}, u32[]{:S(2)}) collective-permute-start(bf16[320,3584]{1,0:T(8,128)(2,1)S(1)} %constant_dynamic-update-slice_fusion.xg_own), channel_id=1, source_target_pairs={{0,2},{1,3},{2,0},{3,1},{4,6},{5,7},{6,4},{7,5},{8,10},{9,11},{10,... | collective-permute-start | bytes 6881288 | tf_op jit(solution)/shard_map/ppermute | solution.py:212
  87.3 1.0 copy-start.2
  87.3 2.5 %copy-start = (bf16[1,1,3584,256]{3,2,1,0:T(8,128)(2,1)S(1)}, bf16[1,1,3584,256]{3,2,1,0:T(8,128)(2,1)}, u32[]{:S(2)}) copy-start(bf16[1,1,3584,256]{3,2,1,0:T(8,128)(2,1)} %param.16) | copy-start | bytes 5505028
  87.3 2.5 %copy-start.1 = (bf16[1,1,256,3584]{3,2,1,0:T(8,128)(2,1)S(1)}, bf16[1,1,256,3584]{3,2,1,0:T(8,128)(2,1)}, u32[]{:S(2)}) copy-start(bf16[1,1,256,3584]{3,2,1,0:T(8,128)(2,1)} %param.17) | copy-start | bytes 5505028
  88.3 16.9 %collective-permute-start.13 = (bf16[64,3584]{1,0:T(8,128)(2,1)S(1)}, bf16[64,3584]{1,0:T(8,128)(2,1)S(1)}, u32[]{:S(2)}, u32[]{:S(2)}) collective-permute-start(bf16[64,3584]{1,0:T(8,128)(2,1)S(1)} %bitcast.38), channel_id=1, source_target_pairs={{0,16},{1,17},{2,18},{3,19},{4,20},{5,21},{6,22},{7,23},{8,24},{9,... | collective-permute-start | bytes 1376264 | tf_op jit(solution)/shard_map/ppermute | solution.py:212
  89.8 4.0 %copy-start.3 = (bf16[128,768]{1,0:T(8,128)(2,1)S(1)}, bf16[128,768]{1,0:T(8,128)(2,1)}, u32[]{:S(2)}) copy-start(bf16[128,768]{1,0:T(8,128)(2,1)} %get-tuple-element.38) | copy-start | bytes 589828
  93.8 11.4 %collective-permute-start.2 = (bf16[128,768]{1,0:T(8,128)(2,1)S(1)}, bf16[128,768]{1,0:T(8,128)(2,1)S(1)}, u32[]{:S(2)}, u32[]{:S(2)}) collective-permute-start(bf16[128,768]{1,0:T(8,128)(2,1)S(1)} %copy-done.3), channel_id=1, source_target_pairs={{0,16},{1,17},{2,18},{3,19},{4,20},{5,21},{6,22},{7,23},{8,24},{9,... | collective-permute-start | bytes 589832 | tf_op jit(solution)/shard_map/ppermute | solution.py:212
  107.6 45.8 %collective-permute-start.14 = (bf16[80,3584]{1,0:T(8,128)(2,1)S(1)}, bf16[80,3584]{1,0:T(8,128)(2,1)S(1)}, u32[]{:S(2)}, u32[]{:S(2)}) collective-permute-start(bf16[80,3584]{1,0:T(8,128)(2,1)S(1)} %get-tuple-element.57), channel_id=1, source_target_pairs={{0,16},{1,17},{2,18},{3,19},{4,20},{5,21},{6,22},{7,23},{8,24},{9,... | collective-permute-start | bytes 1720328 | tf_op jit(solution)/shard_map/ppermute | solution.py:212
  109.2 15.2 %collective-permute-start.15 = (bf16[64,3584]{1,0:T(8,128)(2,1)S(1)}, bf16[64,3584]{1,0:T(8,128)(2,1)S(1)}, u32[]{:S(2)}, u32[]{:S(2)}) collective-permute-start(bf16[64,3584]{1,0:T(8,128)(2,1)S(1)} %slice.66), channel_id=1, source_target_pairs={{0,28},{1,29},{2,30},{3,31},{4,16},{5,17},{6,18},{7,19},{8,20},{9,... | collective-permute-start | bytes 1376264 | tf_op jit(solution)/shard_map/ppermute | solution.py:212
  113.4 40.0 %collective-permute-start.16 = (bf16[64,3584]{1,0:T(8,128)(2,1)S(1)}, bf16[64,3584]{1,0:T(8,128)(2,1)S(1)}, u32[]{:S(2)}, u32[]{:S(2)}) collective-permute-start(bf16[64,3584]{1,0:T(8,128)(2,1)S(1)} %slice.67), channel_id=1, source_target_pairs={{0,24},{1,25},{2,26},{3,27},{4,28},{5,29},{6,30},{7,31},{8,16},{9,... | collective-permute-start | bytes 1376264 | tf_op jit(solution)/shard_map/ppermute | solution.py:212
  114.9 38.5 %collective-permute-start.17 = (bf16[64,3584]{1,0:T(8,128)(2,1)S(1)}, bf16[64,3584]{1,0:T(8,128)(2,1)S(1)}, u32[]{:S(2)}, u32[]{:S(2)}) collective-permute-start(bf16[64,3584]{1,0:T(8,128)(2,1)S(1)} %slice.68), channel_id=1, source_target_pairs={{0,20},{1,21},{2,22},{3,23},{4,24},{5,25},{6,26},{7,27},{8,28},{9,... | collective-permute-start | bytes 1376264 | tf_op jit(solution)/shard_map/ppermute | solution.py:212
  124.4 33.4 %collective-permute-start.11 = (bf16[320,3584]{1,0:T(8,128)(2,1)S(1)}, bf16[320,3584]{1,0:T(8,128)(2,1)S(1)}, u32[]{:S(2)}, u32[]{:S(2)}) collective-permute-start(bf16[320,3584]{1,0:T(8,128)(2,1)S(1)} %constant_dynamic-update-slice_fusion.xg_own), channel_id=1, source_target_pairs={{0,1},{1,0},{2,3},{3,2},{4,5},{5,4},{6,7},{7,6},{8,9},{9,8},{10,11... | collective-permute-start | bytes 6881288 | tf_op jit(solution)/shard_map/ppermute | solution.py:212
  153.4 4.5 %collective-permute-start.18 = (bf16[320,3584]{1,0:T(8,128)(2,1)S(1)}, bf16[320,3584]{1,0:T(8,128)(2,1)S(1)}, u32[]{:S(2)}, u32[]{:S(2)}) collective-permute-start(bf16[320,3584]{1,0:T(8,128)(2,1)S(1)} %collective-permute-done.12.xg_y), channel_id=1, source_target_pairs={{0,1},{1,0},{2,3},{3,2},{4,5},{5,4},{6,7},{7,6},{8,9},{9,8},{10,11... | collective-permute-start | bytes 6881288 | tf_op jit(solution)/shard_map/ppermute | solution.py:212
  153.5 12.3 %collective-permute-start.19 = (bf16[16,3584]{1,0:T(8,128)(2,1)S(1)}, bf16[16,3584]{1,0:T(8,128)(2,1)S(1)}, u32[]{:S(2)}, u32[]{:S(2)}) collective-permute-start(bf16[16,3584]{1,0:T(8,128)(2,1)S(1)} %slice.69), channel_id=1, source_target_pairs={{0,28},{1,29},{2,30},{3,31},{4,16},{5,17},{6,18},{7,19},{8,20},{9,... | collective-permute-start | bytes 344072 | tf_op jit(solution)/shard_map/ppermute | solution.py:212
  154.8 13.6 %collective-permute-start.20 = (bf16[16,3584]{1,0:T(8,128)(2,1)S(1)}, bf16[16,3584]{1,0:T(8,128)(2,1)S(1)}, u32[]{:S(2)}, u32[]{:S(2)}) collective-permute-start(bf16[16,3584]{1,0:T(8,128)(2,1)S(1)} %slice.70), channel_id=1, source_target_pairs={{0,24},{1,25},{2,26},{3,27},{4,28},{5,29},{6,30},{7,31},{8,16},{9,... | collective-permute-start | bytes 344072 | tf_op jit(solution)/shard_map/ppermute | solution.py:212
  157.5 10.9 %collective-permute-start.21 = (bf16[16,3584]{1,0:T(8,128)(2,1)S(1)}, bf16[16,3584]{1,0:T(8,128)(2,1)S(1)}, u32[]{:S(2)}, u32[]{:S(2)}) collective-permute-start(bf16[16,3584]{1,0:T(8,128)(2,1)S(1)} %slice.71), channel_id=1, source_target_pairs={{0,20},{1,21},{2,22},{3,23},{4,24},{5,25},{6,26},{7,27},{8,28},{9,... | collective-permute-start | bytes 344072 | tf_op jit(solution)/shard_map/ppermute | solution.py:212

commit v4 on v3

--- a/solution.py
+++ b/solution.py
@@ -43,7 +43,7 @@
     outs, tables, (f_ref, x_ref, g_ref, sems) = refs[:experts], refs[experts:-4], refs[-4:]
     copies = start_copies(((f_any, f_ref), (x_any, x_ref), (g_any, g_ref)), sems)
     tok_rows = f_ref.shape[0]
-    wide = tables[0].shape[1] // 2
+    wide = table_width(experts, 2 * cap if joined else cap)
     mine = mine_ref[0]
     row = lax.broadcasted_iota(jnp.int32, (tok_rows, tok_rows), 0)
     col = lax.broadcasted_iota(jnp.int32, (tok_rows, tok_rows), 1)
@@ -80,15 +80,22 @@
         outs[k][...] = jnp.concatenate([rows_f, rows_x, rows_g], axis=0).astype(BF16)
 
     if joined:
-        slots_f = [[part for k in range(experts) for part in (parts[k], empty)] for parts in (gated_f, rest_f)]
-        slots_b = [part for k in range(experts) for part in (empty, hits_b[k])]
-        tops = ((tables[0], 0, slots_f), (tables[0], tok_rows, [slots_b, None]))
+        slots = [[part for k in range(experts) for part in (gated_f[k], hits_b[k])]]
+        slots = [(tables[0], slots + [[part for k in range(experts) for part in (rest_f[k], empty)]])]
     else:
-        tops = ((tables[0], 0, [gated_f, rest_f]), (tables[1], 0, [hits_b, None]))
-    for table, low, slots in tops:
-        for i, part in enumerate(slots):
-            value = jnp.zeros((tok_rows, wide), BF16) if part is None else by_token(part)
-            table[low:low + tok_rows, i * wide:(i + 1) * wide] = value
+        slots = [(tables[0], [gated_f, rest_f]), (tables[1], [hits_b])]
+    for table, parts in slots:
+        for i, part in enumerate(parts):
+            table[:, i * wide:(i + 1) * wide] = by_token(part)
+
+
+def table_width(experts, each):
+    return -(-experts * each // LANES) * LANES
+
+
+def stage_kernel(*refs):
+    for copy in start_copies(zip(refs[:4], refs[4:8]), refs[8]):
+        copy.wait()
 
 
 def silu_slope(pre):
@@ -167,24 +174,40 @@
         copy.wait()
 
 
-def combine_kernel(experts, count, tables, *refs):
-    base, refs = refs[:count], refs[count:]
-    whole, late, outs = refs[:experts], refs[experts:2 * experts - 1], refs[2 * experts - 1:]
-    tokens, width = tables.shape[0], whole[0].shape[1]
-    wide = tables.shape[1] // 2
-    each = whole[0].shape[0]
-    table = jnp.concatenate([tables[:, :wide], tables[:, wide:]], axis=0)
-    pieces = [(0, whole[0])]
-    for k in range(1, experts):
-        pieces += [(k * each, whole[k]), (k * each + whole[k].shape[0], late[k - 1])]
-    tile = width // 7
-    for low in range(0, width, tile):
-        cols = slice(low, low + tile)
-        picked = sum(dot(table[:, at:at + part.shape[0]], part[:, cols], (1, 0)) for at, part in pieces)
-        picked = picked[:tokens] + picked[tokens:]
-        rows = tokens // count
+def picked_rows(experts, each, count, table, pieces, cols):
+    tokens, wide = table.shape[0], table_width(experts, each)
+    parts = [table[:, low:low + wide] for low in range(0, table.shape[1], wide)]
+    if count == 2:
+        forth = lax.broadcasted_iota(jnp.int32, (tokens, wide), 1) % each < each // 2
+        parts = [jnp.where(forth, parts[0], 0), jnp.where(forth, 0, parts[0]), parts[1]]
+    tables = jnp.concatenate(parts, axis=0)
+    picked = sum(dot(tables[:, at:at + part.shape[0]], part[:, cols], (1, 0)) for at, part in pieces)
+    total = picked[:count * tokens]
+    if len(parts) > count:
+        low = [picked[count * tokens:]]
+        total = total + jnp.concatenate(low + [jnp.zeros((tokens, low[0].shape[1]), F32)] * (count - 1), axis=0)
+    return total
+
+
+def combine_first_kernel(each, count, table, *refs):
+    base, whole, out = refs[:count], refs[count:-1], refs[-1]
+    rows, width = base[0].shape
+    pieces = [(k * each, part) for k, part in enumerate(whole)]
+    for low in range(0, width, width // 7):
+        cols = slice(low, low + width // 7)
+        picked = picked_rows(len(whole), each, count, table, pieces, cols)
+        for i in range(count):
+            span = slice(i * rows, (i + 1) * rows)
+            out[span, cols] = base[i][:, cols].astype(F32) + picked[span]
+
+
+def combine_kernel(experts, each, at, table, total, late, *outs):
+    rows, width = outs[0].shape
+    for low in range(0, width, width // 7):
+        cols = slice(low, low + width // 7)
+        picked = total[:, cols] + picked_rows(experts, each, len(outs), table, [(at, late)], cols)
         for i, out in enumerate(outs):
-            out[:, cols] = (base[i][:, cols].astype(F32) + picked[i * rows:(i + 1) * rows]).astype(BF16)
+            out[:, cols] = picked[i * rows:(i + 1) * rows].astype(BF16)
 
 
 def local(
@@ -200,7 +223,7 @@
     count = experts * cap
     joined = sections == 2
     each = 2 * cap if joined else cap
-    wide = -(-experts * each // LANES) * LANES
+    wide = table_width(experts, each)
 
     def send(value, planes=0, flip=0, pipes=0):
         pairs = []
@@ -230,7 +253,7 @@
     up_c, down_c = send(up_own, flip=1), send(down_own, flip=1)
     up_y, down_y = send(up_own, flip=2), send(down_own, flip=2)
     res_f = send(fwd_input, pipes=1)
-    tables = [shape(2 * tok_rows, 2 * wide)] if joined else [shape(tok_rows, 2 * wide)] * 2
+    tables = [shape(tok_rows, 2 * wide)] + ([] if joined else [shape(tok_rows, wide)])
     built = call(
         lambda *refs: build_kernel(experts, cap, joined, *refs),
         "build",
@@ -248,55 +271,74 @@
     got = [rows_out[0]] + after(rows_out[1:], up_c, down_c)
     got[-1:] = after(got[-1:], res_f)
     got[1:] = [send(part, planes=k) for k, part in enumerate(got[1:], 1)]
-    up_d, down_d = send(up_y, flip=1), send(down_y, flip=1)
-    out_grad, *tables = after([out_grad, *tables], up_d)
     res_b = send(out_grad, pipes=-1)
     tables = [send(table, pipes=1 - 2 * i) for i, table in enumerate(tables)]
+    up_in, down_in, down_c, up_in_y = call(
+        stage_kernel, "stage",
+        [shape(width, hidden), shape(hidden, width), shape(hidden, width), shape(width, hidden)],
+        after([up_own, down_own, down_c, up_y], res_b),
+        cost(0.01, 0.1),
+        limit=4,
+        in_specs=[HBM] * 4,
+        scratch_shapes=[pltpu.SemaphoreType.DMA((4,))],
+    )
+    up_d = send(up_y, flip=1)
+    down_d = send(*after([down_y], up_in), flip=1)
 
     rows_f, rows_x, rows_g = (
         jnp.concatenate([part[i * cap:(i + 1) * cap] for part in got], axis=0) for i in range(3)
     )
     rows_xg = jnp.concatenate([rows_x, rows_g], axis=0)
+    xg_c = send(rows_xg, flip=1)
     rows = rows_f, rows_x, rows_g = rows_f, rows_x, rows_g
     act_f, dpre = call(
-        own_kernel, "own", [shape(count, 2 * hidden)] * 2, (*rows, up_own, down_own, up_c, down_c), cost(2, 12)
+        own_kernel, "own", [shape(count, 2 * hidden)] * 2, (*rows, up_in, down_in, up_c, down_c), cost(2, 12)
     )
     part_f, part_b = call(
         near_kernel,
         "near",
         [shape(count, width, dtype=F32)] * 2,
-        (*rows, act_f, dpre, up_own, down_own, up_c, down_c, up_y, down_y),
+        (*rows, act_f, dpre, up_in, down_in, up_c, down_c, up_in_y, down_y),
         cost(3, 18),
     )
     outs = call(
         lambda *refs: far_kernel(cap, joined, *refs),
         "far",
         [shape(each, width)] * experts if joined else [shape(cap, width)] * (2 * experts),
-        (*after(rows, res_b, *tables), part_f, part_b, up_d, down_d),
+        (*after(rows, xg_c, *tables), part_f, part_b, up_d, down_d),
         cost(2, 10),
     )
 
-    split = 4 * each // 5 // 16 * 16
-    ways = range(2 * experts if not joined else experts)
-    early = [outs[i] if i % experts == 0 else outs[i][:split] for i in ways]
-    late = [None if i % experts == 0 else outs[i][split:] for i in ways]
+    middle = experts // 2
+    split = max(3 * each // 5 // 16 * 16, each // 2)
+    ways = range(len(outs))
 
     def back(value, i):
         return send(value, planes=-(i % experts), pipes=1 if i < experts else -1)
 
-    ret = [back(early[i], i) for i in ways]
-    ret_late = after([part for part in late if part is not None], *ret)
-    ret_late = [back(part, i) for part, i in zip(ret_late, [i for i in ways if i % experts])]
+    ret = [back(outs[i][:split] if i % experts == middle else outs[i], i) for i in ways]
+    ret_late = after([outs[i][split:] for i in ways if i % experts == middle], *ret)
+    ret_late = [back(part, i * experts + middle) for i, part in enumerate(ret_late)]
 
     xg_y = send(*after([rows_xg], up_y, down_y), flip=2)
-    xg_c = send(*after([rows_xg], up_d, down_d), flip=1)
     xg_d = send(*after([xg_y], *ret), flip=1)
+    bases = [(res_f, res_b)] if joined else [(res_f,), (res_b,)]
+    totals = []
+    for i, (base, table) in enumerate(zip(bases, tables)):
+        totals += call(
+            lambda *refs: combine_first_kernel(each, len(base), *refs),
+            "combine_first",
+            [shape(len(base) * tok_rows, width, dtype=F32)],
+            (table, *base, *ret[i * experts:(i + 1) * experts]),
+            cost(0.2, 4),
+        )
+    xg_d, *totals = after([xg_d, *totals])
     tiles = width // (2 * hidden)
     grad_up, grad_down = call(
         grads_kernel,
         "grads",
         [shape(width, hidden, dtype=F32), shape(hidden, width, dtype=F32)],
-        (rows_xg, xg_c, xg_y, xg_d, up_own, down_own),
+        (rows_xg, xg_c, xg_y, xg_d, up_in, down_in),
         cost(0.01, 0.1),
         limit=16,
         out_specs=[HBM] * 2,
@@ -307,12 +349,13 @@
 
     tables = after(tables, grad_up, grad_down)
     results = []
-    bases = [(res_f, res_b)] if joined else [(res_f,), (res_b,)]
-    for i, (base, table) in enumerate(zip(bases, tables)):
-        parts = (*ret[i * experts:(i + 1) * experts], *ret_late[i * (experts - 1):(i + 1) * (experts - 1)])
+    for i, (table, total) in enumerate(zip(tables, totals)):
         results += call(
-            lambda *refs: combine_kernel(experts, len(base), *refs),
-            "combine", [shape(tok_rows, width)] * (2 if joined else 1), (table, *base, *parts), cost(0.2, 4),
+            lambda *refs: combine_kernel(experts, each, middle * each + split, *refs),
+            "combine",
+            [shape(tok_rows, width)] * len(bases[i]),
+            (table, total, ret_late[i]),
+            cost(0.1, 3),
         )
     fwd_next, back_next = results
     return (fwd_next[None], back_next[None], grad_up[None, None], grad_down[None, None])

time: 173 us -> 166 us (0.960)
  Pallas kernels: 29.5 us -> 26.5 us
  waiting for transfers between devices: 109 us -> 107 us
  starting transfers between devices: 30.2 us -> 28.4 us
    pallas_call x6 -> x8, Pallas kernels: 29.5 us -> 26.5 us  [call(): pl.pallas_call(kernel, out_shape=out_shape, in_specs=more.pop('in_specs',...]
    ppermute x22 -> x20, starting transfers between devices: 30.2 us -> 28.4 us  [send(): return lax.ppermute(value, ('pipe', 'expert'), pairs)]
    ppermute x22 -> x20, waiting for transfers between devices: 109 us -> 107 us  [send(): return lax.ppermute(value, ('pipe', 'expert'), pairs)]
  transfers between devices with their start and end apart: 22 -> 20, of which waited for: 8 -> 8; matrix products, arithmetic and copies ran while one was open for 2% -> 2% of each run, Pallas kernels for 15% -> 15%
where the time goes in v4:
time: 166 us
  waiting for transfers between devices  107 us (64%)
  starting transfers between devices  28.4 us (17%)
  Pallas kernels  26.5 us (16%)
  local copies, waits for them, and re-layouts  2.56 us (2%)
    ppermute x20, waiting for transfers between devices, send(): return lax.ppermute(value, ('pipe', 'expert'), pairs)  107 us
    ppermute x20, starting transfers between devices, send(): return lax.ppermute(value, ('pipe', 'expert'), pairs)  28.4 us
    pallas_call x8, Pallas kernels, call(): pl.pallas_call(kernel, out_shape=out_shape, in_specs=more.pop('in_specs',...  26.5 us
  transfers between devices with their start and end apart: 20, of which 8 were waited for; matrix products, arithmetic and copies ran while one was open for 2% of the time, Pallas kernels for 15%

profile of v4, /device:TPU:0, one launch (start us, length us, event | category | flops | bytes accessed | tf_op | source)
XLA Modules:
  0.0 165.6 jit_solution(17665639233953242593)
XLA Ops:
  0.6 0.5 collective-permute-start.1
  1.2 2.6 %collective-permute-start.8 = (bf16[3584,256]{1,0:T(8,128)(2,1)}, bf16[3584,256]{1,0:T(8,128)(2,1)}, u32[]{:S(2)}, u32[]{:S(2)}) collective-permute-start(bf16[3584,256]{1,0:T(8,128)(2,1)} %bitcast.23), channel_id=1, source_target_pairs={{0,2},{1,3},{2,0},{3,1},{4,6},{5,7},{6,4},{7,5},{8,10},{9,11},{10,... | collective-permute-start | bytes 5505032 | tf_op jit(solution)/shard_map/ppermute | solution.py:235
  3.7 0.2 collective-permute-start.2
  3.9 1.5 collective-permute-start.5
  5.4 0.5 collective-permute-start.11
  5.9 0.0 copy-start.1
  5.9 4.4 %build.1 = (bf16[120,3584]{1,0:T(8,128)(2,1)}, bf16[120,3584]{1,0:T(8,128)(2,1)}, bf16[120,3584]{1,0:T(8,128)(2,1)}, bf16[120,3584]{1,0:T(8,128)(2,1)}, bf16[64,768]{1,0:T(8,128)(2,1)}) custom-call(s32[1]{0:T(128)} %bitcast.refs_0_, s32[2,64]{1,0:T(2,128)} %bitcast.37, f32[2,64]{1,0:T(2,128)} %bitcast.38, s32[2,64]{1,0:T(2,128)} %bitcast.39, ...), custom_call_target="tpu_custom_call" | custom-call | flops 99999997952 | bytes 104857 | tf_op jit(solution)/shard_map/build/pallas_call | solution.py:238
  10.3 0.0 collective-permute-done.1.up_c
  10.3 0.0 copy-done.1
  10.4 0.3 collective-permute-start.9
  10.7 0.0 collective-permute-done.2.refs_2_
  10.7 1.8 %collective-permute-start.3 = (bf16[120,3584]{1,0:T(8,128)(2,1)}, bf16[120,3584]{1,0:T(8,128)(2,1)S(1)}, u32[]{:S(2)}, u32[]{:S(2)}) collective-permute-start(bf16[120,3584]{1,0:T(8,128)(2,1)} %get-tuple-element.48), channel_id=1, source_target_pairs={{0,4},{1,5},{2,6},{3,7},{4,8},{5,9},{6,10},{7,11},{8,12},{9,13},{1... | collective-permute-start | bytes 2580488 | tf_op jit(solution)/shard_map/ppermute | solution.py:235
  12.5 1.2 fusion
  13.7 3.7 %collective-permute-done.5.refs_1_ = bf16[64,3584]{1,0:T(8,128)(2,1)S(1)} collective-permute-done((bf16[64,3584]{1,0:T(8,128)(2,1)}, bf16[64,3584]{1,0:T(8,128)(2,1)S(1)}, u32[]{:S(2)}, u32[]{:S(2)}) %collective-permute-start.5) | collective-permute-done | bytes 458784 | tf_op jit(solution)/shard_map/ppermute | solution.py:235
  17.5 2.6 %collective-permute-start.4 = (bf16[120,3584]{1,0:T(8,128)(2,1)}, bf16[120,3584]{1,0:T(8,128)(2,1)S(1)}, u32[]{:S(2)}, u32[]{:S(2)}) collective-permute-start(bf16[120,3584]{1,0:T(8,128)(2,1)} %get-tuple-element.49), channel_id=1, source_target_pairs={{0,8},{1,9},{2,10},{3,11},{4,12},{5,13},{6,14},{7,15},{8,0},{9,1},... | collective-permute-start | bytes 2580488 | tf_op jit(solution)/shard_map/ppermute | solution.py:235
  20.0 14.8 %collective-permute-done.3 = bf16[120,3584]{1,0:T(8,128)(2,1)S(1)} collective-permute-done((bf16[120,3584]{1,0:T(8,128)(2,1)}, bf16[120,3584]{1,0:T(8,128)(2,1)S(1)}, u32[]{:S(2)}, u32[]{:S(2)}) %collective-permute-start.3) | collective-permute-done | bytes 860192 | tf_op jit(solution)/shard_map/ppermute | solution.py:235
  34.8 0.9 collective-permute-start.6
  35.8 0.1 fusion.1
  35.9 34.6 %collective-permute-done.4 = bf16[120,3584]{1,0:T(8,128)(2,1)S(1)} collective-permute-done((bf16[120,3584]{1,0:T(8,128)(2,1)}, bf16[120,3584]{1,0:T(8,128)(2,1)S(1)}, u32[]{:S(2)}, u32[]{:S(2)}) %collective-permute-start.4) | collective-permute-done | bytes 860192 | tf_op jit(solution)/shard_map/ppermute | solution.py:235
  70.5 0.1 fusion.2
  70.6 0.0 copy-start
  70.6 11.2 %collective-permute-done.6 = bf16[120,3584]{1,0:T(8,128)(2,1)S(1)} collective-permute-done((bf16[120,3584]{1,0:T(8,128)(2,1)}, bf16[120,3584]{1,0:T(8,128)(2,1)S(1)}, u32[]{:S(2)}, u32[]{:S(2)}) %collective-permute-start.6) | collective-permute-done | bytes 860192 | tf_op jit(solution)/shard_map/ppermute | solution.py:235
  81.8 0.1 fusion.3
  81.9 1.0 constant_dynamic-update-slice_fusion.3
  83.0 0.0 copy-start.2
  83.0 0.1 collective-permute-start.7
  83.1 0.0 collective-permute-done.11.refs_2_
  83.1 0.0 collective-permute-done.8.refs_3_
  83.1 0.0 copy-done
  83.1 2.3 %stage.1 = (bf16[3584,256]{1,0:T(8,128)(2,1)S(1)}, bf16[256,3584]{1,0:T(8,128)(2,1)S(1)}, bf16[256,3584]{1,0:T(8,128)(2,1)S(1)}, bf16[3584,256]{1,0:T(8,128)(2,1)S(1)}) custom-call(bf16[3584,256]{1,0:T(8,128)(2,1)S(1)} %bitcast.24, bf16[256,3584]{1,0:T(8,128)(2,1)S(1)} %bitcast.27, bf16[256,3584]{1,0:T(8,128)(2,1)} %collective-permute-done.2.refs_2_, ...), custom_call_target="tpu_custom_call" | custom-call | flops 10000000 | bytes 104857 | tf_op jit(solution)/shard_map/stage/pallas_call | solution.py:238
  85.4 0.0 collective-permute-done.9.down_y
  85.4 0.5 collective-permute-start.13
  86.0 0.1 collective-permute-start.12
  86.1 1.5 collective-permute-start.10
  87.6 0.0 copy-done.2
  87.6 1.5 collective-permute-start
  89.1 0.1 pad_maximum_fusion.2.rows_g.refs_2_
  89.2 0.2 pad_maximum_fusion
  89.4 2.4 %own.1 = (bf16[160,512]{1,0:T(8,128)(2,1)S(1)}, bf16[160,512]{1,0:T(8,128)(2,1)S(1)}) custom-call(bf16[160,3584]{1,0:T(8,128)(2,1)S(1)} %get-tuple-element.53.rows_f.refs_0_, bf16[160,3584]{1,0:T(8,128)(2,1)S(1)} %get-tuple-element.54.rows_x.refs_1_, bf16[160,3584]{1,0:T(8,128)(2,1)S(1)} %pad_maximum_fusion.2.rows_g.refs_2_, ...), custom_call_target="tpu_custom_call" | custom-call | flops 2000000000 | bytes 12582912 | tf_op jit(solution)/shard_map/own/pallas_call | solution.py:238
  91.8 4.0 %near.1 = (f32[160,3584]{1,0:T(8,128)S(1)}, f32[160,3584]{1,0:T(8,128)S(1)}) custom-call(bf16[160,3584]{1,0:T(8,128)(2,1)S(1)} %get-tuple-element.53.rows_f.refs_0_, bf16[160,3584]{1,0:T(8,128)(2,1)S(1)} %get-tuple-element.54.rows_x.refs_1_, bf16[160,3584]{1,0:T(8,128)(2,1)S(1)} %pad_maximum_fusion.2.rows_g.refs_2_, ...), custom_call_target="tpu_custom_call" | custom-call | flops 3000000000 | bytes 18874368 | tf_op jit(solution)/shard_map/near/pallas_call | solution.py:238
  95.8 0.0 collective-permute-done.refs_0_
  95.8 0.0 collective-permute-done.7.xg_c
  95.8 0.0 collective-permute-done.13.refs_6_
  95.8 0.0 collective-permute-done.12.refs_5_
  95.9 2.4 %far.1 = (bf16[80,3584]{1,0:T(8,128)(2,1)S(1)}, bf16[80,3584]{1,0:T(8,128)(2,1)S(1)}, bf16[80,3584]{1,0:T(8,128)(2,1)S(1)}, bf16[80,3584]{1,0:T(8,128)(2,1)S(1)}) custom-call(bf16[160,3584]{1,0:T(8,128)(2,1)S(1)} %get-tuple-element.53.rows_f.refs_0_, bf16[160,3584]{1,0:T(8,128)(2,1)S(1)} %get-tuple-element.54.rows_x.refs_1_, ...), custom_call_target="tpu_custom_call" | custom-call | flops 2000000000 | bytes 10485760 | tf_op jit(solution)/shard_map/far/pallas_call | solution.py:238
  98.2 0.6 collective-permute-start.14
  98.9 9.9 %collective-permute-start.15 = (bf16[80,3584]{1,0:T(8,128)(2,1)S(1)}, bf16[80,3584]{1,0:T(8,128)(2,1)S(1)}, u32[]{:S(2)}, u32[]{:S(2)}) collective-permute-start(bf16[80,3584]{1,0:T(8,128)(2,1)S(1)} %get-tuple-element.70), channel_id=1, source_target_pairs={{0,28},{1,29},{2,30},{3,31},{4,16},{5,17},{6,18},{7,19},{8,20},{9,... | collective-permute-start | bytes 1720328 | tf_op jit(solution)/shard_map/ppermute | solution.py:235
  108.8 0.0 collective-permute-start.17
  108.8 0.7 collective-permute-start.16
  109.5 28.8 %collective-permute-done.10.xg_y = bf16[320,3584]{1,0:T(8,128)(2,1)S(1)} collective-permute-done((bf16[320,3584]{1,0:T(8,128)(2,1)S(1)}, bf16[320,3584]{1,0:T(8,128)(2,1)S(1)}, u32[]{:S(2)}, u32[]{:S(2)}) %collective-permute-start.10) | collective-permute-done | bytes 2293792 | tf_op jit(solution)/shard_map/ppermute | solution.py:235
  138.3 11.0 %collective-permute-done.16.refs_5_ = bf16[48,3584]{1,0:T(8,128)(2,1)S(1)} collective-permute-done((bf16[48,3584]{1,0:T(8,128)(2,1)S(1)}, bf16[48,3584]{1,0:T(8,128)(2,1)S(1)}, u32[]{:S(2)}, u32[]{:S(2)}) %collective-permute-start.16) | collective-permute-done | bytes 344096 | tf_op jit(solution)/shard_map/ppermute | solution.py:235
  149.2 0.0 collective-permute-done.14.refs_3_
  149.3 0.0 collective-permute-done.15.refs_4_
  149.3 0.0 collective-permute-done.17.refs_6_
  149.3 0.1 collective-permute-start.18
  149.4 2.5 %collective-permute-start.19 = (bf16[32,3584]{1,0:T(8,128)(2,1)S(1)}, bf16[32,3584]{1,0:T(8,128)(2,1)S(1)}, u32[]{:S(2)}, u32[]{:S(2)}) collective-permute-start(bf16[32,3584]{1,0:T(8,128)(2,1)S(1)} %slice.55), channel_id=1, source_target_pairs={{0,24},{1,25},{2,26},{3,27},{4,28},{5,29},{6,30},{7,31},{8,16},{9,... | collective-permute-start | bytes 688136 | tf_op jit(solution)/shard_map/ppermute | solution.py:235
  151.8 1.6 combine_first.1.refs_1_
  153.5 0.3 collective-permute-done.18.xg_d
  153.8 7.9 %grads.1 = (f32[3584,256]{1,0:T(8,128)}, f32[256,3584]{1,0:T(8,128)}) custom-call(bf16[320,3584]{1,0:T(8,128)(2,1)S(1)} %constant_dynamic-update-slice_fusion.xg_own, bf16[320,3584]{1,0:T(8,128)(2,1)S(1)} %collective-permute-done.7.xg_c, bf16[320,3584]{1,0:T(8,128)(2,1)S(1)} %collective-permute-done.10.xg_y, ...), custom_call_target="tpu_custom_call" | custom-call | flops 10000000 | bytes 104857 | tf_op jit(solution)/shard_map/grads/pallas_call | solution.py:238
  161.7 2.5 %collective-permute-done.19.refs_2_ = bf16[32,3584]{1,0:T(8,128)(2,1)S(1)} collective-permute-done((bf16[32,3584]{1,0:T(8,128)(2,1)S(1)}, bf16[32,3584]{1,0:T(8,128)(2,1)S(1)}, u32[]{:S(2)}, u32[]{:S(2)}) %collective-permute-start.19) | collective-permute-done | bytes 229408 | tf_op jit(solution)/shard_map/ppermute | solution.py:235
  164.1 1.5 combine.1
  (5 shorter events, 0.1 us)
Async XLA Ops:
  0.6 9.7 %collective-permute-start.1 = (bf16[3584,256]{1,0:T(8,128)(2,1)}, bf16[3584,256]{1,0:T(8,128)(2,1)S(1)}, u32[]{:S(2)}, u32[]{:S(2)}) collective-permute-start(bf16[3584,256]{1,0:T(8,128)(2,1)} %bitcast.22), channel_id=1, source_target_pairs={{0,1},{1,0},{2,3},{3,2},{4,5},{5,4},{6,7},{7,6},{8,9},{9,8},{10,11... | collective-permute-start | bytes 5505032 | tf_op jit(solution)/shard_map/ppermute | solution.py:235
  1.2 81.9 %collective-permute-start.8 = (bf16[3584,256]{1,0:T(8,128)(2,1)}, bf16[3584,256]{1,0:T(8,128)(2,1)}, u32[]{:S(2)}, u32[]{:S(2)}) collective-permute-start(bf16[3584,256]{1,0:T(8,128)(2,1)} %bitcast.23), channel_id=1, source_target_pairs={{0,2},{1,3},{2,0},{3,1},{4,6},{5,7},{6,4},{7,5},{8,10},{9,11},{10,... | collective-permute-start | bytes 5505032 | tf_op jit(solution)/shard_map/ppermute | solution.py:235
  3.7 7.0 %collective-permute-start.2 = (bf16[256,3584]{1,0:T(8,128)(2,1)}, bf16[256,3584]{1,0:T(8,128)(2,1)}, u32[]{:S(2)}, u32[]{:S(2)}) collective-permute-start(bf16[256,3584]{1,0:T(8,128)(2,1)} %bitcast.25), channel_id=1, source_target_pairs={{0,1},{1,0},{2,3},{3,2},{4,5},{5,4},{6,7},{7,6},{8,9},{9,8},{10,11... | collective-permute-start | bytes 5505032 | tf_op jit(solution)/shard_map/ppermute | solution.py:235
  3.9 13.5 %collective-permute-start.5 = (bf16[64,3584]{1,0:T(8,128)(2,1)}, bf16[64,3584]{1,0:T(8,128)(2,1)S(1)}, u32[]{:S(2)}, u32[]{:S(2)}) collective-permute-start(bf16[64,3584]{1,0:T(8,128)(2,1)} %bitcast.31), channel_id=1, source_target_pairs={{0,16},{1,17},{2,18},{3,19},{4,20},{5,21},{6,22},{7,23},{8,24},{9,... | collective-permute-start | bytes 1376264 | tf_op jit(solution)/shard_map/ppermute | solution.py:235
  5.4 77.7 %collective-permute-start.11 = (bf16[64,3584]{1,0:T(8,128)(2,1)}, bf16[64,3584]{1,0:T(8,128)(2,1)S(1)}, u32[]{:S(2)}, u32[]{:S(2)}) collective-permute-start(bf16[64,3584]{1,0:T(8,128)(2,1)} %bitcast.33), channel_id=1, source_target_pairs={{0,16},{1,17},{2,18},{3,19},{4,20},{5,21},{6,22},{7,23},{8,24},{9,... | collective-permute-start | bytes 1376264 | tf_op jit(solution)/shard_map/ppermute | solution.py:235
  5.9 4.4 %copy-start.1 = (bf16[1,1,256,3584]{3,2,1,0:T(8,128)(2,1)S(1)}, bf16[1,1,256,3584]{3,2,1,0:T(8,128)(2,1)}, u32[]{:S(2)}) copy-start(bf16[1,1,256,3584]{3,2,1,0:T(8,128)(2,1)} %param.17) | copy-start | bytes 5505028
  10.4 75.1 %collective-permute-start.9 = (bf16[256,3584]{1,0:T(8,128)(2,1)S(1)}, bf16[256,3584]{1,0:T(8,128)(2,1)S(1)}, u32[]{:S(2)}, u32[]{:S(2)}) collective-permute-start(bf16[256,3584]{1,0:T(8,128)(2,1)S(1)} %bitcast.26), channel_id=1, source_target_pairs={{0,2},{1,3},{2,0},{3,1},{4,6},{5,7},{6,4},{7,5},{8,10},{9,11},{10,... | collective-permute-start | bytes 5505032 | tf_op jit(solution)/shard_map/ppermute | solution.py:235
  10.7 24.1 %collective-permute-start.3 = (bf16[120,3584]{1,0:T(8,128)(2,1)}, bf16[120,3584]{1,0:T(8,128)(2,1)S(1)}, u32[]{:S(2)}, u32[]{:S(2)}) collective-permute-start(bf16[120,3584]{1,0:T(8,128)(2,1)} %get-tuple-element.48), channel_id=1, source_target_pairs={{0,4},{1,5},{2,6},{3,7},{4,8},{5,9},{6,10},{7,11},{8,12},{9,13},{1... | collective-permute-start | bytes 2580488 | tf_op jit(solution)/shard_map/ppermute | solution.py:235
  17.5 53.0 %collective-permute-start.4 = (bf16[120,3584]{1,0:T(8,128)(2,1)}, bf16[120,3584]{1,0:T(8,128)(2,1)S(1)}, u32[]{:S(2)}, u32[]{:S(2)}) collective-permute-start(bf16[120,3584]{1,0:T(8,128)(2,1)} %get-tuple-element.49), channel_id=1, source_target_pairs={{0,8},{1,9},{2,10},{3,11},{4,12},{5,13},{6,14},{7,15},{8,0},{9,1},... | collective-permute-start | bytes 2580488 | tf_op jit(solution)/shard_map/ppermute | solution.py:235
  34.8 47.0 %collective-permute-start.6 = (bf16[120,3584]{1,0:T(8,128)(2,1)}, bf16[120,3584]{1,0:T(8,128)(2,1)S(1)}, u32[]{:S(2)}, u32[]{:S(2)}) collective-permute-start(bf16[120,3584]{1,0:T(8,128)(2,1)} %get-tuple-element.51), channel_id=1, source_target_pairs={{0,12},{1,13},{2,14},{3,15},{4,0},{5,1},{6,2},{7,3},{8,4},{9,5},{1... | collective-permute-start | bytes 2580488 | tf_op jit(solution)/shard_map/ppermute | solution.py:235
  70.6 12.5 %copy-start = (bf16[1,1,3584,256]{3,2,1,0:T(8,128)(2,1)S(1)}, bf16[1,1,3584,256]{3,2,1,0:T(8,128)(2,1)}, u32[]{:S(2)}) copy-start(bf16[1,1,3584,256]{3,2,1,0:T(8,128)(2,1)} %param.16) | copy-start | bytes 5505028
  83.0 4.6 %copy-start.2 = (bf16[64,768]{1,0:T(8,128)(2,1)S(1)}, bf16[64,768]{1,0:T(8,128)(2,1)}, u32[]{:S(2)}) copy-start(bf16[64,768]{1,0:T(8,128)(2,1)} %get-tuple-element.43) | copy-start | bytes 294916
  83.0 12.8 %collective-permute-start.7 = (bf16[320,3584]{1,0:T(8,128)(2,1)S(1)}, bf16[320,3584]{1,0:T(8,128)(2,1)S(1)}, u32[]{:S(2)}, u32[]{:S(2)}) collective-permute-start(bf16[320,3584]{1,0:T(8,128)(2,1)S(1)} %constant_dynamic-update-slice_fusion.xg_own), channel_id=1, source_target_pairs={{0,1},{1,0},{2,3},{3,2},{4,5},{5,4},{6,7},{7,6},{8,9},{9,8},{10,11... | collective-permute-start | bytes 6881288 | tf_op jit(solution)/shard_map/ppermute | solution.py:235
  85.4 10.4 %collective-permute-start.13 = (bf16[256,3584]{1,0:T(8,128)(2,1)S(1)}, bf16[256,3584]{1,0:T(8,128)(2,1)S(1)}, u32[]{:S(2)}, u32[]{:S(2)}) collective-permute-start(bf16[256,3584]{1,0:T(8,128)(2,1)S(1)} %collective-permute-done.9.down_y), channel_id=1, source_target_pairs={{0,1},{1,0},{2,3},{3,2},{4,5},{5,4},{6,7},{7,6},{8,9},{9,8},{10,11... | collective-permute-start | bytes 5505032 | tf_op jit(solution)/shard_map/ppermute | solution.py:235
  86.0 9.9 %collective-permute-start.12 = (bf16[3584,256]{1,0:T(8,128)(2,1)}, bf16[3584,256]{1,0:T(8,128)(2,1)S(1)}, u32[]{:S(2)}, u32[]{:S(2)}) collective-permute-start(bf16[3584,256]{1,0:T(8,128)(2,1)} %collective-permute-done.8.refs_3_), channel_id=1, source_target_pairs={{0,1},{1,0},{2,3},{3,2},{4,5},{5,4},{6,7},{7,6},{8,9},{9,8},{10,11... | collective-permute-start | bytes 5505032 | tf_op jit(solution)/shard_map/ppermute | solution.py:235
  86.1 52.2 %collective-permute-start.10 = (bf16[320,3584]{1,0:T(8,128)(2,1)S(1)}, bf16[320,3584]{1,0:T(8,128)(2,1)S(1)}, u32[]{:S(2)}, u32[]{:S(2)}) collective-permute-start(bf16[320,3584]{1,0:T(8,128)(2,1)S(1)} %constant_dynamic-update-slice_fusion.xg_own), channel_id=1, source_target_pairs={{0,2},{1,3},{2,0},{3,1},{4,6},{5,7},{6,4},{7,5},{8,10},{9,11},{10,... | collective-permute-start | bytes 6881288 | tf_op jit(solution)/shard_map/ppermute | solution.py:235
  87.6 8.2 %collective-permute-start = (bf16[64,768]{1,0:T(8,128)(2,1)S(1)}, bf16[64,768]{1,0:T(8,128)(2,1)S(1)}, u32[]{:S(2)}, u32[]{:S(2)}) collective-permute-start(bf16[64,768]{1,0:T(8,128)(2,1)S(1)} %copy-done.2), channel_id=1, source_target_pairs={{0,16},{1,17},{2,18},{3,19},{4,20},{5,21},{6,22},{7,23},{8,24},{9,... | collective-permute-start | bytes 294920 | tf_op jit(solution)/shard_map/ppermute | solution.py:235
  98.2 51.0 %collective-permute-start.14 = (bf16[80,3584]{1,0:T(8,128)(2,1)S(1)}, bf16[80,3584]{1,0:T(8,128)(2,1)S(1)}, u32[]{:S(2)}, u32[]{:S(2)}) collective-permute-start(bf16[80,3584]{1,0:T(8,128)(2,1)S(1)} %get-tuple-element.69), channel_id=1, source_target_pairs={{0,16},{1,17},{2,18},{3,19},{4,20},{5,21},{6,22},{7,23},{8,24},{9,... | collective-permute-start | bytes 1720328 | tf_op jit(solution)/shard_map/ppermute | solution.py:235
  98.9 50.4 %collective-permute-start.15 = (bf16[80,3584]{1,0:T(8,128)(2,1)S(1)}, bf16[80,3584]{1,0:T(8,128)(2,1)S(1)}, u32[]{:S(2)}, u32[]{:S(2)}) collective-permute-start(bf16[80,3584]{1,0:T(8,128)(2,1)S(1)} %get-tuple-element.70), channel_id=1, source_target_pairs={{0,28},{1,29},{2,30},{3,31},{4,16},{5,17},{6,18},{7,19},{8,20},{9,... | collective-permute-start | bytes 1720328 | tf_op jit(solution)/shard_map/ppermute | solution.py:235
  108.8 40.5 %collective-permute-start.17 = (bf16[80,3584]{1,0:T(8,128)(2,1)S(1)}, bf16[80,3584]{1,0:T(8,128)(2,1)S(1)}, u32[]{:S(2)}, u32[]{:S(2)}) collective-permute-start(bf16[80,3584]{1,0:T(8,128)(2,1)S(1)} %get-tuple-element.72), channel_id=1, source_target_pairs={{0,20},{1,21},{2,22},{3,23},{4,24},{5,25},{6,26},{7,27},{8,28},{9,... | collective-permute-start | bytes 1720328 | tf_op jit(solution)/shard_map/ppermute | solution.py:235
  108.8 40.4 %collective-permute-start.16 = (bf16[48,3584]{1,0:T(8,128)(2,1)S(1)}, bf16[48,3584]{1,0:T(8,128)(2,1)S(1)}, u32[]{:S(2)}, u32[]{:S(2)}) collective-permute-start(bf16[48,3584]{1,0:T(8,128)(2,1)S(1)} %slice.54), channel_id=1, source_target_pairs={{0,24},{1,25},{2,26},{3,27},{4,28},{5,29},{6,30},{7,31},{8,16},{9,... | collective-permute-start | bytes 1032200 | tf_op jit(solution)/shard_map/ppermute | solution.py:235
  149.3 4.5 %collective-permute-start.18 = (bf16[320,3584]{1,0:T(8,128)(2,1)S(1)}, bf16[320,3584]{1,0:T(8,128)(2,1)S(1)}, u32[]{:S(2)}, u32[]{:S(2)}) collective-permute-start(bf16[320,3584]{1,0:T(8,128)(2,1)S(1)} %collective-permute-done.10.xg_y), channel_id=1, source_target_pairs={{0,1},{1,0},{2,3},{3,2},{4,5},{5,4},{6,7},{7,6},{8,9},{9,8},{10,11... | collective-permute-start | bytes 6881288 | tf_op jit(solution)/shard_map/ppermute | solution.py:235
  149.4 14.8 %collective-permute-start.19 = (bf16[32,3584]{1,0:T(8,128)(2,1)S(1)}, bf16[32,3584]{1,0:T(8,128)(2,1)S(1)}, u32[]{:S(2)}, u32[]{:S(2)}) collective-permute-start(bf16[32,3584]{1,0:T(8,128)(2,1)S(1)} %slice.55), channel_id=1, source_target_pairs={{0,24},{1,25},{2,26},{3,27},{4,28},{5,29},{6,30},{7,31},{8,16},{9,... | collective-permute-start | bytes 688136 | tf_op jit(solution)/shard_map/ppermute | solution.py:235

commit v5 on v4

--- a/solution.py
+++ b/solution.py
@@ -40,7 +40,7 @@
 def build_kernel(
     experts, cap, joined, mine_ref, fr_ref, fg_ref, br_ref, bg_ref, f_any, x_any, g_any, *refs
 ):
-    outs, tables, (f_ref, x_ref, g_ref, sems) = refs[:experts], refs[experts:-4], refs[-4:]
+    outs, base_b, more, (f_ref, x_ref, g_ref, sems) = refs[:experts], refs[experts], refs[experts + 1:-4], refs[-4:]
     copies = start_copies(((f_any, f_ref), (x_any, x_ref), (g_any, g_ref)), sems)
     tok_rows = f_ref.shape[0]
     wide = table_width(experts, 2 * cap if joined else cap)
@@ -79,14 +79,20 @@
         rows_g = dot(hits, g_ref[...], (1, 0)) * jnp.sum(gated_b[k], axis=1, keepdims=True)
         outs[k][...] = jnp.concatenate([rows_f, rows_x, rows_g], axis=0).astype(BF16)
 
+    width = f_ref.shape[1]
+    base_b[:, :width] = g_ref[...]
+    tables = [gated_f, rest_f]
     if joined:
-        slots = [[part for k in range(experts) for part in (gated_f[k], hits_b[k])]]
-        slots = [(tables[0], slots + [[part for k in range(experts) for part in (rest_f[k], empty)]])]
+        tables[0] = [part for k in range(experts) for part in (gated_f[k], hits_b[k])]
+        tables[1] = [part for k in range(experts) for part in (rest_f[k], empty)]
     else:
-        slots = [(tables[0], [gated_f, rest_f]), (tables[1], [hits_b])]
-    for table, parts in slots:
-        for i, part in enumerate(parts):
-            table[:, i * wide:(i + 1) * wide] = by_token(part)
+        base_b[:, width:] = by_token(hits_b)
+    for i, part in enumerate(tables):
+        low = i * wide
+        if joined:
+            base_b[:, width + low:width + low + wide] = by_token(part)
+        else:
+            more[0][:, low:low + wide] = by_token(part)
 
 
 def table_width(experts, each):
@@ -94,7 +100,8 @@
 
 
 def stage_kernel(*refs):
-    for copy in start_copies(zip(refs[:4], refs[4:8]), refs[8]):
+    half = len(refs) // 2
+    for copy in start_copies(zip(refs[:half], refs[half:-1]), refs[-1]):
         copy.wait()
 
 
@@ -147,25 +154,44 @@
                 outs[experts + k][:, cols] = out_b[rows].astype(BF16)
 
 
-def grads_kernel(xg_own, xg_c, xg_y, xg_d, own_up, own_down, grad_up, grad_down, up, down, sems):
-    count = xg_own.shape[0] // 2
+def group_units(pieces, up, down):
+    count = pieces[0].shape[0] // 2
+    acts, dpres = [], []
+    for piece in pieces:
+        act, slope = silu_slope(dot(piece[:count], up[...], (1, 0)))
+        dact = dot(piece[count:], down[...], (1, 1))
+        acts.append(act.astype(BF16))
+        dpres.append((dact * slope).astype(BF16))
+    return jnp.concatenate(acts, axis=0), jnp.concatenate(dpres, axis=0)
+
+
+def group_columns(pieces, cols):
+    count = pieces[0].shape[0] // 2
+    return [jnp.concatenate([piece[low:low + count, cols] for piece in pieces], axis=0) for low in (0, count)]
+
+
+def chip_grads_kernel(xg_own, xg_c, own_up, own_down, up, down):
+    pieces = (xg_own, xg_c)
+    act, dpre = group_units(pieces, own_up, own_down)
     side, width = down.shape
-    all_x = [piece.at[:count] for piece in (xg_own, xg_c, xg_y, xg_d)]
-    all_g = [piece.at[count:] for piece in (xg_own, xg_c, xg_y, xg_d)]
-    acts, dpres = [], []
-    for rows_x, rows_g in zip(all_x, all_g):
-        act, slope = silu_slope(dot(rows_x[...], own_up[...], (1, 0)))
-        acts.append(act.astype(BF16))
-        dact = dot(rows_g[...], own_down[...], (1, 1))
-        dpres.append((dact * slope).astype(BF16))
-    act, dpre = jnp.concatenate(acts, axis=0), jnp.concatenate(dpres, axis=0)
-    tile = 2 * side
+    for low in range(0, width, 2 * side):
+        cols = slice(low, low + 2 * side)
+        rows_x, rows_g = group_columns(pieces, cols)
+        up[cols, :] = dot(rows_x, dpre, (0, 0))
+        down[:, cols] = dot(act, rows_g, (0, 0))
+
+
+def grads_kernel(xg_y, xg_d, own_up, own_down, chip_up, chip_down, grad_up, grad_down, up, down, sems):
+    pieces = (xg_y, xg_d)
+    act, dpre = group_units(pieces, own_up, own_down)
+    side, width = down.shape
     copies = []
-    for t, low in enumerate(range(0, width, tile)):
-        cols = slice(low, low + tile)
-        up[cols, :] = dot(jnp.concatenate([rows[:, cols] for rows in all_x], axis=0), dpre, (0, 0))
-        down[:, cols] = dot(act, jnp.concatenate([rows[:, cols] for rows in all_g], axis=0), (0, 0))
-        span = pl.ds(low, tile)
+    for t, low in enumerate(range(0, width, 2 * side)):
+        cols = slice(low, low + 2 * side)
+        rows_x, rows_g = group_columns(pieces, cols)
+        up[cols, :] = chip_up[cols, :] + dot(rows_x, dpre, (0, 0))
+        down[:, cols] = chip_down[:, cols] + dot(act, rows_g, (0, 0))
+        span = pl.ds(low, 2 * side)
         copies.append(pltpu.make_async_copy(up.at[span], grad_up.at[span], sems.at[0, t]))
         copies.append(pltpu.make_async_copy(down.at[:, span], grad_down.at[:, span], sems.at[1, t]))
         copies[-2].start()
@@ -191,7 +217,7 @@
 
 def combine_first_kernel(each, count, table, *refs):
     base, whole, out = refs[:count], refs[count:-1], refs[-1]
-    rows, width = base[0].shape
+    rows, width = base[0].shape[0], out.shape[1]
     pieces = [(k * each, part) for k, part in enumerate(whole)]
     for low in range(0, width, width // 7):
         cols = slice(low, low + width // 7)
@@ -251,9 +277,10 @@
 
     up_own, down_own = w_up[0, 0], w_down[0, 0]
     up_c, down_c = send(up_own, flip=1), send(down_own, flip=1)
-    up_y, down_y = send(up_own, flip=2), send(down_own, flip=2)
     res_f = send(fwd_input, pipes=1)
-    tables = [shape(tok_rows, 2 * wide)] + ([] if joined else [shape(tok_rows, wide)])
+    tables = [shape(tok_rows, width + 2 * wide)]
+    if not joined:
+        tables = [shape(tok_rows, width + wide), shape(tok_rows, 2 * wide)]
     built = call(
         lambda *refs: build_kernel(experts, cap, joined, *refs),
         "build",
@@ -267,30 +294,33 @@
         in_specs=[SMEM] + [VMEM] * 4 + [HBM] * 3,
         scratch_shapes=[pltpu.VMEM((tok_rows, width), BF16)] * 3 + [pltpu.SemaphoreType.DMA((3,))],
     )
-    rows_out, tables = built[:experts], built[experts:]
-    got = [rows_out[0]] + after(rows_out[1:], up_c, down_c)
-    got[-1:] = after(got[-1:], res_f)
-    got[1:] = [send(part, planes=k) for k, part in enumerate(got[1:], 1)]
-    res_b = send(out_grad, pipes=-1)
-    tables = [send(table, pipes=1 - 2 * i) for i, table in enumerate(tables)]
-    up_in, down_in, down_c, up_in_y = call(
+    got, tables = list(built[:experts]), built[experts:]
+
+    up_sent, down_sent = after([up_own, down_own], tables[0])
+    up_y, down_y = send(up_sent, flip=2), send(down_sent, flip=2)
+    base_b = send(tables[0], pipes=-1)
+    table_f = None if joined else send(tables[1], pipes=1)
+    got[1:] = after(got[1:], up_c, down_c)
+    got[1:-1] = [send(part, planes=k) for k, part in enumerate(got[1:-1], 1)]
+    up_in, down_in, down_c = call(
         stage_kernel, "stage",
-        [shape(width, hidden), shape(hidden, width), shape(hidden, width), shape(width, hidden)],
-        after([up_own, down_own, down_c, up_y], res_b),
+        [shape(width, hidden), shape(hidden, width), shape(hidden, width)],
+        (up_own, down_own, down_c),
         cost(0.01, 0.1),
         limit=4,
-        in_specs=[HBM] * 4,
-        scratch_shapes=[pltpu.SemaphoreType.DMA((4,))],
-    )
+        in_specs=[HBM] * 3,
+        scratch_shapes=[pltpu.SemaphoreType.DMA((3,))],
+    )
+    got[-1] = send(*after([got[-1]], up_in, res_f), planes=experts - 1)
     up_d = send(up_y, flip=1)
-    down_d = send(*after([down_y], up_in), flip=1)
+    down_d = send(*after([down_y], up_in, base_b), flip=1)
 
     rows_f, rows_x, rows_g = (
         jnp.concatenate([part[i * cap:(i + 1) * cap] for part in got], axis=0) for i in range(3)
     )
     rows_xg = jnp.concatenate([rows_x, rows_g], axis=0)
     xg_c = send(rows_xg, flip=1)
-    rows = rows_f, rows_x, rows_g = rows_f, rows_x, rows_g
+    rows = rows_f, rows_x, rows_g
     act_f, dpre = call(
         own_kernel, "own", [shape(count, 2 * hidden)] * 2, (*rows, up_in, down_in, up_c, down_c), cost(2, 12)
     )
@@ -298,19 +328,19 @@
         near_kernel,
         "near",
         [shape(count, width, dtype=F32)] * 2,
-        (*rows, act_f, dpre, up_in, down_in, up_c, down_c, up_in_y, down_y),
+        (*rows, act_f, dpre, up_in, down_in, up_c, down_c, up_y, down_y),
         cost(3, 18),
     )
     outs = call(
         lambda *refs: far_kernel(cap, joined, *refs),
         "far",
         [shape(each, width)] * experts if joined else [shape(cap, width)] * (2 * experts),
-        (*after(rows, xg_c, *tables), part_f, part_b, up_d, down_d),
+        (*after(rows, xg_c), part_f, part_b, up_d, down_d),
         cost(2, 10),
     )
 
     middle = experts // 2
-    split = max(3 * each // 5 // 16 * 16, each // 2)
+    split = 7 * each // 10 // 8 * 8
     ways = range(len(outs))
 
     def back(value, i):
@@ -321,8 +351,17 @@
     ret_late = [back(part, i * experts + middle) for i, part in enumerate(ret_late)]
 
     xg_y = send(*after([rows_xg], up_y, down_y), flip=2)
-    xg_d = send(*after([xg_y], *ret), flip=1)
-    bases = [(res_f, res_b)] if joined else [(res_f,), (res_b,)]
+    chip_up, chip_down = call(
+        chip_grads_kernel,
+        "chip_grads",
+        [shape(width, hidden, dtype=F32), shape(hidden, width, dtype=F32)],
+        (rows_xg, xg_c, up_in, down_in),
+        cost(2, 10),
+        limit=12,
+    )
+    xg_d = send(*after([xg_y], chip_up, chip_down, *ret), flip=1)
+    tables = [base_b[:, width:]] if joined else [table_f, base_b[:, width:]]
+    bases = [(res_f, base_b)] if joined else [(res_f,), (base_b,)]
     totals = []
     for i, (base, table) in enumerate(zip(bases, tables)):
         totals += call(
@@ -338,7 +377,7 @@
         grads_kernel,
         "grads",
         [shape(width, hidden, dtype=F32), shape(hidden, width, dtype=F32)],
-        (rows_xg, xg_c, xg_y, xg_d, up_in, down_in),
+        (xg_y, xg_d, up_in, down_in, chip_up, chip_down),
         cost(0.01, 0.1),
         limit=16,
         out_specs=[HBM] * 2,

time: 166 us -> 164 us (0.988)
  starting transfers between devices: 28.4 us -> 23.8 us
  Pallas kernels: 26.5 us -> 29.2 us
    ppermute x20 -> x19, starting transfers between devices: 28.4 us -> 23.8 us  [send(): return lax.ppermute(value, ('pipe', 'expert'), pairs)]
    pallas_call x8 -> x9, Pallas kernels: 26.5 us -> 29.2 us  [call(): pl.pallas_call(kernel, out_shape=out_shape, in_specs=more.pop('in_specs',...]
    ppermute x20 -> x19, waiting for transfers between devices: 107 us -> 107 us  [send(): return lax.ppermute(value, ('pipe', 'expert'), pairs)]
  transfers between devices with their start and end apart: 20 -> 19, of which waited for: 8 -> 8; matrix products, arithmetic and copies ran while one was open for 2% -> 2% of each run, Pallas kernels for 15% -> 17%
where the time goes in v5:
time: 164 us; the launch traced here: 163 us
  waiting for transfers between devices  107 us (65%)
  Pallas kernels  29.2 us (18%)
  starting transfers between devices  23.8 us (15%)
  local copies, waits for them, and re-layouts  2.57 us (2%)
    ppermute x19, waiting for transfers between devices, send(): return lax.ppermute(value, ('pipe', 'expert'), pairs)  107 us
    pallas_call x9, Pallas kernels, call(): pl.pallas_call(kernel, out_shape=out_shape, in_specs=more.pop('in_specs',...  29.2 us
    ppermute x19, starting transfers between devices, send(): return lax.ppermute(value, ('pipe', 'expert'), pairs)  23.8 us
  transfers between devices with their start and end apart: 19, of which 8 were waited for; matrix products, arithmetic and copies ran while one was open for 2% of the time, Pallas kernels for 17%

profile of v5, /device:TPU:0, one launch (start us, length us, event | category | flops | bytes accessed | tf_op | source)
XLA Modules:
  0.0 163.5 jit_solution(11842626925159086805)
XLA Ops:
  0.6 0.5 collective-permute-start.1
  1.2 0.1 collective-permute-start.2
  1.2 2.9 %collective-permute-start.5 = (bf16[64,3584]{1,0:T(8,128)(2,1)}, bf16[64,3584]{1,0:T(8,128)(2,1)S(1)}, u32[]{:S(2)}, u32[]{:S(2)}) collective-permute-start(bf16[64,3584]{1,0:T(8,128)(2,1)} %bitcast.32), channel_id=1, source_target_pairs={{0,16},{1,17},{2,18},{3,19},{4,20},{5,21},{6,22},{7,23},{8,24},{9,... | collective-permute-start | bytes 1376264 | tf_op jit(solution)/shard_map/ppermute | solution.py:261
  4.1 0.0 copy-start.1
  4.2 0.0 copy-start
  4.2 5.1 %build.1 = (bf16[120,3584]{1,0:T(8,128)(2,1)}, bf16[120,3584]{1,0:T(8,128)(2,1)}, bf16[120,3584]{1,0:T(8,128)(2,1)}, bf16[120,3584]{1,0:T(8,128)(2,1)}, bf16[64,4352]{1,0:T(8,128)(2,1)}) custom-call(s32[1]{0:T(128)} %bitcast.refs_0_, s32[2,64]{1,0:T(2,128)} %bitcast.36, f32[2,64]{1,0:T(2,128)} %bitcast.37, s32[2,64]{1,0:T(2,128)} %bitcast.38, ...), custom_call_target="tpu_custom_call" | custom-call | flops 99999997952 | bytes 104857 | tf_op jit(solution)/shard_map/build/pallas_call | solution.py:264
  9.3 0.1 collective-permute-start
  9.3 0.0 copy-done.1
  9.3 2.0 %collective-permute-start.7 = (bf16[3584,256]{1,0:T(8,128)(2,1)S(1)}, bf16[3584,256]{1,0:T(8,128)(2,1)S(1)}, u32[]{:S(2)}, u32[]{:S(2)}) collective-permute-start(bf16[3584,256]{1,0:T(8,128)(2,1)S(1)} %bitcast.26), channel_id=1, source_target_pairs={{0,2},{1,3},{2,0},{3,1},{4,6},{5,7},{6,4},{7,5},{8,10},{9,11},{10,... | collective-permute-start | bytes 5505032 | tf_op jit(solution)/shard_map/ppermute | solution.py:261
  11.4 0.0 collective-permute-done.1.up_c
  11.4 0.0 copy-done
  11.4 0.1 collective-permute-start.8
  11.5 0.0 collective-permute-done.2.refs_2_
  11.5 2.0 %collective-permute-start.3 = (bf16[120,3584]{1,0:T(8,128)(2,1)}, bf16[120,3584]{1,0:T(8,128)(2,1)S(1)}, u32[]{:S(2)}, u32[]{:S(2)}) collective-permute-start(bf16[120,3584]{1,0:T(8,128)(2,1)} %get-tuple-element.47), channel_id=1, source_target_pairs={{0,4},{1,5},{2,6},{3,7},{4,8},{5,9},{6,10},{7,11},{8,12},{9,13},{1... | collective-permute-start | bytes 2580488 | tf_op jit(solution)/shard_map/ppermute | solution.py:261
  13.5 1.2 fusion
  14.7 0.0 copy-start.3
  14.7 0.0 copy-start.2
  14.7 1.9 %stage.1 = (bf16[3584,256]{1,0:T(8,128)(2,1)S(1)}, bf16[256,3584]{1,0:T(8,128)(2,1)S(1)}, bf16[256,3584]{1,0:T(8,128)(2,1)S(1)}) custom-call(bf16[3584,256]{1,0:T(8,128)(2,1)S(1)} %bitcast.27, bf16[256,3584]{1,0:T(8,128)(2,1)S(1)} %bitcast.24, bf16[256,3584]{1,0:T(8,128)(2,1)} %collective-permute-done.2.refs_2_), custom_call_target="tpu_custom_call" | custom-call | flops 10000000 | bytes 104857 | tf_op jit(solution)/shard_map/stage/pallas_call | solution.py:264
  16.6 0.0 collective-permute-done.5.refs_1_
  16.6 0.0 copy-done.3
  16.6 2.7 %collective-permute-start.4 = (bf16[120,3584]{1,0:T(8,128)(2,1)S(1)}, bf16[120,3584]{1,0:T(8,128)(2,1)S(1)}, u32[]{:S(2)}, u32[]{:S(2)}) collective-permute-start(bf16[120,3584]{1,0:T(8,128)(2,1)S(1)} %copy-done.3), channel_id=1, source_target_pairs={{0,8},{1,9},{2,10},{3,11},{4,12},{5,13},{6,14},{7,15},{8,0},{9,1},... | collective-permute-start | bytes 2580488 | tf_op jit(solution)/shard_map/ppermute | solution.py:261
  19.3 16.5 %collective-permute-done.3 = bf16[120,3584]{1,0:T(8,128)(2,1)S(1)} collective-permute-done((bf16[120,3584]{1,0:T(8,128)(2,1)}, bf16[120,3584]{1,0:T(8,128)(2,1)S(1)}, u32[]{:S(2)}, u32[]{:S(2)}) %collective-permute-start.3) | collective-permute-done | bytes 860192 | tf_op jit(solution)/shard_map/ppermute | solution.py:261
  35.8 0.0 copy-done.2
  35.8 0.5 collective-permute-start.6
  36.4 0.1 fusion.1
  36.5 34.4 %collective-permute-done.4 = bf16[120,3584]{1,0:T(8,128)(2,1)S(1)} collective-permute-done((bf16[120,3584]{1,0:T(8,128)(2,1)S(1)}, bf16[120,3584]{1,0:T(8,128)(2,1)S(1)}, u32[]{:S(2)}, u32[]{:S(2)}) %collective-permute-start.4) | collective-permute-done | bytes 860192 | tf_op jit(solution)/shard_map/ppermute | solution.py:261
  70.9 0.1 fusion.2
  71.0 11.6 %collective-permute-done.6 = bf16[120,3584]{1,0:T(8,128)(2,1)S(1)} collective-permute-done((bf16[120,3584]{1,0:T(8,128)(2,1)S(1)}, bf16[120,3584]{1,0:T(8,128)(2,1)S(1)}, u32[]{:S(2)}, u32[]{:S(2)}) %collective-permute-start.6) | collective-permute-done | bytes 860192 | tf_op jit(solution)/shard_map/ppermute | solution.py:261
  82.6 0.1 fusion.3
  82.7 1.0 constant_dynamic-update-slice_fusion.3
  83.7 0.1 collective-permute-start.10
  83.8 0.0 collective-permute-done.refs_2_
  83.8 6.6 %collective-permute-done.8.down_y = bf16[256,3584]{1,0:T(8,128)(2,1)S(1)} collective-permute-done((bf16[256,3584]{1,0:T(8,128)(2,1)S(1)}, bf16[256,3584]{1,0:T(8,128)(2,1)S(1)}, u32[]{:S(2)}, u32[]{:S(2)}) %collective-permute-start.8) | collective-permute-done | bytes 1835040 | tf_op jit(solution)/shard_map/ppermute | solution.py:261
  90.4 0.0 collective-permute-start.12
  90.4 0.0 collective-permute-done.7.up_y
  90.5 0.5 collective-permute-start.11
  91.0 1.7 %collective-permute-start.9 = (bf16[320,3584]{1,0:T(8,128)(2,1)S(1)}, bf16[320,3584]{1,0:T(8,128)(2,1)S(1)}, u32[]{:S(2)}, u32[]{:S(2)}) collective-permute-start(bf16[320,3584]{1,0:T(8,128)(2,1)S(1)} %constant_dynamic-update-slice_fusion.xg_own), channel_id=1, source_target_pairs={{0,2},{1,3},{2,0},{3,1},{4,6},{5,7},{6,4},{7,5},{8,10},{9,11},{10,... | collective-permute-start | bytes 6881288 | tf_op jit(solution)/shard_map/ppermute | solution.py:261
  92.7 0.1 pad_maximum_fusion.2.rows_g.refs_2_
  92.8 0.2 pad_maximum_fusion
  93.0 2.4 %own.1 = (bf16[160,512]{1,0:T(8,128)(2,1)S(1)}, bf16[160,512]{1,0:T(8,128)(2,1)S(1)}) custom-call(bf16[160,3584]{1,0:T(8,128)(2,1)S(1)} %get-tuple-element.58.rows_f.refs_0_, bf16[160,3584]{1,0:T(8,128)(2,1)S(1)} %get-tuple-element.59.rows_x.refs_1_, bf16[160,3584]{1,0:T(8,128)(2,1)S(1)} %pad_maximum_fusion.2.rows_g.refs_2_, ...), custom_call_target="tpu_custom_call" | custom-call | flops 2000000000 | bytes 12582912 | tf_op jit(solution)/shard_map/own/pallas_call | solution.py:264
  95.4 4.0 %near.1 = (f32[160,3584]{1,0:T(8,128)S(1)}, f32[160,3584]{1,0:T(8,128)S(1)}) custom-call(bf16[160,3584]{1,0:T(8,128)(2,1)S(1)} %get-tuple-element.58.rows_f.refs_0_, bf16[160,3584]{1,0:T(8,128)(2,1)S(1)} %get-tuple-element.59.rows_x.refs_1_, bf16[160,3584]{1,0:T(8,128)(2,1)S(1)} %pad_maximum_fusion.2.rows_g.refs_2_, ...), custom_call_target="tpu_custom_call" | custom-call | flops 3000000000 | bytes 18874368 | tf_op jit(solution)/shard_map/near/pallas_call | solution.py:264
  99.4 0.0 collective-permute-done.10.xg_c
  99.4 0.0 collective-permute-done.12.refs_6_
  99.4 0.0 collective-permute-done.11.refs_5_
  99.4 2.4 %far.1 = (bf16[80,3584]{1,0:T(8,128)(2,1)S(1)}, bf16[80,3584]{1,0:T(8,128)(2,1)S(1)}, bf16[80,3584]{1,0:T(8,128)(2,1)S(1)}, bf16[80,3584]{1,0:T(8,128)(2,1)S(1)}) custom-call(bf16[160,3584]{1,0:T(8,128)(2,1)S(1)} %get-tuple-element.58.rows_f.refs_0_, bf16[160,3584]{1,0:T(8,128)(2,1)S(1)} %get-tuple-element.59.rows_x.refs_1_, ...), custom_call_target="tpu_custom_call" | custom-call | flops 2000000000 | bytes 10485760 | tf_op jit(solution)/shard_map/far/pallas_call | solution.py:264
  101.8 1.5 collective-permute-start.13
  103.4 3.6 %collective-permute-start.14 = (bf16[80,3584]{1,0:T(8,128)(2,1)S(1)}, bf16[80,3584]{1,0:T(8,128)(2,1)S(1)}, u32[]{:S(2)}, u32[]{:S(2)}) collective-permute-start(bf16[80,3584]{1,0:T(8,128)(2,1)S(1)} %get-tuple-element.68), channel_id=1, source_target_pairs={{0,28},{1,29},{2,30},{3,31},{4,16},{5,17},{6,18},{7,19},{8,20},{9,... | collective-permute-start | bytes 1720328 | tf_op jit(solution)/shard_map/ppermute | solution.py:261
  106.9 0.0 collective-permute-start.16
  107.0 2.0 %collective-permute-start.15 = (bf16[56,3584]{1,0:T(8,128)(2,1)S(1)}, bf16[56,3584]{1,0:T(8,128)(2,1)S(1)}, u32[]{:S(2)}, u32[]{:S(2)}) collective-permute-start(bf16[56,3584]{1,0:T(8,128)(2,1)S(1)} %slice.58), channel_id=1, source_target_pairs={{0,24},{1,25},{2,26},{3,27},{4,28},{5,29},{6,30},{7,31},{8,16},{9,... | collective-permute-start | bytes 1204232 | tf_op jit(solution)/shard_map/ppermute | solution.py:261
  108.9 4.5 %chip_grads.1 = (f32[3584,256]{1,0:T(8,128)S(1)}, f32[256,3584]{1,0:T(8,128)S(1)}) custom-call(bf16[320,3584]{1,0:T(8,128)(2,1)S(1)} %constant_dynamic-update-slice_fusion.xg_own, bf16[320,3584]{1,0:T(8,128)(2,1)S(1)} %collective-permute-done.10.xg_c, bf16[3584,256]{1,0:T(8,128)(2,1)S(1)} %get-tuple-element.50.own_up.up, ...), custom_call_target="tpu_custom_call" | custom-call | flops 2000000000 | bytes 10485760 | tf_op jit(solution)/shard_map/chip_grads/pallas_call | solution.py:264
  113.5 29.2 %collective-permute-done.9.xg_y = bf16[320,3584]{1,0:T(8,128)(2,1)S(1)} collective-permute-done((bf16[320,3584]{1,0:T(8,128)(2,1)S(1)}, bf16[320,3584]{1,0:T(8,128)(2,1)S(1)}, u32[]{:S(2)}, u32[]{:S(2)}) %collective-permute-start.9) | collective-permute-done | bytes 2293792 | tf_op jit(solution)/shard_map/ppermute | solution.py:261
  142.7 6.7 %collective-permute-done.15.refs_5_ = bf16[56,3584]{1,0:T(8,128)(2,1)S(1)} collective-permute-done((bf16[56,3584]{1,0:T(8,128)(2,1)S(1)}, bf16[56,3584]{1,0:T(8,128)(2,1)S(1)}, u32[]{:S(2)}, u32[]{:S(2)}) %collective-permute-start.15) | collective-permute-done | bytes 401440 | tf_op jit(solution)/shard_map/ppermute | solution.py:261
  149.4 0.2 collective-permute-done.13.refs_3_
  149.6 0.0 collective-permute-done.14.refs_4_
  149.7 0.0 collective-permute-done.16.refs_6_
  149.7 0.0 collective-permute-start.17
  149.7 3.6 %collective-permute-start.18 = (bf16[24,3584]{1,0:T(8,128)(2,1)S(1)}, bf16[24,3584]{1,0:T(8,128)(2,1)S(1)}, u32[]{:S(2)}, u32[]{:S(2)}) collective-permute-start(bf16[24,3584]{1,0:T(8,128)(2,1)S(1)} %slice.59), channel_id=1, source_target_pairs={{0,24},{1,25},{2,26},{3,27},{4,28},{5,29},{6,30},{7,31},{8,16},{9,... | collective-permute-start | bytes 516104 | tf_op jit(solution)/shard_map/ppermute | solution.py:261
  153.3 1.6 combine_first.1.refs_1_
  154.9 0.0 collective-permute-done.17.xg_d
  154.9 5.8 %grads.1 = (f32[3584,256]{1,0:T(8,128)}, f32[256,3584]{1,0:T(8,128)}) custom-call(bf16[320,3584]{1,0:T(8,128)(2,1)S(1)} %collective-permute-done.9.xg_y, bf16[320,3584]{1,0:T(8,128)(2,1)S(1)} %collective-permute-done.17.xg_d, bf16[3584,256]{1,0:T(8,128)(2,1)S(1)} %get-tuple-element.50.own_up.up, bf16[256,3584]{1,0:T(8,128)(2,1)S(1)} %get-tuple-element.55.own_down.down, ...), custom_call_target="tpu_custom_call" | custom-call | flops 10000000 | bytes 104857 | tf_op jit(solution)/shard_map/grads/pallas_call | solution.py:264
  160.7 1.3 collective-permute-done.18.refs_2_
  162.0 1.5 combine.1
  (6 shorter events, 0.1 us)
Async XLA Ops:
  0.6 10.7 %collective-permute-start.1 = (bf16[3584,256]{1,0:T(8,128)(2,1)}, bf16[3584,256]{1,0:T(8,128)(2,1)S(1)}, u32[]{:S(2)}, u32[]{:S(2)}) collective-permute-start(bf16[3584,256]{1,0:T(8,128)(2,1)} %bitcast.25), channel_id=1, source_target_pairs={{0,1},{1,0},{2,3},{3,2},{4,5},{5,4},{6,7},{7,6},{8,9},{9,8},{10,11... | collective-permute-start | bytes 5505032 | tf_op jit(solution)/shard_map/ppermute | solution.py:261
  1.2 10.3 %collective-permute-start.2 = (bf16[256,3584]{1,0:T(8,128)(2,1)}, bf16[256,3584]{1,0:T(8,128)(2,1)}, u32[]{:S(2)}, u32[]{:S(2)}) collective-permute-start(bf16[256,3584]{1,0:T(8,128)(2,1)} %bitcast.22), channel_id=1, source_target_pairs={{0,1},{1,0},{2,3},{3,2},{4,5},{5,4},{6,7},{7,6},{8,9},{9,8},{10,11... | collective-permute-start | bytes 5505032 | tf_op jit(solution)/shard_map/ppermute | solution.py:261
  1.2 15.4 %collective-permute-start.5 = (bf16[64,3584]{1,0:T(8,128)(2,1)}, bf16[64,3584]{1,0:T(8,128)(2,1)S(1)}, u32[]{:S(2)}, u32[]{:S(2)}) collective-permute-start(bf16[64,3584]{1,0:T(8,128)(2,1)} %bitcast.32), channel_id=1, source_target_pairs={{0,16},{1,17},{2,18},{3,19},{4,20},{5,21},{6,22},{7,23},{8,24},{9,... | collective-permute-start | bytes 1376264 | tf_op jit(solution)/shard_map/ppermute | solution.py:261
  4.1 5.2 %copy-start.1 = (bf16[1,1,3584,256]{3,2,1,0:T(8,128)(2,1)S(1)}, bf16[1,1,3584,256]{3,2,1,0:T(8,128)(2,1)}, u32[]{:S(2)}) copy-start(bf16[1,1,3584,256]{3,2,1,0:T(8,128)(2,1)} %param.16) | copy-start | bytes 5505028
  4.2 7.2 %copy-start = (bf16[1,1,256,3584]{3,2,1,0:T(8,128)(2,1)S(1)}, bf16[1,1,256,3584]{3,2,1,0:T(8,128)(2,1)}, u32[]{:S(2)}) copy-start(bf16[1,1,256,3584]{3,2,1,0:T(8,128)(2,1)} %param.17) | copy-start | bytes 5505028
  9.3 74.6 %collective-permute-start = (bf16[64,4352]{1,0:T(8,128)(2,1)}, bf16[64,4352]{1,0:T(8,128)(2,1)S(1)}, u32[]{:S(2)}, u32[]{:S(2)}) collective-permute-start(bf16[64,4352]{1,0:T(8,128)(2,1)} %get-tuple-element.42), channel_id=1, source_target_pairs={{0,16},{1,17},{2,18},{3,19},{4,20},{5,21},{6,22},{7,23},{8,24},{9,... | collective-permute-start | bytes 1671176 | tf_op jit(solution)/shard_map/ppermute | solution.py:261
  9.3 81.1 %collective-permute-start.7 = (bf16[3584,256]{1,0:T(8,128)(2,1)S(1)}, bf16[3584,256]{1,0:T(8,128)(2,1)S(1)}, u32[]{:S(2)}, u32[]{:S(2)}) collective-permute-start(bf16[3584,256]{1,0:T(8,128)(2,1)S(1)} %bitcast.26), channel_id=1, source_target_pairs={{0,2},{1,3},{2,0},{3,1},{4,6},{5,7},{6,4},{7,5},{8,10},{9,11},{10,... | collective-permute-start | bytes 5505032 | tf_op jit(solution)/shard_map/ppermute | solution.py:261
  11.4 79.1 %collective-permute-start.8 = (bf16[256,3584]{1,0:T(8,128)(2,1)S(1)}, bf16[256,3584]{1,0:T(8,128)(2,1)S(1)}, u32[]{:S(2)}, u32[]{:S(2)}) collective-permute-start(bf16[256,3584]{1,0:T(8,128)(2,1)S(1)} %bitcast.23), channel_id=1, source_target_pairs={{0,2},{1,3},{2,0},{3,1},{4,6},{5,7},{6,4},{7,5},{8,10},{9,11},{10,... | collective-permute-start | bytes 5505032 | tf_op jit(solution)/shard_map/ppermute | solution.py:261
  11.5 24.4 %collective-permute-start.3 = (bf16[120,3584]{1,0:T(8,128)(2,1)}, bf16[120,3584]{1,0:T(8,128)(2,1)S(1)}, u32[]{:S(2)}, u32[]{:S(2)}) collective-permute-start(bf16[120,3584]{1,0:T(8,128)(2,1)} %get-tuple-element.47), channel_id=1, source_target_pairs={{0,4},{1,5},{2,6},{3,7},{4,8},{5,9},{6,10},{7,11},{8,12},{9,13},{1... | collective-permute-start | bytes 2580488 | tf_op jit(solution)/shard_map/ppermute | solution.py:261
  14.7 1.9 %copy-start.3 = (bf16[120,3584]{1,0:T(8,128)(2,1)S(1)}, bf16[120,3584]{1,0:T(8,128)(2,1)}, u32[]{:S(2)}) copy-start(bf16[120,3584]{1,0:T(8,128)(2,1)} %get-tuple-element.48) | copy-start | bytes 2580484
  14.7 21.2 %copy-start.2 = (bf16[120,3584]{1,0:T(8,128)(2,1)S(1)}, bf16[120,3584]{1,0:T(8,128)(2,1)}, u32[]{:S(2)}) copy-start(bf16[120,3584]{1,0:T(8,128)(2,1)} %get-tuple-element.51) | copy-start | bytes 2580484
  16.6 54.3 %collective-permute-start.4 = (bf16[120,3584]{1,0:T(8,128)(2,1)S(1)}, bf16[120,3584]{1,0:T(8,128)(2,1)S(1)}, u32[]{:S(2)}, u32[]{:S(2)}) collective-permute-start(bf16[120,3584]{1,0:T(8,128)(2,1)S(1)} %copy-done.3), channel_id=1, source_target_pairs={{0,8},{1,9},{2,10},{3,11},{4,12},{5,13},{6,14},{7,15},{8,0},{9,1},... | collective-permute-start | bytes 2580488 | tf_op jit(solution)/shard_map/ppermute | solution.py:261
  35.8 46.7 %collective-permute-start.6 = (bf16[120,3584]{1,0:T(8,128)(2,1)S(1)}, bf16[120,3584]{1,0:T(8,128)(2,1)S(1)}, u32[]{:S(2)}, u32[]{:S(2)}) collective-permute-start(bf16[120,3584]{1,0:T(8,128)(2,1)S(1)} %copy-done.2), channel_id=1, source_target_pairs={{0,12},{1,13},{2,14},{3,15},{4,0},{5,1},{6,2},{7,3},{8,4},{9,5},{1... | collective-permute-start | bytes 2580488 | tf_op jit(solution)/shard_map/ppermute | solution.py:261
  83.7 15.6 %collective-permute-start.10 = (bf16[320,3584]{1,0:T(8,128)(2,1)S(1)}, bf16[320,3584]{1,0:T(8,128)(2,1)S(1)}, u32[]{:S(2)}, u32[]{:S(2)}) collective-permute-start(bf16[320,3584]{1,0:T(8,128)(2,1)S(1)} %constant_dynamic-update-slice_fusion.xg_own), channel_id=1, source_target_pairs={{0,1},{1,0},{2,3},{3,2},{4,5},{5,4},{6,7},{7,6},{8,9},{9,8},{10,11... | collective-permute-start | bytes 6881288 | tf_op jit(solution)/shard_map/ppermute | solution.py:261
  90.4 8.9 %collective-permute-start.12 = (bf16[256,3584]{1,0:T(8,128)(2,1)S(1)}, bf16[256,3584]{1,0:T(8,128)(2,1)S(1)}, u32[]{:S(2)}, u32[]{:S(2)}) collective-permute-start(bf16[256,3584]{1,0:T(8,128)(2,1)S(1)} %collective-permute-done.8.down_y), channel_id=1, source_target_pairs={{0,1},{1,0},{2,3},{3,2},{4,5},{5,4},{6,7},{7,6},{8,9},{9,8},{10,11... | collective-permute-start | bytes 5505032 | tf_op jit(solution)/shard_map/ppermute | solution.py:261
  90.5 8.9 %collective-permute-start.11 = (bf16[3584,256]{1,0:T(8,128)(2,1)S(1)}, bf16[3584,256]{1,0:T(8,128)(2,1)S(1)}, u32[]{:S(2)}, u32[]{:S(2)}) collective-permute-start(bf16[3584,256]{1,0:T(8,128)(2,1)S(1)} %collective-permute-done.7.up_y), channel_id=1, source_target_pairs={{0,1},{1,0},{2,3},{3,2},{4,5},{5,4},{6,7},{7,6},{8,9},{9,8},{10,11... | collective-permute-start | bytes 5505032 | tf_op jit(solution)/shard_map/ppermute | solution.py:261
  91.0 51.8 %collective-permute-start.9 = (bf16[320,3584]{1,0:T(8,128)(2,1)S(1)}, bf16[320,3584]{1,0:T(8,128)(2,1)S(1)}, u32[]{:S(2)}, u32[]{:S(2)}) collective-permute-start(bf16[320,3584]{1,0:T(8,128)(2,1)S(1)} %constant_dynamic-update-slice_fusion.xg_own), channel_id=1, source_target_pairs={{0,2},{1,3},{2,0},{3,1},{4,6},{5,7},{6,4},{7,5},{8,10},{9,11},{10,... | collective-permute-start | bytes 6881288 | tf_op jit(solution)/shard_map/ppermute | solution.py:261
  101.8 47.8 %collective-permute-start.13 = (bf16[80,3584]{1,0:T(8,128)(2,1)S(1)}, bf16[80,3584]{1,0:T(8,128)(2,1)S(1)}, u32[]{:S(2)}, u32[]{:S(2)}) collective-permute-start(bf16[80,3584]{1,0:T(8,128)(2,1)S(1)} %get-tuple-element.67), channel_id=1, source_target_pairs={{0,16},{1,17},{2,18},{3,19},{4,20},{5,21},{6,22},{7,23},{8,24},{9,... | collective-permute-start | bytes 1720328 | tf_op jit(solution)/shard_map/ppermute | solution.py:261
  103.4 46.3 %collective-permute-start.14 = (bf16[80,3584]{1,0:T(8,128)(2,1)S(1)}, bf16[80,3584]{1,0:T(8,128)(2,1)S(1)}, u32[]{:S(2)}, u32[]{:S(2)}) collective-permute-start(bf16[80,3584]{1,0:T(8,128)(2,1)S(1)} %get-tuple-element.68), channel_id=1, source_target_pairs={{0,28},{1,29},{2,30},{3,31},{4,16},{5,17},{6,18},{7,19},{8,20},{9,... | collective-permute-start | bytes 1720328 | tf_op jit(solution)/shard_map/ppermute | solution.py:261
  106.9 42.7 %collective-permute-start.16 = (bf16[80,3584]{1,0:T(8,128)(2,1)S(1)}, bf16[80,3584]{1,0:T(8,128)(2,1)S(1)}, u32[]{:S(2)}, u32[]{:S(2)}) collective-permute-start(bf16[80,3584]{1,0:T(8,128)(2,1)S(1)} %get-tuple-element.70), channel_id=1, source_target_pairs={{0,20},{1,21},{2,22},{3,23},{4,24},{5,25},{6,26},{7,27},{8,28},{9,... | collective-permute-start | bytes 1720328 | tf_op jit(solution)/shard_map/ppermute | solution.py:261
  107.0 42.5 %collective-permute-start.15 = (bf16[56,3584]{1,0:T(8,128)(2,1)S(1)}, bf16[56,3584]{1,0:T(8,128)(2,1)S(1)}, u32[]{:S(2)}, u32[]{:S(2)}) collective-permute-start(bf16[56,3584]{1,0:T(8,128)(2,1)S(1)} %slice.58), channel_id=1, source_target_pairs={{0,24},{1,25},{2,26},{3,27},{4,28},{5,29},{6,30},{7,31},{8,16},{9,... | collective-permute-start | bytes 1204232 | tf_op jit(solution)/shard_map/ppermute | solution.py:261
  149.7 5.3 %collective-permute-start.17 = (bf16[320,3584]{1,0:T(8,128)(2,1)S(1)}, bf16[320,3584]{1,0:T(8,128)(2,1)S(1)}, u32[]{:S(2)}, u32[]{:S(2)}) collective-permute-start(bf16[320,3584]{1,0:T(8,128)(2,1)S(1)} %collective-permute-done.9.xg_y), channel_id=1, source_target_pairs={{0,1},{1,0},{2,3},{3,2},{4,5},{5,4},{6,7},{7,6},{8,9},{9,8},{10,11... | collective-permute-start | bytes 6881288 | tf_op jit(solution)/shard_map/ppermute | solution.py:261
  149.7 12.3 %collective-permute-start.18 = (bf16[24,3584]{1,0:T(8,128)(2,1)S(1)}, bf16[24,3584]{1,0:T(8,128)(2,1)S(1)}, u32[]{:S(2)}, u32[]{:S(2)}) collective-permute-start(bf16[24,3584]{1,0:T(8,128)(2,1)S(1)} %slice.59), channel_id=1, source_target_pairs={{0,24},{1,25},{2,26},{3,27},{4,28},{5,29},{6,30},{7,31},{8,16},{9,... | collective-permute-start | bytes 516104 | tf_op jit(solution)/shard_map/ppermute | solution.py:261

commit v6 on v5

--- a/solution.py
+++ b/solution.py
@@ -339,16 +339,16 @@
         cost(2, 10),
     )
 
-    middle = experts // 2
-    split = 7 * each // 10 // 8 * 8
+    shift = 1
+    split = 4 * each // 10 // 8 * 8
     ways = range(len(outs))
 
     def back(value, i):
         return send(value, planes=-(i % experts), pipes=1 if i < experts else -1)
 
-    ret = [back(outs[i][:split] if i % experts == middle else outs[i], i) for i in ways]
-    ret_late = after([outs[i][split:] for i in ways if i % experts == middle], *ret)
-    ret_late = [back(part, i * experts + middle) for i, part in enumerate(ret_late)]
+    ret = [back(outs[i][:split] if i % experts == shift else outs[i], i) for i in ways]
+    ret_late = after([outs[i][split:] for i in ways if i % experts == shift], *ret)
+    ret_late = [back(part, i * experts + shift) for i, part in enumerate(ret_late)]
 
     xg_y = send(*after([rows_xg], up_y, down_y), flip=2)
     chip_up, chip_down = call(
@@ -390,7 +390,7 @@
     results = []
     for i, (table, total) in enumerate(zip(tables, totals)):
         results += call(
-            lambda *refs: combine_kernel(experts, each, middle * each + split, *refs),
+            lambda *refs: combine_kernel(experts, each, shift * each + split, *refs),
             "combine",
             [shape(tok_rows, width)] * len(bases[i]),
             (table, total, ret_late[i]),

time: 164 us -> 161 us (0.982)
  waiting for transfers between devices: 107 us -> 100 us
  starting transfers between devices: 23.8 us -> 26.8 us
    ppermute x19, waiting for transfers between devices: 107 us -> 100 us  [send(): return lax.ppermute(value, ('pipe', 'expert'), pairs)]
    ppermute x19, starting transfers between devices: 23.8 us -> 26.8 us  [send(): return lax.ppermute(value, ('pipe', 'expert'), pairs)]
  transfers between devices with their start and end apart: 19 -> 19, of which waited for: 8 -> 7; matrix products, arithmetic and copies ran while one was open for 2% -> 2% of each run, Pallas kernels for 17% -> 17%
where the time goes in v6:
time: 161 us; the launch traced here: 160 us
  waiting for transfers between devices  100 us (62%)
  Pallas kernels  29.2 us (18%)
  starting transfers between devices  26.8 us (17%)
  local copies, waits for them, and re-layouts  2.57 us (2%)
    ppermute x19, waiting for transfers between devices, send(): return lax.ppermute(value, ('pipe', 'expert'), pairs)  100 us
    pallas_call x9, Pallas kernels, call(): pl.pallas_call(kernel, out_shape=out_shape, in_specs=more.pop('in_specs',...  29.2 us
    ppermute x19, starting transfers between devices, send(): return lax.ppermute(value, ('pipe', 'expert'), pairs)  26.8 us
  transfers between devices with their start and end apart: 19, of which 7 were waited for; matrix products, arithmetic and copies ran while one was open for 2% of the time, Pallas kernels for 17%

profile of v6, /device:TPU:0, one launch (start us, length us, event | category | flops | bytes accessed | tf_op | source)
XLA Modules:
  0.0 160.1 jit_solution(368808206920404678)
XLA Ops:
  0.6 0.5 collective-permute-start.1
  1.2 0.1 collective-permute-start.2
  1.2 2.9 %collective-permute-start.5 = (bf16[64,3584]{1,0:T(8,128)(2,1)}, bf16[64,3584]{1,0:T(8,128)(2,1)S(1)}, u32[]{:S(2)}, u32[]{:S(2)}) collective-permute-start(bf16[64,3584]{1,0:T(8,128)(2,1)} %bitcast.32), channel_id=1, source_target_pairs={{0,16},{1,17},{2,18},{3,19},{4,20},{5,21},{6,22},{7,23},{8,24},{9,... | collective-permute-start | bytes 1376264 | tf_op jit(solution)/shard_map/ppermute | solution.py:261
  4.1 0.0 copy-start.1
  4.2 0.0 copy-start
  4.2 5.1 %build.1 = (bf16[120,3584]{1,0:T(8,128)(2,1)}, bf16[120,3584]{1,0:T(8,128)(2,1)}, bf16[120,3584]{1,0:T(8,128)(2,1)}, bf16[120,3584]{1,0:T(8,128)(2,1)}, bf16[64,4352]{1,0:T(8,128)(2,1)}) custom-call(s32[1]{0:T(128)} %bitcast.refs_0_, s32[2,64]{1,0:T(2,128)} %bitcast.36, f32[2,64]{1,0:T(2,128)} %bitcast.37, s32[2,64]{1,0:T(2,128)} %bitcast.38, ...), custom_call_target="tpu_custom_call" | custom-call | flops 99999997952 | bytes 104857 | tf_op jit(solution)/shard_map/build/pallas_call | solution.py:264
  9.3 0.1 collective-permute-start
  9.3 0.0 copy-done.1
  9.3 2.0 %collective-permute-start.7 = (bf16[3584,256]{1,0:T(8,128)(2,1)S(1)}, bf16[3584,256]{1,0:T(8,128)(2,1)S(1)}, u32[]{:S(2)}, u32[]{:S(2)}) collective-permute-start(bf16[3584,256]{1,0:T(8,128)(2,1)S(1)} %bitcast.26), channel_id=1, source_target_pairs={{0,2},{1,3},{2,0},{3,1},{4,6},{5,7},{6,4},{7,5},{8,10},{9,11},{10,... | collective-permute-start | bytes 5505032 | tf_op jit(solution)/shard_map/ppermute | solution.py:261
  11.4 0.0 collective-permute-done.1.up_c
  11.4 0.0 copy-done
  11.4 0.1 collective-permute-start.8
  11.5 0.0 collective-permute-done.2.refs_2_
  11.5 2.0 %collective-permute-start.3 = (bf16[120,3584]{1,0:T(8,128)(2,1)}, bf16[120,3584]{1,0:T(8,128)(2,1)S(1)}, u32[]{:S(2)}, u32[]{:S(2)}) collective-permute-start(bf16[120,3584]{1,0:T(8,128)(2,1)} %get-tuple-element.47), channel_id=1, source_target_pairs={{0,4},{1,5},{2,6},{3,7},{4,8},{5,9},{6,10},{7,11},{8,12},{9,13},{1... | collective-permute-start | bytes 2580488 | tf_op jit(solution)/shard_map/ppermute | solution.py:261
  13.5 1.2 fusion
  14.7 0.0 copy-start.3
  14.7 0.0 copy-start.2
  14.7 1.9 %stage.1 = (bf16[3584,256]{1,0:T(8,128)(2,1)S(1)}, bf16[256,3584]{1,0:T(8,128)(2,1)S(1)}, bf16[256,3584]{1,0:T(8,128)(2,1)S(1)}) custom-call(bf16[3584,256]{1,0:T(8,128)(2,1)S(1)} %bitcast.27, bf16[256,3584]{1,0:T(8,128)(2,1)S(1)} %bitcast.24, bf16[256,3584]{1,0:T(8,128)(2,1)} %collective-permute-done.2.refs_2_), custom_call_target="tpu_custom_call" | custom-call | flops 10000000 | bytes 104857 | tf_op jit(solution)/shard_map/stage/pallas_call | solution.py:264
  16.6 0.0 collective-permute-done.5.refs_1_
  16.6 0.0 copy-done.3
  16.6 2.7 %collective-permute-start.4 = (bf16[120,3584]{1,0:T(8,128)(2,1)S(1)}, bf16[120,3584]{1,0:T(8,128)(2,1)S(1)}, u32[]{:S(2)}, u32[]{:S(2)}) collective-permute-start(bf16[120,3584]{1,0:T(8,128)(2,1)S(1)} %copy-done.3), channel_id=1, source_target_pairs={{0,8},{1,9},{2,10},{3,11},{4,12},{5,13},{6,14},{7,15},{8,0},{9,1},... | collective-permute-start | bytes 2580488 | tf_op jit(solution)/shard_map/ppermute | solution.py:261
  19.3 16.5 %collective-permute-done.3 = bf16[120,3584]{1,0:T(8,128)(2,1)S(1)} collective-permute-done((bf16[120,3584]{1,0:T(8,128)(2,1)}, bf16[120,3584]{1,0:T(8,128)(2,1)S(1)}, u32[]{:S(2)}, u32[]{:S(2)}) %collective-permute-start.3) | collective-permute-done | bytes 860192 | tf_op jit(solution)/shard_map/ppermute | solution.py:261
  35.8 0.0 copy-done.2
  35.8 0.5 collective-permute-start.6
  36.4 0.1 fusion.1
  36.5 34.4 %collective-permute-done.4 = bf16[120,3584]{1,0:T(8,128)(2,1)S(1)} collective-permute-done((bf16[120,3584]{1,0:T(8,128)(2,1)S(1)}, bf16[120,3584]{1,0:T(8,128)(2,1)S(1)}, u32[]{:S(2)}, u32[]{:S(2)}) %collective-permute-start.4) | collective-permute-done | bytes 860192 | tf_op jit(solution)/shard_map/ppermute | solution.py:261
  70.9 0.1 fusion.2
  71.0 11.6 %collective-permute-done.6 = bf16[120,3584]{1,0:T(8,128)(2,1)S(1)} collective-permute-done((bf16[120,3584]{1,0:T(8,128)(2,1)S(1)}, bf16[120,3584]{1,0:T(8,128)(2,1)S(1)}, u32[]{:S(2)}, u32[]{:S(2)}) %collective-permute-start.6) | collective-permute-done | bytes 860192 | tf_op jit(solution)/shard_map/ppermute | solution.py:261
  82.6 0.1 fusion.3
  82.7 1.0 constant_dynamic-update-slice_fusion.3
  83.7 0.1 collective-permute-start.10
  83.8 0.0 collective-permute-done.refs_2_
  83.8 6.6 %collective-permute-done.8.down_y = bf16[256,3584]{1,0:T(8,128)(2,1)S(1)} collective-permute-done((bf16[256,3584]{1,0:T(8,128)(2,1)S(1)}, bf16[256,3584]{1,0:T(8,128)(2,1)S(1)}, u32[]{:S(2)}, u32[]{:S(2)}) %collective-permute-start.8) | collective-permute-done | bytes 1835040 | tf_op jit(solution)/shard_map/ppermute | solution.py:261
  90.4 0.0 collective-permute-start.12
  90.4 0.0 collective-permute-done.7.up_y
  90.5 0.5 collective-permute-start.11
  91.0 1.7 %collective-permute-start.9 = (bf16[320,3584]{1,0:T(8,128)(2,1)S(1)}, bf16[320,3584]{1,0:T(8,128)(2,1)S(1)}, u32[]{:S(2)}, u32[]{:S(2)}) collective-permute-start(bf16[320,3584]{1,0:T(8,128)(2,1)S(1)} %constant_dynamic-update-slice_fusion.xg_own), channel_id=1, source_target_pairs={{0,2},{1,3},{2,0},{3,1},{4,6},{5,7},{6,4},{7,5},{8,10},{9,11},{10,... | collective-permute-start | bytes 6881288 | tf_op jit(solution)/shard_map/ppermute | solution.py:261
  92.7 0.1 pad_maximum_fusion.2.rows_g.refs_2_
  92.8 0.2 pad_maximum_fusion
  93.0 2.4 %own.1 = (bf16[160,512]{1,0:T(8,128)(2,1)S(1)}, bf16[160,512]{1,0:T(8,128)(2,1)S(1)}) custom-call(bf16[160,3584]{1,0:T(8,128)(2,1)S(1)} %get-tuple-element.58.rows_f.refs_0_, bf16[160,3584]{1,0:T(8,128)(2,1)S(1)} %get-tuple-element.59.rows_x.refs_1_, bf16[160,3584]{1,0:T(8,128)(2,1)S(1)} %pad_maximum_fusion.2.rows_g.refs_2_, ...), custom_call_target="tpu_custom_call" | custom-call | flops 2000000000 | bytes 12582912 | tf_op jit(solution)/shard_map/own/pallas_call | solution.py:264
  95.4 4.0 %near.1 = (f32[160,3584]{1,0:T(8,128)S(1)}, f32[160,3584]{1,0:T(8,128)S(1)}) custom-call(bf16[160,3584]{1,0:T(8,128)(2,1)S(1)} %get-tuple-element.58.rows_f.refs_0_, bf16[160,3584]{1,0:T(8,128)(2,1)S(1)} %get-tuple-element.59.rows_x.refs_1_, bf16[160,3584]{1,0:T(8,128)(2,1)S(1)} %pad_maximum_fusion.2.rows_g.refs_2_, ...), custom_call_target="tpu_custom_call" | custom-call | flops 3000000000 | bytes 18874368 | tf_op jit(solution)/shard_map/near/pallas_call | solution.py:264
  99.4 0.0 collective-permute-done.10.xg_c
  99.4 0.0 collective-permute-done.12.refs_6_
  99.4 0.0 collective-permute-done.11.refs_5_
  99.4 2.4 %far.1 = (bf16[80,3584]{1,0:T(8,128)(2,1)S(1)}, bf16[80,3584]{1,0:T(8,128)(2,1)S(1)}, bf16[80,3584]{1,0:T(8,128)(2,1)S(1)}, bf16[80,3584]{1,0:T(8,128)(2,1)S(1)}) custom-call(bf16[160,3584]{1,0:T(8,128)(2,1)S(1)} %get-tuple-element.58.rows_f.refs_0_, bf16[160,3584]{1,0:T(8,128)(2,1)S(1)} %get-tuple-element.59.rows_x.refs_1_, ...), custom_call_target="tpu_custom_call" | custom-call | flops 2000000000 | bytes 10485760 | tf_op jit(solution)/shard_map/far/pallas_call | solution.py:264
  101.8 1.5 collective-permute-start.13
  103.4 2.5 %collective-permute-start.15 = (bf16[80,3584]{1,0:T(8,128)(2,1)S(1)}, bf16[80,3584]{1,0:T(8,128)(2,1)S(1)}, u32[]{:S(2)}, u32[]{:S(2)}) collective-permute-start(bf16[80,3584]{1,0:T(8,128)(2,1)S(1)} %get-tuple-element.69), channel_id=1, source_target_pairs={{0,24},{1,25},{2,26},{3,27},{4,28},{5,29},{6,30},{7,31},{8,16},{9,... | collective-permute-start | bytes 1720328 | tf_op jit(solution)/shard_map/ppermute | solution.py:261
  105.9 2.5 %collective-permute-start.16 = (bf16[80,3584]{1,0:T(8,128)(2,1)S(1)}, bf16[80,3584]{1,0:T(8,128)(2,1)S(1)}, u32[]{:S(2)}, u32[]{:S(2)}) collective-permute-start(bf16[80,3584]{1,0:T(8,128)(2,1)S(1)} %get-tuple-element.70), channel_id=1, source_target_pairs={{0,20},{1,21},{2,22},{3,23},{4,24},{5,25},{6,26},{7,27},{8,28},{9,... | collective-permute-start | bytes 1720328 | tf_op jit(solution)/shard_map/ppermute | solution.py:261
  108.5 2.4 %collective-permute-start.14 = (bf16[32,3584]{1,0:T(8,128)(2,1)S(1)}, bf16[32,3584]{1,0:T(8,128)(2,1)S(1)}, u32[]{:S(2)}, u32[]{:S(2)}) collective-permute-start(bf16[32,3584]{1,0:T(8,128)(2,1)S(1)} %slice.58), channel_id=1, source_target_pairs={{0,28},{1,29},{2,30},{3,31},{4,16},{5,17},{6,18},{7,19},{8,20},{9,... | collective-permute-start | bytes 688136 | tf_op jit(solution)/shard_map/ppermute | solution.py:261
  110.9 4.5 %chip_grads.1 = (f32[3584,256]{1,0:T(8,128)S(1)}, f32[256,3584]{1,0:T(8,128)S(1)}) custom-call(bf16[320,3584]{1,0:T(8,128)(2,1)S(1)} %constant_dynamic-update-slice_fusion.xg_own, bf16[320,3584]{1,0:T(8,128)(2,1)S(1)} %collective-permute-done.10.xg_c, bf16[3584,256]{1,0:T(8,128)(2,1)S(1)} %get-tuple-element.50.own_up.up, ...), custom_call_target="tpu_custom_call" | custom-call | flops 2000000000 | bytes 10485760 | tf_op jit(solution)/shard_map/chip_grads/pallas_call | solution.py:264
  115.4 27.3 %collective-permute-done.9.xg_y = bf16[320,3584]{1,0:T(8,128)(2,1)S(1)} collective-permute-done((bf16[320,3584]{1,0:T(8,128)(2,1)S(1)}, bf16[320,3584]{1,0:T(8,128)(2,1)S(1)}, u32[]{:S(2)}, u32[]{:S(2)}) %collective-permute-start.9) | collective-permute-done | bytes 2293792 | tf_op jit(solution)/shard_map/ppermute | solution.py:261
  142.7 0.0 collective-permute-done.14.refs_4_
  142.7 3.2 %collective-permute-done.13.refs_3_ = bf16[80,3584]{1,0:T(8,128)(2,1)S(1)} collective-permute-done((bf16[80,3584]{1,0:T(8,128)(2,1)S(1)}, bf16[80,3584]{1,0:T(8,128)(2,1)S(1)}, u32[]{:S(2)}, u32[]{:S(2)}) %collective-permute-start.13) | collective-permute-done | bytes 573472 | tf_op jit(solution)/shard_map/ppermute | solution.py:261
  146.0 0.0 collective-permute-done.15.refs_5_
  146.0 0.0 collective-permute-done.16.refs_6_
  146.0 0.0 collective-permute-start.17
  146.0 4.6 %collective-permute-start.18 = (bf16[48,3584]{1,0:T(8,128)(2,1)S(1)}, bf16[48,3584]{1,0:T(8,128)(2,1)S(1)}, u32[]{:S(2)}, u32[]{:S(2)}) collective-permute-start(bf16[48,3584]{1,0:T(8,128)(2,1)S(1)} %slice.59), channel_id=1, source_target_pairs={{0,28},{1,29},{2,30},{3,31},{4,16},{5,17},{6,18},{7,19},{8,20},{9,... | collective-permute-start | bytes 1032200 | tf_op jit(solution)/shard_map/ppermute | solution.py:261
  150.6 1.6 %combine_first.1.refs_1_ = f32[128,3584]{1,0:T(8,128)S(1)} custom-call(bf16[64,768]{1,0:T(8,128)(2,1)S(1)} %slice.60.refs_0_, bf16[64,3584]{1,0:T(8,128)(2,1)S(1)} %collective-permute-done.5.refs_1_, bf16[64,4352]{1,0:T(8,128)(2,1)S(1)} %collective-permute-done.refs_2_, bf16[80,3584]{1,0:T(8,128)(2,1)S(1)} %collective-permute-done.13.refs_3_, ...), custom_call_target="tpu_custom_call" | custom-call | flops 200000000 | bytes 4194304 | tf_op jit(solution)/shard_map/combine_first/pallas_call | solution.py:264
  152.2 0.0 collective-permute-done.17.xg_d
  152.2 5.8 %grads.1 = (f32[3584,256]{1,0:T(8,128)}, f32[256,3584]{1,0:T(8,128)}) custom-call(bf16[320,3584]{1,0:T(8,128)(2,1)S(1)} %collective-permute-done.9.xg_y, bf16[320,3584]{1,0:T(8,128)(2,1)S(1)} %collective-permute-done.17.xg_d, bf16[3584,256]{1,0:T(8,128)(2,1)S(1)} %get-tuple-element.50.own_up.up, bf16[256,3584]{1,0:T(8,128)(2,1)S(1)} %get-tuple-element.55.own_down.down, ...), custom_call_target="tpu_custom_call" | custom-call | flops 10000000 | bytes 104857 | tf_op jit(solution)/shard_map/grads/pallas_call | solution.py:264
  158.1 0.5 collective-permute-done.18.refs_2_
  158.6 1.5 combine.1
  (6 shorter events, 0.1 us)
Async XLA Ops:
  0.6 10.7 %collective-permute-start.1 = (bf16[3584,256]{1,0:T(8,128)(2,1)}, bf16[3584,256]{1,0:T(8,128)(2,1)S(1)}, u32[]{:S(2)}, u32[]{:S(2)}) collective-permute-start(bf16[3584,256]{1,0:T(8,128)(2,1)} %bitcast.25), channel_id=1, source_target_pairs={{0,1},{1,0},{2,3},{3,2},{4,5},{5,4},{6,7},{7,6},{8,9},{9,8},{10,11... | collective-permute-start | bytes 5505032 | tf_op jit(solution)/shard_map/ppermute | solution.py:261
  1.2 10.3 %collective-permute-start.2 = (bf16[256,3584]{1,0:T(8,128)(2,1)}, bf16[256,3584]{1,0:T(8,128)(2,1)}, u32[]{:S(2)}, u32[]{:S(2)}) collective-permute-start(bf16[256,3584]{1,0:T(8,128)(2,1)} %bitcast.22), channel_id=1, source_target_pairs={{0,1},{1,0},{2,3},{3,2},{4,5},{5,4},{6,7},{7,6},{8,9},{9,8},{10,11... | collective-permute-start | bytes 5505032 | tf_op jit(solution)/shard_map/ppermute | solution.py:261
  1.2 15.4 %collective-permute-start.5 = (bf16[64,3584]{1,0:T(8,128)(2,1)}, bf16[64,3584]{1,0:T(8,128)(2,1)S(1)}, u32[]{:S(2)}, u32[]{:S(2)}) collective-permute-start(bf16[64,3584]{1,0:T(8,128)(2,1)} %bitcast.32), channel_id=1, source_target_pairs={{0,16},{1,17},{2,18},{3,19},{4,20},{5,21},{6,22},{7,23},{8,24},{9,... | collective-permute-start | bytes 1376264 | tf_op jit(solution)/shard_map/ppermute | solution.py:261
  4.1 5.2 %copy-start.1 = (bf16[1,1,3584,256]{3,2,1,0:T(8,128)(2,1)S(1)}, bf16[1,1,3584,256]{3,2,1,0:T(8,128)(2,1)}, u32[]{:S(2)}) copy-start(bf16[1,1,3584,256]{3,2,1,0:T(8,128)(2,1)} %param.16) | copy-start | bytes 5505028
  4.2 7.2 %copy-start = (bf16[1,1,256,3584]{3,2,1,0:T(8,128)(2,1)S(1)}, bf16[1,1,256,3584]{3,2,1,0:T(8,128)(2,1)}, u32[]{:S(2)}) copy-start(bf16[1,1,256,3584]{3,2,1,0:T(8,128)(2,1)} %param.17) | copy-start | bytes 5505028
  9.3 74.6 %collective-permute-start = (bf16[64,4352]{1,0:T(8,128)(2,1)}, bf16[64,4352]{1,0:T(8,128)(2,1)S(1)}, u32[]{:S(2)}, u32[]{:S(2)}) collective-permute-start(bf16[64,4352]{1,0:T(8,128)(2,1)} %get-tuple-element.42), channel_id=1, source_target_pairs={{0,16},{1,17},{2,18},{3,19},{4,20},{5,21},{6,22},{7,23},{8,24},{9,... | collective-permute-start | bytes 1671176 | tf_op jit(solution)/shard_map/ppermute | solution.py:261
  9.3 81.1 %collective-permute-start.7 = (bf16[3584,256]{1,0:T(8,128)(2,1)S(1)}, bf16[3584,256]{1,0:T(8,128)(2,1)S(1)}, u32[]{:S(2)}, u32[]{:S(2)}) collective-permute-start(bf16[3584,256]{1,0:T(8,128)(2,1)S(1)} %bitcast.26), channel_id=1, source_target_pairs={{0,2},{1,3},{2,0},{3,1},{4,6},{5,7},{6,4},{7,5},{8,10},{9,11},{10,... | collective-permute-start | bytes 5505032 | tf_op jit(solution)/shard_map/ppermute | solution.py:261
  11.4 79.1 %collective-permute-start.8 = (bf16[256,3584]{1,0:T(8,128)(2,1)S(1)}, bf16[256,3584]{1,0:T(8,128)(2,1)S(1)}, u32[]{:S(2)}, u32[]{:S(2)}) collective-permute-start(bf16[256,3584]{1,0:T(8,128)(2,1)S(1)} %bitcast.23), channel_id=1, source_target_pairs={{0,2},{1,3},{2,0},{3,1},{4,6},{5,7},{6,4},{7,5},{8,10},{9,11},{10,... | collective-permute-start | bytes 5505032 | tf_op jit(solution)/shard_map/ppermute | solution.py:261
  11.5 24.4 %collective-permute-start.3 = (bf16[120,3584]{1,0:T(8,128)(2,1)}, bf16[120,3584]{1,0:T(8,128)(2,1)S(1)}, u32[]{:S(2)}, u32[]{:S(2)}) collective-permute-start(bf16[120,3584]{1,0:T(8,128)(2,1)} %get-tuple-element.47), channel_id=1, source_target_pairs={{0,4},{1,5},{2,6},{3,7},{4,8},{5,9},{6,10},{7,11},{8,12},{9,13},{1... | collective-permute-start | bytes 2580488 | tf_op jit(solution)/shard_map/ppermute | solution.py:261
  14.7 1.9 %copy-start.3 = (bf16[120,3584]{1,0:T(8,128)(2,1)S(1)}, bf16[120,3584]{1,0:T(8,128)(2,1)}, u32[]{:S(2)}) copy-start(bf16[120,3584]{1,0:T(8,128)(2,1)} %get-tuple-element.48) | copy-start | bytes 2580484
  14.7 21.2 %copy-start.2 = (bf16[120,3584]{1,0:T(8,128)(2,1)S(1)}, bf16[120,3584]{1,0:T(8,128)(2,1)}, u32[]{:S(2)}) copy-start(bf16[120,3584]{1,0:T(8,128)(2,1)} %get-tuple-element.51) | copy-start | bytes 2580484
  16.6 54.3 %collective-permute-start.4 = (bf16[120,3584]{1,0:T(8,128)(2,1)S(1)}, bf16[120,3584]{1,0:T(8,128)(2,1)S(1)}, u32[]{:S(2)}, u32[]{:S(2)}) collective-permute-start(bf16[120,3584]{1,0:T(8,128)(2,1)S(1)} %copy-done.3), channel_id=1, source_target_pairs={{0,8},{1,9},{2,10},{3,11},{4,12},{5,13},{6,14},{7,15},{8,0},{9,1},... | collective-permute-start | bytes 2580488 | tf_op jit(solution)/shard_map/ppermute | solution.py:261
  35.8 46.7 %collective-permute-start.6 = (bf16[120,3584]{1,0:T(8,128)(2,1)S(1)}, bf16[120,3584]{1,0:T(8,128)(2,1)S(1)}, u32[]{:S(2)}, u32[]{:S(2)}) collective-permute-start(bf16[120,3584]{1,0:T(8,128)(2,1)S(1)} %copy-done.2), channel_id=1, source_target_pairs={{0,12},{1,13},{2,14},{3,15},{4,0},{5,1},{6,2},{7,3},{8,4},{9,5},{1... | collective-permute-start | bytes 2580488 | tf_op jit(solution)/shard_map/ppermute | solution.py:261
  83.7 15.6 %collective-permute-start.10 = (bf16[320,3584]{1,0:T(8,128)(2,1)S(1)}, bf16[320,3584]{1,0:T(8,128)(2,1)S(1)}, u32[]{:S(2)}, u32[]{:S(2)}) collective-permute-start(bf16[320,3584]{1,0:T(8,128)(2,1)S(1)} %constant_dynamic-update-slice_fusion.xg_own), channel_id=1, source_target_pairs={{0,1},{1,0},{2,3},{3,2},{4,5},{5,4},{6,7},{7,6},{8,9},{9,8},{10,11... | collective-permute-start | bytes 6881288 | tf_op jit(solution)/shard_map/ppermute | solution.py:261
  90.4 8.9 %collective-permute-start.12 = (bf16[256,3584]{1,0:T(8,128)(2,1)S(1)}, bf16[256,3584]{1,0:T(8,128)(2,1)S(1)}, u32[]{:S(2)}, u32[]{:S(2)}) collective-permute-start(bf16[256,3584]{1,0:T(8,128)(2,1)S(1)} %collective-permute-done.8.down_y), channel_id=1, source_target_pairs={{0,1},{1,0},{2,3},{3,2},{4,5},{5,4},{6,7},{7,6},{8,9},{9,8},{10,11... | collective-permute-start | bytes 5505032 | tf_op jit(solution)/shard_map/ppermute | solution.py:261
  90.5 8.9 %collective-permute-start.11 = (bf16[3584,256]{1,0:T(8,128)(2,1)S(1)}, bf16[3584,256]{1,0:T(8,128)(2,1)S(1)}, u32[]{:S(2)}, u32[]{:S(2)}) collective-permute-start(bf16[3584,256]{1,0:T(8,128)(2,1)S(1)} %collective-permute-done.7.up_y), channel_id=1, source_target_pairs={{0,1},{1,0},{2,3},{3,2},{4,5},{5,4},{6,7},{7,6},{8,9},{9,8},{10,11... | collective-permute-start | bytes 5505032 | tf_op jit(solution)/shard_map/ppermute | solution.py:261
  91.0 51.8 %collective-permute-start.9 = (bf16[320,3584]{1,0:T(8,128)(2,1)S(1)}, bf16[320,3584]{1,0:T(8,128)(2,1)S(1)}, u32[]{:S(2)}, u32[]{:S(2)}) collective-permute-start(bf16[320,3584]{1,0:T(8,128)(2,1)S(1)} %constant_dynamic-update-slice_fusion.xg_own), channel_id=1, source_target_pairs={{0,2},{1,3},{2,0},{3,1},{4,6},{5,7},{6,4},{7,5},{8,10},{9,11},{10,... | collective-permute-start | bytes 6881288 | tf_op jit(solution)/shard_map/ppermute | solution.py:261
  101.8 44.1 %collective-permute-start.13 = (bf16[80,3584]{1,0:T(8,128)(2,1)S(1)}, bf16[80,3584]{1,0:T(8,128)(2,1)S(1)}, u32[]{:S(2)}, u32[]{:S(2)}) collective-permute-start(bf16[80,3584]{1,0:T(8,128)(2,1)S(1)} %get-tuple-element.67), channel_id=1, source_target_pairs={{0,16},{1,17},{2,18},{3,19},{4,20},{5,21},{6,22},{7,23},{8,24},{9,... | collective-permute-start | bytes 1720328 | tf_op jit(solution)/shard_map/ppermute | solution.py:261
  103.4 42.6 %collective-permute-start.15 = (bf16[80,3584]{1,0:T(8,128)(2,1)S(1)}, bf16[80,3584]{1,0:T(8,128)(2,1)S(1)}, u32[]{:S(2)}, u32[]{:S(2)}) collective-permute-start(bf16[80,3584]{1,0:T(8,128)(2,1)S(1)} %get-tuple-element.69), channel_id=1, source_target_pairs={{0,24},{1,25},{2,26},{3,27},{4,28},{5,29},{6,30},{7,31},{8,16},{9,... | collective-permute-start | bytes 1720328 | tf_op jit(solution)/shard_map/ppermute | solution.py:261
  105.9 40.1 %collective-permute-start.16 = (bf16[80,3584]{1,0:T(8,128)(2,1)S(1)}, bf16[80,3584]{1,0:T(8,128)(2,1)S(1)}, u32[]{:S(2)}, u32[]{:S(2)}) collective-permute-start(bf16[80,3584]{1,0:T(8,128)(2,1)S(1)} %get-tuple-element.70), channel_id=1, source_target_pairs={{0,20},{1,21},{2,22},{3,23},{4,24},{5,25},{6,26},{7,27},{8,28},{9,... | collective-permute-start | bytes 1720328 | tf_op jit(solution)/shard_map/ppermute | solution.py:261
  108.5 34.2 %collective-permute-start.14 = (bf16[32,3584]{1,0:T(8,128)(2,1)S(1)}, bf16[32,3584]{1,0:T(8,128)(2,1)S(1)}, u32[]{:S(2)}, u32[]{:S(2)}) collective-permute-start(bf16[32,3584]{1,0:T(8,128)(2,1)S(1)} %slice.58), channel_id=1, source_target_pairs={{0,28},{1,29},{2,30},{3,31},{4,16},{5,17},{6,18},{7,19},{8,20},{9,... | collective-permute-start | bytes 688136 | tf_op jit(solution)/shard_map/ppermute | solution.py:261
  146.0 6.3 %collective-permute-start.17 = (bf16[320,3584]{1,0:T(8,128)(2,1)S(1)}, bf16[320,3584]{1,0:T(8,128)(2,1)S(1)}, u32[]{:S(2)}, u32[]{:S(2)}) collective-permute-start(bf16[320,3584]{1,0:T(8,128)(2,1)S(1)} %collective-permute-done.9.xg_y), channel_id=1, source_target_pairs={{0,1},{1,0},{2,3},{3,2},{4,5},{5,4},{6,7},{7,6},{8,9},{9,8},{10,11... | collective-permute-start | bytes 6881288 | tf_op jit(solution)/shard_map/ppermute | solution.py:261
  146.0 12.6 %collective-permute-start.18 = (bf16[48,3584]{1,0:T(8,128)(2,1)S(1)}, bf16[48,3584]{1,0:T(8,128)(2,1)S(1)}, u32[]{:S(2)}, u32[]{:S(2)}) collective-permute-start(bf16[48,3584]{1,0:T(8,128)(2,1)S(1)} %slice.59), channel_id=1, source_target_pairs={{0,28},{1,29},{2,30},{3,31},{4,16},{5,17},{6,18},{7,19},{8,20},{9,... | collective-permute-start | bytes 1032200 | tf_op jit(solution)/shard_map/ppermute | solution.py:261

commit v7 on v6

--- a/solution.py
+++ b/solution.py
@@ -40,8 +40,11 @@
 def build_kernel(
     experts, cap, joined, mine_ref, fr_ref, fg_ref, br_ref, bg_ref, f_any, x_any, g_any, *refs
 ):
-    outs, base_b, more, (f_ref, x_ref, g_ref, sems) = refs[:experts], refs[experts], refs[experts + 1:-4], refs[-4:]
+    (f_ref, x_ref, g_ref, sems), refs = refs[-4:], refs[:-4]
+    targets, held = refs[:len(refs) // 2], refs[len(refs) // 2:]
+    outs, base_b, more = held[:experts], held[experts], held[experts + 1:]
     copies = start_copies(((f_any, f_ref), (x_any, x_ref), (g_any, g_ref)), sems)
+    leaving = [pltpu.make_async_copy(src, dst, sems.at[3 + i]) for i, (src, dst) in enumerate(zip(held, targets))]
     tok_rows = f_ref.shape[0]
     wide = table_width(experts, 2 * cap if joined else cap)
     mine = mine_ref[0]
@@ -78,6 +81,7 @@
         rows_x = dot(hits, x_ref[...], (1, 0))
         rows_g = dot(hits, g_ref[...], (1, 0)) * jnp.sum(gated_b[k], axis=1, keepdims=True)
         outs[k][...] = jnp.concatenate([rows_f, rows_x, rows_g], axis=0).astype(BF16)
+        leaving[k].start()
 
     width = f_ref.shape[1]
     base_b[:, :width] = g_ref[...]
@@ -93,6 +97,10 @@
             base_b[:, width + low:width + low + wide] = by_token(part)
         else:
             more[0][:, low:low + wide] = by_token(part)
+    for copy in leaving[experts:]:
+        copy.start()
+    for copy in leaving:
+        copy.wait()
 
 
 def table_width(experts, each):
@@ -281,10 +289,11 @@
     tables = [shape(tok_rows, width + 2 * wide)]
     if not joined:
         tables = [shape(tok_rows, width + wide), shape(tok_rows, 2 * wide)]
+    leaving = [shape(3 * cap, width)] * experts + tables
     built = call(
         lambda *refs: build_kernel(experts, cap, joined, *refs),
         "build",
-        [shape(3 * cap, width)] * experts + tables,
+        leaving,
         (
             mine.reshape(1), fwd_routes[0].T, fwd_gates[0].T, back_routes[0].T, back_gates[0].T,
             fwd_input, back_input, out_grad,
@@ -292,7 +301,10 @@
         cost(100, 0.1),
         limit=56,
         in_specs=[SMEM] + [VMEM] * 4 + [HBM] * 3,
-        scratch_shapes=[pltpu.VMEM((tok_rows, width), BF16)] * 3 + [pltpu.SemaphoreType.DMA((3,))],
+        out_specs=[HBM] * len(leaving),
+        scratch_shapes=[pltpu.VMEM(part.shape, BF16) for part in leaving]
+        + [pltpu.VMEM((tok_rows, width), BF16)] * 3
+        + [pltpu.SemaphoreType.DMA((3 + len(leaving),))],
     )
     got, tables = list(built[:experts]), built[experts:]
 

time: 161 us -> 160 us (level)
  no operation moved by 1% of the time
where the time goes in v7:
time: 160 us
  waiting for transfers between devices  100 us (62%)
  Pallas kernels  29 us (18%)
  starting transfers between devices  26.8 us (17%)
  local copies, waits for them, and re-layouts  2.57 us (2%)
    ppermute x19, waiting for transfers between devices, send(): return lax.ppermute(value, ('pipe', 'expert'), pairs)  100 us
    pallas_call x9, Pallas kernels, call(): pl.pallas_call(kernel, out_shape=out_shape, in_specs=more.pop('in_specs',...  29 us
    ppermute x19, starting transfers between devices, send(): return lax.ppermute(value, ('pipe', 'expert'), pairs)  26.8 us
  transfers between devices with their start and end apart: 19, of which 7 were waited for; matrix products, arithmetic and copies ran while one was open for 2% of the time, Pallas kernels for 17%

profile of v7, /device:TPU:0, one launch (start us, length us, event | category | flops | bytes accessed | tf_op | source)
XLA Modules:
  0.0 159.8 jit_solution(574032873142632533)
XLA Ops:
  0.6 0.5 collective-permute-start.1
  1.2 0.1 collective-permute-start.2
  1.2 2.9 %collective-permute-start.5 = (bf16[64,3584]{1,0:T(8,128)(2,1)}, bf16[64,3584]{1,0:T(8,128)(2,1)S(1)}, u32[]{:S(2)}, u32[]{:S(2)}) collective-permute-start(bf16[64,3584]{1,0:T(8,128)(2,1)} %bitcast.32), channel_id=1, source_target_pairs={{0,16},{1,17},{2,18},{3,19},{4,20},{5,21},{6,22},{7,23},{8,24},{9,... | collective-permute-start | bytes 1376264 | tf_op jit(solution)/shard_map/ppermute | solution.py:269
  4.1 0.0 copy-start.1
  4.2 0.0 copy-start
  4.2 4.9 %build.1 = (bf16[120,3584]{1,0:T(8,128)(2,1)}, bf16[120,3584]{1,0:T(8,128)(2,1)}, bf16[120,3584]{1,0:T(8,128)(2,1)}, bf16[120,3584]{1,0:T(8,128)(2,1)}, bf16[64,4352]{1,0:T(8,128)(2,1)}) custom-call(s32[1]{0:T(128)} %bitcast.refs_0_, s32[2,64]{1,0:T(2,128)} %bitcast.36, f32[2,64]{1,0:T(2,128)} %bitcast.37, s32[2,64]{1,0:T(2,128)} %bitcast.38, ...), custom_call_target="tpu_custom_call" | custom-call | flops 99999997952 | bytes 104857 | tf_op jit(solution)/shard_map/build/pallas_call | solution.py:272
  9.0 0.1 collective-permute-start
  9.1 0.0 copy-done.1
  9.1 2.0 %collective-permute-start.7 = (bf16[3584,256]{1,0:T(8,128)(2,1)S(1)}, bf16[3584,256]{1,0:T(8,128)(2,1)S(1)}, u32[]{:S(2)}, u32[]{:S(2)}) collective-permute-start(bf16[3584,256]{1,0:T(8,128)(2,1)S(1)} %bitcast.26), channel_id=1, source_target_pairs={{0,2},{1,3},{2,0},{3,1},{4,6},{5,7},{6,4},{7,5},{8,10},{9,11},{10,... | collective-permute-start | bytes 5505032 | tf_op jit(solution)/shard_map/ppermute | solution.py:269
  11.2 0.0 collective-permute-done.1.up_c
  11.2 0.0 copy-done
  11.2 0.1 collective-permute-start.8
  11.2 0.0 collective-permute-done.2.refs_2_
  11.2 2.0 %collective-permute-start.3 = (bf16[120,3584]{1,0:T(8,128)(2,1)}, bf16[120,3584]{1,0:T(8,128)(2,1)S(1)}, u32[]{:S(2)}, u32[]{:S(2)}) collective-permute-start(bf16[120,3584]{1,0:T(8,128)(2,1)} %get-tuple-element.47), channel_id=1, source_target_pairs={{0,4},{1,5},{2,6},{3,7},{4,8},{5,9},{6,10},{7,11},{8,12},{9,13},{1... | collective-permute-start | bytes 2580488 | tf_op jit(solution)/shard_map/ppermute | solution.py:269
  13.2 1.2 fusion
  14.5 0.0 copy-start.3
  14.5 0.0 copy-start.2
  14.5 1.9 %stage.1 = (bf16[3584,256]{1,0:T(8,128)(2,1)S(1)}, bf16[256,3584]{1,0:T(8,128)(2,1)S(1)}, bf16[256,3584]{1,0:T(8,128)(2,1)S(1)}) custom-call(bf16[3584,256]{1,0:T(8,128)(2,1)S(1)} %bitcast.27, bf16[256,3584]{1,0:T(8,128)(2,1)S(1)} %bitcast.24, bf16[256,3584]{1,0:T(8,128)(2,1)} %collective-permute-done.2.refs_2_), custom_call_target="tpu_custom_call" | custom-call | flops 10000000 | bytes 104857 | tf_op jit(solution)/shard_map/stage/pallas_call | solution.py:272
  16.4 0.0 collective-permute-done.5.refs_1_
  16.4 0.0 copy-done.3
  16.4 2.7 %collective-permute-start.4 = (bf16[120,3584]{1,0:T(8,128)(2,1)S(1)}, bf16[120,3584]{1,0:T(8,128)(2,1)S(1)}, u32[]{:S(2)}, u32[]{:S(2)}) collective-permute-start(bf16[120,3584]{1,0:T(8,128)(2,1)S(1)} %copy-done.3), channel_id=1, source_target_pairs={{0,8},{1,9},{2,10},{3,11},{4,12},{5,13},{6,14},{7,15},{8,0},{9,1},... | collective-permute-start | bytes 2580488 | tf_op jit(solution)/shard_map/ppermute | solution.py:269
  19.1 16.5 %collective-permute-done.3 = bf16[120,3584]{1,0:T(8,128)(2,1)S(1)} collective-permute-done((bf16[120,3584]{1,0:T(8,128)(2,1)}, bf16[120,3584]{1,0:T(8,128)(2,1)S(1)}, u32[]{:S(2)}, u32[]{:S(2)}) %collective-permute-start.3) | collective-permute-done | bytes 860192 | tf_op jit(solution)/shard_map/ppermute | solution.py:269
  35.6 0.0 copy-done.2
  35.6 0.5 collective-permute-start.6
  36.2 0.1 fusion.1
  36.2 34.4 %collective-permute-done.4 = bf16[120,3584]{1,0:T(8,128)(2,1)S(1)} collective-permute-done((bf16[120,3584]{1,0:T(8,128)(2,1)S(1)}, bf16[120,3584]{1,0:T(8,128)(2,1)S(1)}, u32[]{:S(2)}, u32[]{:S(2)}) %collective-permute-start.4) | collective-permute-done | bytes 860192 | tf_op jit(solution)/shard_map/ppermute | solution.py:269
  70.7 0.1 fusion.2
  70.8 11.6 %collective-permute-done.6 = bf16[120,3584]{1,0:T(8,128)(2,1)S(1)} collective-permute-done((bf16[120,3584]{1,0:T(8,128)(2,1)S(1)}, bf16[120,3584]{1,0:T(8,128)(2,1)S(1)}, u32[]{:S(2)}, u32[]{:S(2)}) %collective-permute-start.6) | collective-permute-done | bytes 860192 | tf_op jit(solution)/shard_map/ppermute | solution.py:269
  82.3 0.1 fusion.3
  82.4 1.0 constant_dynamic-update-slice_fusion.3
  83.5 0.1 collective-permute-start.10
  83.6 0.0 collective-permute-done.refs_2_
  83.6 6.6 %collective-permute-done.8.down_y = bf16[256,3584]{1,0:T(8,128)(2,1)S(1)} collective-permute-done((bf16[256,3584]{1,0:T(8,128)(2,1)S(1)}, bf16[256,3584]{1,0:T(8,128)(2,1)S(1)}, u32[]{:S(2)}, u32[]{:S(2)}) %collective-permute-start.8) | collective-permute-done | bytes 1835040 | tf_op jit(solution)/shard_map/ppermute | solution.py:269
  90.2 0.0 collective-permute-start.12
  90.2 0.0 collective-permute-done.7.up_y
  90.2 0.5 collective-permute-start.11
  90.7 1.7 %collective-permute-start.9 = (bf16[320,3584]{1,0:T(8,128)(2,1)S(1)}, bf16[320,3584]{1,0:T(8,128)(2,1)S(1)}, u32[]{:S(2)}, u32[]{:S(2)}) collective-permute-start(bf16[320,3584]{1,0:T(8,128)(2,1)S(1)} %constant_dynamic-update-slice_fusion.xg_own), channel_id=1, source_target_pairs={{0,2},{1,3},{2,0},{3,1},{4,6},{5,7},{6,4},{7,5},{8,10},{9,11},{10,... | collective-permute-start | bytes 6881288 | tf_op jit(solution)/shard_map/ppermute | solution.py:269
  92.4 0.1 pad_maximum_fusion.2.rows_g.refs_2_
  92.5 0.2 pad_maximum_fusion
  92.8 2.4 %own.1 = (bf16[160,512]{1,0:T(8,128)(2,1)S(1)}, bf16[160,512]{1,0:T(8,128)(2,1)S(1)}) custom-call(bf16[160,3584]{1,0:T(8,128)(2,1)S(1)} %get-tuple-element.58.rows_f.refs_0_, bf16[160,3584]{1,0:T(8,128)(2,1)S(1)} %get-tuple-element.59.rows_x.refs_1_, bf16[160,3584]{1,0:T(8,128)(2,1)S(1)} %pad_maximum_fusion.2.rows_g.refs_2_, ...), custom_call_target="tpu_custom_call" | custom-call | flops 2000000000 | bytes 12582912 | tf_op jit(solution)/shard_map/own/pallas_call | solution.py:272
  95.2 4.0 %near.1 = (f32[160,3584]{1,0:T(8,128)S(1)}, f32[160,3584]{1,0:T(8,128)S(1)}) custom-call(bf16[160,3584]{1,0:T(8,128)(2,1)S(1)} %get-tuple-element.58.rows_f.refs_0_, bf16[160,3584]{1,0:T(8,128)(2,1)S(1)} %get-tuple-element.59.rows_x.refs_1_, bf16[160,3584]{1,0:T(8,128)(2,1)S(1)} %pad_maximum_fusion.2.rows_g.refs_2_, ...), custom_call_target="tpu_custom_call" | custom-call | flops 3000000000 | bytes 18874368 | tf_op jit(solution)/shard_map/near/pallas_call | solution.py:272
  99.1 0.0 collective-permute-done.10.xg_c
  99.2 0.0 collective-permute-done.12.refs_6_
  99.2 0.0 collective-permute-done.11.refs_5_
  99.2 2.4 %far.1 = (bf16[80,3584]{1,0:T(8,128)(2,1)S(1)}, bf16[80,3584]{1,0:T(8,128)(2,1)S(1)}, bf16[80,3584]{1,0:T(8,128)(2,1)S(1)}, bf16[80,3584]{1,0:T(8,128)(2,1)S(1)}) custom-call(bf16[160,3584]{1,0:T(8,128)(2,1)S(1)} %get-tuple-element.58.rows_f.refs_0_, bf16[160,3584]{1,0:T(8,128)(2,1)S(1)} %get-tuple-element.59.rows_x.refs_1_, ...), custom_call_target="tpu_custom_call" | custom-call | flops 2000000000 | bytes 10485760 | tf_op jit(solution)/shard_map/far/pallas_call | solution.py:272
  101.6 1.6 collective-permute-start.13
  103.2 2.6 %collective-permute-start.15 = (bf16[80,3584]{1,0:T(8,128)(2,1)S(1)}, bf16[80,3584]{1,0:T(8,128)(2,1)S(1)}, u32[]{:S(2)}, u32[]{:S(2)}) collective-permute-start(bf16[80,3584]{1,0:T(8,128)(2,1)S(1)} %get-tuple-element.69), channel_id=1, source_target_pairs={{0,24},{1,25},{2,26},{3,27},{4,28},{5,29},{6,30},{7,31},{8,16},{9,... | collective-permute-start | bytes 1720328 | tf_op jit(solution)/shard_map/ppermute | solution.py:269
  105.7 2.5 %collective-permute-start.16 = (bf16[80,3584]{1,0:T(8,128)(2,1)S(1)}, bf16[80,3584]{1,0:T(8,128)(2,1)S(1)}, u32[]{:S(2)}, u32[]{:S(2)}) collective-permute-start(bf16[80,3584]{1,0:T(8,128)(2,1)S(1)} %get-tuple-element.70), channel_id=1, source_target_pairs={{0,20},{1,21},{2,22},{3,23},{4,24},{5,25},{6,26},{7,27},{8,28},{9,... | collective-permute-start | bytes 1720328 | tf_op jit(solution)/shard_map/ppermute | solution.py:269
  108.2 2.4 %collective-permute-start.14 = (bf16[32,3584]{1,0:T(8,128)(2,1)S(1)}, bf16[32,3584]{1,0:T(8,128)(2,1)S(1)}, u32[]{:S(2)}, u32[]{:S(2)}) collective-permute-start(bf16[32,3584]{1,0:T(8,128)(2,1)S(1)} %slice.58), channel_id=1, source_target_pairs={{0,28},{1,29},{2,30},{3,31},{4,16},{5,17},{6,18},{7,19},{8,20},{9,... | collective-permute-start | bytes 688136 | tf_op jit(solution)/shard_map/ppermute | solution.py:269
  110.7 4.5 %chip_grads.1 = (f32[3584,256]{1,0:T(8,128)S(1)}, f32[256,3584]{1,0:T(8,128)S(1)}) custom-call(bf16[320,3584]{1,0:T(8,128)(2,1)S(1)} %constant_dynamic-update-slice_fusion.xg_own, bf16[320,3584]{1,0:T(8,128)(2,1)S(1)} %collective-permute-done.10.xg_c, bf16[3584,256]{1,0:T(8,128)(2,1)S(1)} %get-tuple-element.50.own_up.up, ...), custom_call_target="tpu_custom_call" | custom-call | flops 2000000000 | bytes 10485760 | tf_op jit(solution)/shard_map/chip_grads/pallas_call | solution.py:272
  115.2 27.3 %collective-permute-done.9.xg_y = bf16[320,3584]{1,0:T(8,128)(2,1)S(1)} collective-permute-done((bf16[320,3584]{1,0:T(8,128)(2,1)S(1)}, bf16[320,3584]{1,0:T(8,128)(2,1)S(1)}, u32[]{:S(2)}, u32[]{:S(2)}) %collective-permute-start.9) | collective-permute-done | bytes 2293792 | tf_op jit(solution)/shard_map/ppermute | solution.py:269
  142.5 0.0 collective-permute-done.14.refs_4_
  142.5 3.2 %collective-permute-done.13.refs_3_ = bf16[80,3584]{1,0:T(8,128)(2,1)S(1)} collective-permute-done((bf16[80,3584]{1,0:T(8,128)(2,1)S(1)}, bf16[80,3584]{1,0:T(8,128)(2,1)S(1)}, u32[]{:S(2)}, u32[]{:S(2)}) %collective-permute-start.13) | collective-permute-done | bytes 573472 | tf_op jit(solution)/shard_map/ppermute | solution.py:269
  145.7 0.0 collective-permute-done.15.refs_5_
  145.7 0.0 collective-permute-done.16.refs_6_
  145.7 0.0 collective-permute-start.17
  145.8 4.6 %collective-permute-start.18 = (bf16[48,3584]{1,0:T(8,128)(2,1)S(1)}, bf16[48,3584]{1,0:T(8,128)(2,1)S(1)}, u32[]{:S(2)}, u32[]{:S(2)}) collective-permute-start(bf16[48,3584]{1,0:T(8,128)(2,1)S(1)} %slice.59), channel_id=1, source_target_pairs={{0,28},{1,29},{2,30},{3,31},{4,16},{5,17},{6,18},{7,19},{8,20},{9,... | collective-permute-start | bytes 1032200 | tf_op jit(solution)/shard_map/ppermute | solution.py:269
  150.4 1.6 %combine_first.1.refs_1_ = f32[128,3584]{1,0:T(8,128)S(1)} custom-call(bf16[64,768]{1,0:T(8,128)(2,1)S(1)} %slice.60.refs_0_, bf16[64,3584]{1,0:T(8,128)(2,1)S(1)} %collective-permute-done.5.refs_1_, bf16[64,4352]{1,0:T(8,128)(2,1)S(1)} %collective-permute-done.refs_2_, bf16[80,3584]{1,0:T(8,128)(2,1)S(1)} %collective-permute-done.13.refs_3_, ...), custom_call_target="tpu_custom_call" | custom-call | flops 200000000 | bytes 4194304 | tf_op jit(solution)/shard_map/combine_first/pallas_call | solution.py:272
  152.0 0.0 collective-permute-done.17.xg_d
  152.0 5.8 %grads.1 = (f32[3584,256]{1,0:T(8,128)}, f32[256,3584]{1,0:T(8,128)}) custom-call(bf16[320,3584]{1,0:T(8,128)(2,1)S(1)} %collective-permute-done.9.xg_y, bf16[320,3584]{1,0:T(8,128)(2,1)S(1)} %collective-permute-done.17.xg_d, bf16[3584,256]{1,0:T(8,128)(2,1)S(1)} %get-tuple-element.50.own_up.up, bf16[256,3584]{1,0:T(8,128)(2,1)S(1)} %get-tuple-element.55.own_down.down, ...), custom_call_target="tpu_custom_call" | custom-call | flops 10000000 | bytes 104857 | tf_op jit(solution)/shard_map/grads/pallas_call | solution.py:272
  157.8 0.5 collective-permute-done.18.refs_2_
  158.3 1.5 combine.1
  (6 shorter events, 0.1 us)
Async XLA Ops:
  0.6 10.5 %collective-permute-start.1 = (bf16[3584,256]{1,0:T(8,128)(2,1)}, bf16[3584,256]{1,0:T(8,128)(2,1)S(1)}, u32[]{:S(2)}, u32[]{:S(2)}) collective-permute-start(bf16[3584,256]{1,0:T(8,128)(2,1)} %bitcast.25), channel_id=1, source_target_pairs={{0,1},{1,0},{2,3},{3,2},{4,5},{5,4},{6,7},{7,6},{8,9},{9,8},{10,11... | collective-permute-start | bytes 5505032 | tf_op jit(solution)/shard_map/ppermute | solution.py:269
  1.2 10.1 %collective-permute-start.2 = (bf16[256,3584]{1,0:T(8,128)(2,1)}, bf16[256,3584]{1,0:T(8,128)(2,1)}, u32[]{:S(2)}, u32[]{:S(2)}) collective-permute-start(bf16[256,3584]{1,0:T(8,128)(2,1)} %bitcast.22), channel_id=1, source_target_pairs={{0,1},{1,0},{2,3},{3,2},{4,5},{5,4},{6,7},{7,6},{8,9},{9,8},{10,11... | collective-permute-start | bytes 5505032 | tf_op jit(solution)/shard_map/ppermute | solution.py:269
  1.2 15.2 %collective-permute-start.5 = (bf16[64,3584]{1,0:T(8,128)(2,1)}, bf16[64,3584]{1,0:T(8,128)(2,1)S(1)}, u32[]{:S(2)}, u32[]{:S(2)}) collective-permute-start(bf16[64,3584]{1,0:T(8,128)(2,1)} %bitcast.32), channel_id=1, source_target_pairs={{0,16},{1,17},{2,18},{3,19},{4,20},{5,21},{6,22},{7,23},{8,24},{9,... | collective-permute-start | bytes 1376264 | tf_op jit(solution)/shard_map/ppermute | solution.py:269
  4.1 5.0 %copy-start.1 = (bf16[1,1,3584,256]{3,2,1,0:T(8,128)(2,1)S(1)}, bf16[1,1,3584,256]{3,2,1,0:T(8,128)(2,1)}, u32[]{:S(2)}) copy-start(bf16[1,1,3584,256]{3,2,1,0:T(8,128)(2,1)} %param.16) | copy-start | bytes 5505028
  4.2 7.0 %copy-start = (bf16[1,1,256,3584]{3,2,1,0:T(8,128)(2,1)S(1)}, bf16[1,1,256,3584]{3,2,1,0:T(8,128)(2,1)}, u32[]{:S(2)}) copy-start(bf16[1,1,256,3584]{3,2,1,0:T(8,128)(2,1)} %param.17) | copy-start | bytes 5505028
  9.0 74.6 %collective-permute-start = (bf16[64,4352]{1,0:T(8,128)(2,1)}, bf16[64,4352]{1,0:T(8,128)(2,1)S(1)}, u32[]{:S(2)}, u32[]{:S(2)}) collective-permute-start(bf16[64,4352]{1,0:T(8,128)(2,1)} %get-tuple-element.42), channel_id=1, source_target_pairs={{0,16},{1,17},{2,18},{3,19},{4,20},{5,21},{6,22},{7,23},{8,24},{9,... | collective-permute-start | bytes 1671176 | tf_op jit(solution)/shard_map/ppermute | solution.py:269
  9.1 81.1 %collective-permute-start.7 = (bf16[3584,256]{1,0:T(8,128)(2,1)S(1)}, bf16[3584,256]{1,0:T(8,128)(2,1)S(1)}, u32[]{:S(2)}, u32[]{:S(2)}) collective-permute-start(bf16[3584,256]{1,0:T(8,128)(2,1)S(1)} %bitcast.26), channel_id=1, source_target_pairs={{0,2},{1,3},{2,0},{3,1},{4,6},{5,7},{6,4},{7,5},{8,10},{9,11},{10,... | collective-permute-start | bytes 5505032 | tf_op jit(solution)/shard_map/ppermute | solution.py:269
  11.2 79.1 %collective-permute-start.8 = (bf16[256,3584]{1,0:T(8,128)(2,1)S(1)}, bf16[256,3584]{1,0:T(8,128)(2,1)S(1)}, u32[]{:S(2)}, u32[]{:S(2)}) collective-permute-start(bf16[256,3584]{1,0:T(8,128)(2,1)S(1)} %bitcast.23), channel_id=1, source_target_pairs={{0,2},{1,3},{2,0},{3,1},{4,6},{5,7},{6,4},{7,5},{8,10},{9,11},{10,... | collective-permute-start | bytes 5505032 | tf_op jit(solution)/shard_map/ppermute | solution.py:269
  11.2 24.4 %collective-permute-start.3 = (bf16[120,3584]{1,0:T(8,128)(2,1)}, bf16[120,3584]{1,0:T(8,128)(2,1)S(1)}, u32[]{:S(2)}, u32[]{:S(2)}) collective-permute-start(bf16[120,3584]{1,0:T(8,128)(2,1)} %get-tuple-element.47), channel_id=1, source_target_pairs={{0,4},{1,5},{2,6},{3,7},{4,8},{5,9},{6,10},{7,11},{8,12},{9,13},{1... | collective-permute-start | bytes 2580488 | tf_op jit(solution)/shard_map/ppermute | solution.py:269
  14.5 1.9 %copy-start.3 = (bf16[120,3584]{1,0:T(8,128)(2,1)S(1)}, bf16[120,3584]{1,0:T(8,128)(2,1)}, u32[]{:S(2)}) copy-start(bf16[120,3584]{1,0:T(8,128)(2,1)} %get-tuple-element.48) | copy-start | bytes 2580484
  14.5 21.2 %copy-start.2 = (bf16[120,3584]{1,0:T(8,128)(2,1)S(1)}, bf16[120,3584]{1,0:T(8,128)(2,1)}, u32[]{:S(2)}) copy-start(bf16[120,3584]{1,0:T(8,128)(2,1)} %get-tuple-element.51) | copy-start | bytes 2580484
  16.4 54.3 %collective-permute-start.4 = (bf16[120,3584]{1,0:T(8,128)(2,1)S(1)}, bf16[120,3584]{1,0:T(8,128)(2,1)S(1)}, u32[]{:S(2)}, u32[]{:S(2)}) collective-permute-start(bf16[120,3584]{1,0:T(8,128)(2,1)S(1)} %copy-done.3), channel_id=1, source_target_pairs={{0,8},{1,9},{2,10},{3,11},{4,12},{5,13},{6,14},{7,15},{8,0},{9,1},... | collective-permute-start | bytes 2580488 | tf_op jit(solution)/shard_map/ppermute | solution.py:269
  35.6 46.7 %collective-permute-start.6 = (bf16[120,3584]{1,0:T(8,128)(2,1)S(1)}, bf16[120,3584]{1,0:T(8,128)(2,1)S(1)}, u32[]{:S(2)}, u32[]{:S(2)}) collective-permute-start(bf16[120,3584]{1,0:T(8,128)(2,1)S(1)} %copy-done.2), channel_id=1, source_target_pairs={{0,12},{1,13},{2,14},{3,15},{4,0},{5,1},{6,2},{7,3},{8,4},{9,5},{1... | collective-permute-start | bytes 2580488 | tf_op jit(solution)/shard_map/ppermute | solution.py:269
  83.5 15.6 %collective-permute-start.10 = (bf16[320,3584]{1,0:T(8,128)(2,1)S(1)}, bf16[320,3584]{1,0:T(8,128)(2,1)S(1)}, u32[]{:S(2)}, u32[]{:S(2)}) collective-permute-start(bf16[320,3584]{1,0:T(8,128)(2,1)S(1)} %constant_dynamic-update-slice_fusion.xg_own), channel_id=1, source_target_pairs={{0,1},{1,0},{2,3},{3,2},{4,5},{5,4},{6,7},{7,6},{8,9},{9,8},{10,11... | collective-permute-start | bytes 6881288 | tf_op jit(solution)/shard_map/ppermute | solution.py:269
  90.2 8.9 %collective-permute-start.12 = (bf16[256,3584]{1,0:T(8,128)(2,1)S(1)}, bf16[256,3584]{1,0:T(8,128)(2,1)S(1)}, u32[]{:S(2)}, u32[]{:S(2)}) collective-permute-start(bf16[256,3584]{1,0:T(8,128)(2,1)S(1)} %collective-permute-done.8.down_y), channel_id=1, source_target_pairs={{0,1},{1,0},{2,3},{3,2},{4,5},{5,4},{6,7},{7,6},{8,9},{9,8},{10,11... | collective-permute-start | bytes 5505032 | tf_op jit(solution)/shard_map/ppermute | solution.py:269
  90.2 8.9 %collective-permute-start.11 = (bf16[3584,256]{1,0:T(8,128)(2,1)S(1)}, bf16[3584,256]{1,0:T(8,128)(2,1)S(1)}, u32[]{:S(2)}, u32[]{:S(2)}) collective-permute-start(bf16[3584,256]{1,0:T(8,128)(2,1)S(1)} %collective-permute-done.7.up_y), channel_id=1, source_target_pairs={{0,1},{1,0},{2,3},{3,2},{4,5},{5,4},{6,7},{7,6},{8,9},{9,8},{10,11... | collective-permute-start | bytes 5505032 | tf_op jit(solution)/shard_map/ppermute | solution.py:269
  90.7 51.8 %collective-permute-start.9 = (bf16[320,3584]{1,0:T(8,128)(2,1)S(1)}, bf16[320,3584]{1,0:T(8,128)(2,1)S(1)}, u32[]{:S(2)}, u32[]{:S(2)}) collective-permute-start(bf16[320,3584]{1,0:T(8,128)(2,1)S(1)} %constant_dynamic-update-slice_fusion.xg_own), channel_id=1, source_target_pairs={{0,2},{1,3},{2,0},{3,1},{4,6},{5,7},{6,4},{7,5},{8,10},{9,11},{10,... | collective-permute-start | bytes 6881288 | tf_op jit(solution)/shard_map/ppermute | solution.py:269
  101.6 44.1 %collective-permute-start.13 = (bf16[80,3584]{1,0:T(8,128)(2,1)S(1)}, bf16[80,3584]{1,0:T(8,128)(2,1)S(1)}, u32[]{:S(2)}, u32[]{:S(2)}) collective-permute-start(bf16[80,3584]{1,0:T(8,128)(2,1)S(1)} %get-tuple-element.67), channel_id=1, source_target_pairs={{0,16},{1,17},{2,18},{3,19},{4,20},{5,21},{6,22},{7,23},{8,24},{9,... | collective-permute-start | bytes 1720328 | tf_op jit(solution)/shard_map/ppermute | solution.py:269
  103.2 42.6 %collective-permute-start.15 = (bf16[80,3584]{1,0:T(8,128)(2,1)S(1)}, bf16[80,3584]{1,0:T(8,128)(2,1)S(1)}, u32[]{:S(2)}, u32[]{:S(2)}) collective-permute-start(bf16[80,3584]{1,0:T(8,128)(2,1)S(1)} %get-tuple-element.69), channel_id=1, source_target_pairs={{0,24},{1,25},{2,26},{3,27},{4,28},{5,29},{6,30},{7,31},{8,16},{9,... | collective-permute-start | bytes 1720328 | tf_op jit(solution)/shard_map/ppermute | solution.py:269
  105.7 40.0 %collective-permute-start.16 = (bf16[80,3584]{1,0:T(8,128)(2,1)S(1)}, bf16[80,3584]{1,0:T(8,128)(2,1)S(1)}, u32[]{:S(2)}, u32[]{:S(2)}) collective-permute-start(bf16[80,3584]{1,0:T(8,128)(2,1)S(1)} %get-tuple-element.70), channel_id=1, source_target_pairs={{0,20},{1,21},{2,22},{3,23},{4,24},{5,25},{6,26},{7,27},{8,28},{9,... | collective-permute-start | bytes 1720328 | tf_op jit(solution)/shard_map/ppermute | solution.py:269
  108.2 34.3 %collective-permute-start.14 = (bf16[32,3584]{1,0:T(8,128)(2,1)S(1)}, bf16[32,3584]{1,0:T(8,128)(2,1)S(1)}, u32[]{:S(2)}, u32[]{:S(2)}) collective-permute-start(bf16[32,3584]{1,0:T(8,128)(2,1)S(1)} %slice.58), channel_id=1, source_target_pairs={{0,28},{1,29},{2,30},{3,31},{4,16},{5,17},{6,18},{7,19},{8,20},{9,... | collective-permute-start | bytes 688136 | tf_op jit(solution)/shard_map/ppermute | solution.py:269
  145.7 6.3 %collective-permute-start.17 = (bf16[320,3584]{1,0:T(8,128)(2,1)S(1)}, bf16[320,3584]{1,0:T(8,128)(2,1)S(1)}, u32[]{:S(2)}, u32[]{:S(2)}) collective-permute-start(bf16[320,3584]{1,0:T(8,128)(2,1)S(1)} %collective-permute-done.9.xg_y), channel_id=1, source_target_pairs={{0,1},{1,0},{2,3},{3,2},{4,5},{5,4},{6,7},{7,6},{8,9},{9,8},{10,11... | collective-permute-start | bytes 6881288 | tf_op jit(solution)/shard_map/ppermute | solution.py:269
  145.8 12.6 %collective-permute-start.18 = (bf16[48,3584]{1,0:T(8,128)(2,1)S(1)}, bf16[48,3584]{1,0:T(8,128)(2,1)S(1)}, u32[]{:S(2)}, u32[]{:S(2)}) collective-permute-start(bf16[48,3584]{1,0:T(8,128)(2,1)S(1)} %slice.59), channel_id=1, source_target_pairs={{0,28},{1,29},{2,30},{3,31},{4,16},{5,17},{6,18},{7,19},{8,20},{9,... | collective-permute-start | bytes 1032200 | tf_op jit(solution)/shard_map/ppermute | solution.py:269
